TPU v7x, 512 devices: a whole 4x4x16 slice. The times are simulated.
512 devices in a mesh: gx: 16 (over z), gy: 4 (over x), gz: 8 (over y, core).
Axes of the slice: x: 4, y: 4, z: 16, core: 2. Of those that a mesh axis runs over, the one named last changes fastest.
Arguments:
- positions: float32 [3, 16, 4, 8, 1024], P(None, 'gx', 'gy', 'gz'), as said below
- velocities: float32 [3, 16, 4, 8, 1024], P(None, 'gx', 'gy', 'gz'), may hold values from -6 to 6
- radius: float32 [16, 4, 8, 1024], P('gx', 'gy', 'gz'), may hold values from 0.4 to 0.7
- group: int32 [16, 4, 8, 1024], P('gx', 'gy', 'gz'), may hold values from 0 to 1
- broken: int32 [16, 4, 8, 1024], P('gx', 'gy', 'gz'), may hold values 0 or 1
- cell: int32 [16, 4, 8, 1024], P('gx', 'gy', 'gz'), may hold values from 0 to 511
- neighbours: int32 [16, 4, 8, 8, 6], P('gx', 'gy', 'gz'), may hold values from 7 to 208, as said below
- counts: int32 [16, 4, 8, 8], P('gx', 'gy', 'gz'), may hold values from 2 to 6, as said below
Outputs:
- new_positions: float32 [3, 16, 4, 8, 1024], P(None, 'gx', 'gy', 'gz')
- new_velocities: float32 [3, 16, 4, 8, 1024], P(None, 'gx', 'gy', 'gz')
- smooth_stress: float32 [6, 128, 32, 64], P(None, 'gx', ('gy', 'gz'))
- smooth_motion: float32 [4, 128, 32, 64], P(None, 'gx', ('gy', 'gz'))
- energies: float32 [3], replicated
Inputs may be any that keep to these rules, and one draw needn't show every extreme that they name: `positions`: particle p of brick (bx, by, bz) lies inside that brick's cube of edge e = 1024^(1/3), with its x coordinate between (bx + (p // 128) / 8) e and (bx + (p // 128 + 1) / 8) e. `neighbours`: a tile's slots name distinct tiles; for tile t each is tile t - 1, t or t + 1 of a brick at y and z offsets -1, 0, 1 and x offset 0, where t - 1 = -1 stands for tile 8 - 1 of the brick at x offset -1 and t + 1 = 8 for tile 0 of the brick at x offset 1. `counts`: some bricks have a tile whose list uses all 6 slots.
All inputs are finite; a program needn't handle non-finite values. No bound on the sum of `broken` on one device may be relied on, other than what follows from the above.
Results may differ from a plain program's by a relative error of at most 0.0003.
Values sent between devices are 32-bit elements; how exact they have to be, the bound alone decides.
No kernel may reach another device: no remote copies, remote signals or barrier semaphores. Data moves between devices by JAX's collectives and lax.ppermute only.
A program may use at most 64 MiB of HBM per device.

v0:
```python
import jax
import jax.numpy as jnp
from jax import lax
from jax.sharding import PartitionSpec as P

STEPS = 2
CX = 8
CY = 8
CZ = 8
SIGMA = 2
HW = 6


KN = 1.0
GAMMA = 1.0
KB = 2.0
REACH = 1.5
STEP_DT = 0.02
DENS = 4.0
SOFT = 0.0001


def extended(cells, sides, width):
    for axis, dim in sides:
        count = lax.axis_size(axis)
        ends = count - 1
        head = lax.slice_in_dim(cells, 0, width, axis=dim)
        tail = lax.slice_in_dim(cells, cells.shape[dim] - width, cells.shape[dim], axis=dim)
        cells = jnp.concatenate(
            [
                lax.ppermute(tail, axis, [(i, (i + 1) % count) for i in range(ends)]),
                cells,
                lax.ppermute(head, axis, [((i + 1) % count, i) for i in range(ends)]),
            ],
            axis=dim,
        )
    return cells


def pair_terms(own_tile, partner, live_mask, bond_mask):
    offsets = partner[0:3, :, None, :] - own_tile[0:3, :, :, None]
    distance = jnp.sqrt(jnp.sum(offsets * offsets, axis=0) + SOFT)
    direction = offsets / distance
    contact_reach = own_tile[6][:, :, None] + partner[6][:, None, :]
    intersection = jnp.maximum(contact_reach - distance, 0.0) * live_mask
    closing = jnp.sum((partner[3:6, :, None, :] - own_tile[3:6, :, :, None]) * direction, axis=0)
    intersection_root = jnp.sqrt(intersection)
    window = jnp.maximum(1.0 - distance / (REACH * contact_reach), 0.0)
    window = window * window * bond_mask
    stretch = distance - contact_reach
    magnitude = (
        -KN * intersection * intersection_root
        + GAMMA * intersection_root * closing
        + KB * stretch * window
    )
    force = jnp.sum(magnitude[None] * direction, axis=3)
    scaled = -0.5 * magnitude / distance
    component_pairs = [(0, 0), (1, 1), (2, 2), (0, 1), (0, 2), (1, 2)]
    virial = jnp.stack(
        [
            jnp.sum(scaled * offsets[first] * offsets[second], axis=2)
            for first, second in component_pairs
        ]
    )
    contact_energy = jnp.sum(0.4 * KN * intersection * intersection * intersection_root, axis=2)
    bond_energy = jnp.sum(0.5 * KB * stretch * stretch * window, axis=2)
    return (force, virial, contact_energy, bond_energy)


def brick_forces(tiles, neighbour_list, listed, group_tiles, broken_tiles):
    tile_count = neighbour_list.shape[0]
    slots = neighbour_list.shape[1]
    centre = 13 * tile_count
    own_tile = tiles[:, centre : centre + tile_count, :]
    lanes = jnp.arange(128)
    diagonal = lanes[:, None] == lanes[None, :]
    keeping = 1.0 - broken_tiles.astype(jnp.float32)
    tile_ids = jnp.arange(tile_count)

    def visit(column, carried):
        picked = neighbour_list[:, column]
        partner = jnp.take(tiles, picked, axis=1)
        active = (column < listed).astype(jnp.float32)
        relative = picked - centre
        inside = ((relative >= 0) & (relative < tile_count)).astype(jnp.float32)
        position_slot = jnp.clip(relative, 0, tile_count - 1)
        itself = ((relative == tile_ids)[:, None, None] & diagonal[None]).astype(jnp.float32)
        present = (partner[6] > 0).astype(jnp.float32)
        live_mask = active[:, None, None] * present[:, None, :] * (1.0 - itself)
        partner_group = jnp.take(group_tiles, position_slot, axis=0)
        partner_keep = jnp.take(keeping, position_slot, axis=0)
        same_group = (group_tiles[:, :, None] == partner_group[:, None, :]).astype(jnp.float32)
        bond_mask = (
            live_mask
            * inside[:, None, None]
            * same_group
            * keeping[:, :, None]
            * partner_keep[:, None, :]
        )
        terms = pair_terms(own_tile, partner, live_mask, bond_mask)
        return tuple((previous + added for previous, added in zip(carried, terms)))

    starting = (
        jnp.zeros((3, tile_count, 128), jnp.float32),
        jnp.zeros((6, tile_count, 128), jnp.float32),
        jnp.zeros((tile_count, 128), jnp.float32),
        jnp.zeros((tile_count, 128), jnp.float32),
    )
    return lax.fori_loop(0, slots, visit, starting)


def band_matrix(rows_out, cols_in, shift):
    out_index = lax.broadcasted_iota(jnp.int32, (rows_out, cols_in), 0)
    in_index = lax.broadcasted_iota(jnp.int32, (rows_out, cols_in), 1)
    offset_cells = in_index - out_index - shift
    offset_table = jnp.arange(-HW, HW + 1).astype(jnp.float32)
    normaliser = jnp.sum(jnp.exp(-offset_table * offset_table / (2.0 * SIGMA * SIGMA)))
    as_float = offset_cells.astype(jnp.float32)
    weights = jnp.exp(-as_float * as_float / (2.0 * SIGMA * SIGMA)) / normaliser
    return jnp.where(jnp.abs(offset_cells) <= HW, weights, 0.0)


def shards(positions, velocities, radius, group, broken, cell, neighbours, counts):
    width = radius.shape[-1]
    tile_count = width // 128
    state = jnp.concatenate([positions, velocities, radius[None]], axis=0)
    group_tiles = group.reshape(tile_count, 128)
    broken_tiles = broken.reshape(tile_count, 128)
    lists = neighbours.reshape(tile_count, neighbours.shape[-1])
    listed = counts.reshape(tile_count)
    mass = DENS * radius * radius * radius
    for repeat in range(STEPS):
        shell_state = extended(state, (("gx", 1), ("gy", 2), ("gz", 3)), 1)
        tiles = shell_state.reshape(7, 27 * tile_count, 128)
        force, virial, contact, bonding = brick_forces(
            tiles, lists, listed, group_tiles, broken_tiles
        )
        speed = state[3:6] + STEP_DT * force.reshape(3, 1, 1, 1, width) / mass
        place = state[0:3] + STEP_DT * speed
        state = jnp.concatenate([place, speed, state[6:7]], axis=0)
    speed = state[3:6]
    kinetic = 0.5 * mass * jnp.sum(speed * speed, axis=0)
    scale = float(CX * CY * CZ) / float(width)
    values = (
        jnp.concatenate(
            [virial.reshape(6, width), (mass * speed).reshape(3, width), kinetic.reshape(1, width)],
            axis=0,
        )
        * scale
    )
    deposit = jax.ops.segment_sum(values.T, cell.reshape(width), num_segments=CX * CY * CZ).T
    field = deposit.reshape(10, CX, CY, CZ)
    widened = extended(field, (("gy", 2),), HW)
    field = jnp.einsum(
        "cxez,ye->cxyz", widened, band_matrix(CY, CY + 2 * HW, HW), precision=lax.Precision.HIGHEST
    )
    field = lax.all_to_all(field, "gz", split_axis=2, concat_axis=3, tiled=True)
    line_length = field.shape[3]
    field = jnp.einsum(
        "cxye,ze->cxyz",
        field,
        band_matrix(line_length, line_length, 0),
        precision=lax.Precision.HIGHEST,
    )
    widened = extended(field, (("gx", 1),), HW)
    field = jnp.einsum(
        "cwyz,xw->cxyz", widened, band_matrix(CX, CX + 2 * HW, HW), precision=lax.Precision.HIGHEST
    )
    totals = lax.psum((jnp.sum(kinetic), jnp.sum(contact), jnp.sum(bonding)), ("gx", "gy", "gz"))
    energies = jnp.stack([totals[0], totals[1], totals[2]])
    return (state[0:3], state[3:6], field[0:6], field[6:10], energies)


def solution(mesh):
    placed = (
        P(None, "gx", "gy", "gz", None),
        P(None, "gx", "gy", "gz", None),
        P("gx", "gy", "gz", None),
        P("gx", "gy", "gz", None),
        P("gx", "gy", "gz", None),
        P("gx", "gy", "gz", None),
        P("gx", "gy", "gz", None, None),
        P("gx", "gy", "gz", None),
    )
    return jax.shard_map(
        shards,
        mesh=mesh,
        in_specs=placed,
        out_specs=(
            P(None, "gx", "gy", "gz", None),
            P(None, "gx", "gy", "gz", None),
            P(None, "gx", ("gy", "gz"), None),
            P(None, "gx", ("gy", "gz"), None),
            P(),
        ),
        check_vma=False,
    )
```

profile of v0, /device:TPU:1, one launch (start us, length us, event | category | flops | bytes accessed | tf_op | source)
XLA Modules:
  0.0 327.8 jit_solution(7477199572738300959)
XLA Ops:
  1.4 4.4 %collective-permute-start = (f32[7,1,1,1,1024]{4,3,2,1,0:T(1,128)S(1)}, f32[7,1,1,1,1024]{4,3,2,1,0:T(1,128)S(1)}, u32[]{:S(2)}, u32[]{:S(2)}) collective-permute-start(f32[7,1,1,1,1024]{4,3,2,1,0:T(1,128)S(1)} %pad_maximum_fusion.7), channel_id=1, source_target_pairs={{0,32},{32,64},{64,96},{96,128},{128,160},{160,192},{192,224},{224... | collective-permute-start | bytes 86024 | tf_op jit(solution)/shard_map/ppermute | solution.py:31
  7.1 3.5 %collective-permute-done.1 = f32[7,1,1,1,1024]{4,3,2,1,0:T(1,128)S(1)} collective-permute-done((f32[7,1,1,1,1024]{4,3,2,1,0:T(1,128)S(1)}, f32[7,1,1,1,1024]{4,3,2,1,0:T(1,128)S(1)}, u32[]{:S(2)}, u32[]{:S(2)}) %collective-permute-start.1) | collective-permute-done | bytes 28704 | tf_op jit(solution)/shard_map/ppermute | solution.py:33
  11.4 3.1 collective-permute-start.2
  16.0 3.7 %collective-permute-done.3 = f32[7,3,1,1,1024]{4,3,2,1,0:T(1,128)S(1)} collective-permute-done((f32[7,3,1,1,1024]{4,3,2,1,0:T(1,128)S(1)}, f32[7,3,1,1,1024]{4,3,2,1,0:T(1,128)S(1)}, u32[]{:S(2)}, u32[]{:S(2)}) %collective-permute-start.3) | collective-permute-done | bytes 86048 | tf_op jit(solution)/shard_map/ppermute | solution.py:33
  20.8 6.4 %collective-permute-start.4 = (f32[7,3,3,1,1024]{4,3,2,1,0:T(1,128)S(1)}, f32[7,3,3,1,1024]{4,3,2,1,0:T(1,128)S(1)}, u32[]{:S(2)}, u32[]{:S(2)}) collective-permute-start(f32[7,3,3,1,1024]{4,3,2,1,0:T(1,128)S(1)} %pad_maximum_fusion.3), channel_id=1, source_target_pairs={{0,1},{1,2},{2,3},{3,4},{4,5},{5,6},{6,7},{8,9},{9,10},{10,11},{11... | collective-permute-start | bytes 774152 | tf_op jit(solution)/shard_map/ppermute | solution.py:31
  27.2 1.9 collective-permute-start.5
  31.2 3.6 %collective-permute-done.5 = f32[7,3,3,1,1024]{4,3,2,1,0:T(1,128)S(1)} collective-permute-done((f32[7,3,3,1,1024]{4,3,2,1,0:T(1,128)S(1)}, f32[7,3,3,1,1024]{4,3,2,1,0:T(1,128)S(1)}, u32[]{:S(2)}, u32[]{:S(2)}) %collective-permute-start.5) | collective-permute-done | bytes 258080 | tf_op jit(solution)/shard_map/ppermute | solution.py:33
  37.0 34.0 %while.38 = (s32[]{:T(128)}, f32[3,8,128]{2,1,0:T(8,128)S(1)}, f32[7,8,128]{2,1,0:T(8,128)S(1)}, s32[8,6]{0,1:T(8,128)S(1)}, f32[7,216,128]{2,0,1:T(8,128)S(1)},...) while((s32[]{:T(128)}, f32[3,8,128]{2,1,0:T(8,128)S(1)}, ...), condition=%wide.region_4.8_spmd.clone, body=%wide.region_0.7_spmd.clone.sunk | while | flops 8159435 | bytes 5781167 | solution.py:109
  71.2 3.5 %collective-permute-start.6 = (f32[7,1,1,1,1024]{4,0,3,2,1:T(8,128)S(1)}, f32[7,1,1,1,1024]{4,0,3,2,1:T(8,128)S(1)}, u32[]{:S(2)}, u32[]{:S(2)}) collective-permute-start(f32[7,1,1,1,1024]{4,0,3,2,1:T(8,128)S(1)} %pad_maximum_fusion.6), channel_id=1, source_target_pairs={{0,32},{32,64},{64,96},{96,128},{128,160},{160,192},{192,224},{224... | collective-permute-start | bytes 86024 | tf_op jit(solution)/shard_map/ppermute | solution.py:31
  76.0 4.6 %collective-permute-done.7 = f32[7,1,1,1,1024]{4,0,3,2,1:T(8,128)S(1)} collective-permute-done((f32[7,1,1,1,1024]{4,0,3,2,1:T(8,128)S(1)}, f32[7,1,1,1,1024]{4,0,3,2,1:T(8,128)S(1)}, u32[]{:S(2)}, u32[]{:S(2)}) %collective-permute-start.7) | collective-permute-done | bytes 28704 | tf_op jit(solution)/shard_map/ppermute | solution.py:33
  80.7 3.1 collective-permute-start.8
  85.4 3.7 %collective-permute-done.9 = f32[7,3,1,1,1024]{4,0,3,2,1:T(8,128)S(1)} collective-permute-done((f32[7,3,1,1,1024]{4,0,3,2,1:T(8,128)S(1)}, f32[7,3,1,1,1024]{4,0,3,2,1:T(8,128)S(1)}, u32[]{:S(2)}, u32[]{:S(2)}) %collective-permute-start.9) | collective-permute-done | bytes 86048 | tf_op jit(solution)/shard_map/ppermute | solution.py:33
  89.2 4.8 %collective-permute-start.10 = (f32[7,3,3,1,1024]{4,0,3,2,1:T(8,128)S(1)}, f32[7,3,3,1,1024]{4,0,3,2,1:T(8,128)S(1)}, u32[]{:S(2)}, u32[]{:S(2)}) collective-permute-start(f32[7,3,3,1,1024]{4,0,3,2,1:T(8,128)S(1)} %pad_maximum_fusion.2), channel_id=1, source_target_pairs={{0,1},{1,2},{2,3},{3,4},{4,5},{5,6},{6,7},{8,9},{9,10},{10,11},{11... | collective-permute-start | bytes 774152 | tf_op jit(solution)/shard_map/ppermute | solution.py:31
  94.1 1.9 collective-permute-start.11
  97.7 4.4 %collective-permute-done.11 = f32[7,3,3,1,1024]{4,0,3,2,1:T(8,128)S(1)} collective-permute-done((f32[7,3,3,1,1024]{4,0,3,2,1:T(8,128)S(1)}, f32[7,3,3,1,1024]{4,0,3,2,1:T(8,128)S(1)}, u32[]{:S(2)}, u32[]{:S(2)}) %collective-permute-start.11) | collective-permute-done | bytes 258080 | tf_op jit(solution)/shard_map/ppermute | solution.py:33
  103.9 68.3 %while.39 = (s32[]{:T(128)}, f32[3,8,128]{2,1,0:T(8,128)S(1)}, f32[6,8,128]{2,1,0:T(8,128)S(1)}, f32[8,128]{1,0:T(8,128)S(1)}, f32[8,128]{1,0:T(8,128)S(1)}, /*i...) while((s32[]{:T(128)}, f32[3,8,128]{2,1,0:T(8,128)S(1)}, ...), condition=%wide.region_17.21_spmd.clone, body=%wide.region_5.20_spmd.clone.sunk | while | flops 11313355 | bytes 10154705 | solution.py:109
  104.0 1.7 gather_fusion.5
  106.5 1.7 broadcast_subtract_fusion.2
  109.5 2.8 multiply_reduce_fusion.21
  112.4 1.9 multiply_reduce_fusion.23
  115.4 1.7 gather_fusion.5
  117.8 1.7 broadcast_subtract_fusion.2
  120.9 2.8 multiply_reduce_fusion.21
  123.7 1.9 multiply_reduce_fusion.23
  126.8 1.7 gather_fusion.5
  129.2 1.7 broadcast_subtract_fusion.2
  132.3 2.8 multiply_reduce_fusion.21
  135.1 1.9 multiply_reduce_fusion.23
  138.1 1.7 gather_fusion.5
  140.6 1.7 broadcast_subtract_fusion.2
  143.7 2.8 multiply_reduce_fusion.21
  146.5 1.9 multiply_reduce_fusion.23
  149.5 1.7 gather_fusion.5
  152.0 1.7 broadcast_subtract_fusion.2
  155.1 2.8 multiply_reduce_fusion.21
  157.9 1.9 multiply_reduce_fusion.23
  160.9 1.7 gather_fusion.5
  163.4 1.7 broadcast_subtract_fusion.2
  166.4 2.8 multiply_reduce_fusion.21
  169.3 1.9 multiply_reduce_fusion.23
  173.2 6.4 %scatter_custom_fusion = f32[512,10]{1,0:T(8,128)S(1)} fusion(s32[1024]{0:T(1024)} %bitcast.208, f32[1024,10]{1,0:T(8,128)S(1)} %copy.125, f32[]{:T(128)} %constant.322.clone.1), kind=kCustom, calls=%fused_computation.122 | custom fusion | flops 10240 | bytes 20992 | tf_op jit(solution)/shard_map/scatter-add | solution.py:151
  180.3 2.9 collective-permute-start.12
  185.0 5.7 %collective-permute-done.12 = f32[10,8,6,8]{2,0,3,1:T(8,128)S(1)} collective-permute-done((f32[10,8,6,8]{2,0,3,1:T(8,128)S(1)}, f32[10,8,6,8]{2,0,3,1:T(8,128)S(1)}, u32[]{:S(2)}, u32[]{:S(2)}) %collective-permute-start.12) | collective-permute-done | bytes 15392 | tf_op jit(solution)/shard_map/ppermute | solution.py:31
  190.7 4.1 %collective-permute-done.13 = f32[10,8,6,8]{2,0,3,1:T(8,128)S(1)} collective-permute-done((f32[10,8,6,8]{2,0,3,1:T(8,128)S(1)}, f32[10,8,6,8]{2,0,3,1:T(8,128)S(1)}, u32[]{:S(2)}, u32[]{:S(2)}) %collective-permute-start.13) | collective-permute-done | bytes 15392 | tf_op jit(solution)/shard_map/ppermute | solution.py:33
  194.8 4.5 %convolution_bitcast_fusion = f32[10,8,8,8]{0,2,3,1:T(8,128)S(1)} fusion(f32[10,8,6,8]{2,0,3,1:T(8,128)S(1)} %collective-permute-done.13, f32[10,8,8,8]{2,0,3,1:T(8,128)S(1)} %copy.127, f32[10,8,6,8]{2,0,3,1:T(8,128)S(1)} %collective-permute-done.12, f32[]{:T(128)} %fusion.64), kind=kOutput, calls=%fused_computation.109 | convolution fusion | flops 1256000 | bytes 71684 | tf_op jit(solution)/shard_map/cxez,ye->cxyz/dot_general | solution.py:154
  200.2 8.0 %all-to-all-start = ((f32[8,1,640]{2,1,0:T(1,128)}), f32[8,1,640]{2,1,0:T(1,128)S(1)}, u32[]{:S(2)}, u32[]{:S(2)}) async-start(f32[8,1,640]{2,1,0:T(1,128)} %reshape.490), calls=%async_computation | async-start | bytes 40960 | tf_op jit(solution)/shard_map/all_to_all | solution.py:157
  209.4 106.9 %all-reduce = (f32[1]{0:T(128)}, f32[1]{0:T(128)}, f32[1]{0:T(128)}) all-reduce(f32[1]{0:T(128)} %bitcast.32, f32[1]{0:T(128)} %bitcast.31, f32[1]{0:T(128)} %bitcast.30), channel_id=1, replica_groups=mesh['gx'=16,'gy'=4,'gz'=8] {'gx','gy','gz'}, use_global_device_ids=true, to_apply=%region_26.30 | all-reduce | flops 3 | bytes 24 | tf_op jit(solution)/shard_map/psum | solution.py:169
  321.9 2.6 pad_maximum_fusion.8
  (414 shorter events, 81.8 us)
Async XLA Ops:
  1.4 5.7 %collective-permute-start = (f32[7,1,1,1,1024]{4,3,2,1,0:T(1,128)S(1)}, f32[7,1,1,1,1024]{4,3,2,1,0:T(1,128)S(1)}, u32[]{:S(2)}, u32[]{:S(2)}) collective-permute-start(f32[7,1,1,1,1024]{4,3,2,1,0:T(1,128)S(1)} %pad_maximum_fusion.7), channel_id=1, source_target_pairs={{0,32},{32,64},{64,96},{96,128},{128,160},{160,192},{192,224},{224... | collective-permute-start | bytes 86024 | tf_op jit(solution)/shard_map/ppermute | solution.py:31
  5.8 4.8 %collective-permute-start.1 = (f32[7,1,1,1,1024]{4,3,2,1,0:T(1,128)S(1)}, f32[7,1,1,1,1024]{4,3,2,1,0:T(1,128)S(1)}, u32[]{:S(2)}, u32[]{:S(2)}) collective-permute-start(f32[7,1,1,1,1024]{4,3,2,1,0:T(1,128)S(1)} %pad_maximum_fusion.7), channel_id=1, source_target_pairs={{32,0},{64,32},{96,64},{128,96},{160,128},{192,160},{224,192},{256... | collective-permute-start | bytes 86024 | tf_op jit(solution)/shard_map/ppermute | solution.py:33
  11.4 4.6 %collective-permute-start.2 = (f32[7,3,1,1,1024]{4,3,2,1,0:T(1,128)S(1)}, f32[7,3,1,1,1024]{4,3,2,1,0:T(1,128)S(1)}, u32[]{:S(2)}, u32[]{:S(2)}) collective-permute-start(f32[7,3,1,1,1024]{4,3,2,1,0:T(1,128)S(1)} %pad_maximum_fusion.5), channel_id=1, source_target_pairs={{0,8},{8,16},{16,24},{1,9},{9,17},{17,25},{2,10},{10,18},{18,26},{... | collective-permute-start | bytes 258056 | tf_op jit(solution)/shard_map/ppermute | solution.py:31
  14.5 5.2 %collective-permute-start.3 = (f32[7,3,1,1,1024]{4,3,2,1,0:T(1,128)S(1)}, f32[7,3,1,1,1024]{4,3,2,1,0:T(1,128)S(1)}, u32[]{:S(2)}, u32[]{:S(2)}) collective-permute-start(f32[7,3,1,1,1024]{4,3,2,1,0:T(1,128)S(1)} %pad_maximum_fusion.5), channel_id=1, source_target_pairs={{8,0},{16,8},{24,16},{9,1},{17,9},{25,17},{10,2},{18,10},{26,18},{... | collective-permute-start | bytes 258056 | tf_op jit(solution)/shard_map/ppermute | solution.py:33
  20.8 10.5 %collective-permute-start.4 = (f32[7,3,3,1,1024]{4,3,2,1,0:T(1,128)S(1)}, f32[7,3,3,1,1024]{4,3,2,1,0:T(1,128)S(1)}, u32[]{:S(2)}, u32[]{:S(2)}) collective-permute-start(f32[7,3,3,1,1024]{4,3,2,1,0:T(1,128)S(1)} %pad_maximum_fusion.3), channel_id=1, source_target_pairs={{0,1},{1,2},{2,3},{3,4},{4,5},{5,6},{6,7},{8,9},{9,10},{10,11},{11... | collective-permute-start | bytes 774152 | tf_op jit(solution)/shard_map/ppermute | solution.py:31
  27.2 7.6 %collective-permute-start.5 = (f32[7,3,3,1,1024]{4,3,2,1,0:T(1,128)S(1)}, f32[7,3,3,1,1024]{4,3,2,1,0:T(1,128)S(1)}, u32[]{:S(2)}, u32[]{:S(2)}) collective-permute-start(f32[7,3,3,1,1024]{4,3,2,1,0:T(1,128)S(1)} %pad_maximum_fusion.3), channel_id=1, source_target_pairs={{1,0},{2,1},{3,2},{4,3},{5,4},{6,5},{7,6},{9,8},{10,9},{11,10},{12... | collective-permute-start | bytes 774152 | tf_op jit(solution)/shard_map/ppermute | solution.py:33
  36.3 0.7 copy-start
  36.3 0.7 copy-start.4
  37.0 34.1 %copy-start.1 = (f32[3,1,1,1,1024]{4,3,2,1,0:T(1,128)S(1)}, f32[3,1,1,1,1024]{4,3,2,1,0:T(1,128)}, u32[]{:S(2)}) copy-start(f32[3,1,1,1,1024]{4,3,2,1,0:T(1,128)} %param.18) | copy-start | bytes 36868
  37.0 34.1 %copy-start.3 = (f32[3,1,1,1,1024]{4,3,2,1,0:T(1,128)S(1)}, f32[3,1,1,1,1024]{4,3,2,1,0:T(1,128)}, u32[]{:S(2)}) copy-start(f32[3,1,1,1,1024]{4,3,2,1,0:T(1,128)} %param.19) | copy-start | bytes 36868
  37.0 34.1 %copy-start.2 = (f32[1,1,1,1024]{3,2,1,0:T(1,128)S(1)}, f32[1,1,1,1024]{3,2,1,0:T(1,128)}, u32[]{:S(2)}) copy-start(f32[1,1,1,1024]{3,2,1,0:T(1,128)} %param.20) | copy-start | bytes 12292
  71.2 4.9 %collective-permute-start.6 = (f32[7,1,1,1,1024]{4,0,3,2,1:T(8,128)S(1)}, f32[7,1,1,1,1024]{4,0,3,2,1:T(8,128)S(1)}, u32[]{:S(2)}, u32[]{:S(2)}) collective-permute-start(f32[7,1,1,1,1024]{4,0,3,2,1:T(8,128)S(1)} %pad_maximum_fusion.6), channel_id=1, source_target_pairs={{0,32},{32,64},{64,96},{96,128},{128,160},{160,192},{192,224},{224... | collective-permute-start | bytes 86024 | tf_op jit(solution)/shard_map/ppermute | solution.py:31
  74.7 6.0 %collective-permute-start.7 = (f32[7,1,1,1,1024]{4,0,3,2,1:T(8,128)S(1)}, f32[7,1,1,1,1024]{4,0,3,2,1:T(8,128)S(1)}, u32[]{:S(2)}, u32[]{:S(2)}) collective-permute-start(f32[7,1,1,1,1024]{4,0,3,2,1:T(8,128)S(1)} %pad_maximum_fusion.6), channel_id=1, source_target_pairs={{32,0},{64,32},{96,64},{128,96},{160,128},{192,160},{224,192},{256... | collective-permute-start | bytes 86024 | tf_op jit(solution)/shard_map/ppermute | solution.py:33
  80.7 4.7 %collective-permute-start.8 = (f32[7,3,1,1,1024]{4,0,3,2,1:T(8,128)S(1)}, f32[7,3,1,1,1024]{4,0,3,2,1:T(8,128)S(1)}, u32[]{:S(2)}, u32[]{:S(2)}) collective-permute-start(f32[7,3,1,1,1024]{4,0,3,2,1:T(8,128)S(1)} %pad_maximum_fusion.4), channel_id=1, source_target_pairs={{0,8},{8,16},{16,24},{1,9},{9,17},{17,25},{2,10},{10,18},{18,26},{... | collective-permute-start | bytes 258056 | tf_op jit(solution)/shard_map/ppermute | solution.py:31
  83.8 5.4 %collective-permute-start.9 = (f32[7,3,1,1,1024]{4,0,3,2,1:T(8,128)S(1)}, f32[7,3,1,1,1024]{4,0,3,2,1:T(8,128)S(1)}, u32[]{:S(2)}, u32[]{:S(2)}) collective-permute-start(f32[7,3,1,1,1024]{4,0,3,2,1:T(8,128)S(1)} %pad_maximum_fusion.4), channel_id=1, source_target_pairs={{8,0},{16,8},{24,16},{9,1},{17,9},{25,17},{10,2},{18,10},{26,18},{... | collective-permute-start | bytes 258056 | tf_op jit(solution)/shard_map/ppermute | solution.py:33
  89.2 8.5 %collective-permute-start.10 = (f32[7,3,3,1,1024]{4,0,3,2,1:T(8,128)S(1)}, f32[7,3,3,1,1024]{4,0,3,2,1:T(8,128)S(1)}, u32[]{:S(2)}, u32[]{:S(2)}) collective-permute-start(f32[7,3,3,1,1024]{4,0,3,2,1:T(8,128)S(1)} %pad_maximum_fusion.2), channel_id=1, source_target_pairs={{0,1},{1,2},{2,3},{3,4},{4,5},{5,6},{6,7},{8,9},{9,10},{10,11},{11... | collective-permute-start | bytes 774152 | tf_op jit(solution)/shard_map/ppermute | solution.py:31
  94.1 8.0 %collective-permute-start.11 = (f32[7,3,3,1,1024]{4,0,3,2,1:T(8,128)S(1)}, f32[7,3,3,1,1024]{4,0,3,2,1:T(8,128)S(1)}, u32[]{:S(2)}, u32[]{:S(2)}) collective-permute-start(f32[7,3,3,1,1024]{4,0,3,2,1:T(8,128)S(1)} %pad_maximum_fusion.2), channel_id=1, source_target_pairs={{1,0},{2,1},{3,2},{4,3},{5,4},{6,5},{7,6},{9,8},{10,9},{11,10},{12... | collective-permute-start | bytes 774152 | tf_op jit(solution)/shard_map/ppermute | solution.py:33
  180.3 10.5 %collective-permute-start.12 = (f32[10,8,6,8]{2,0,3,1:T(8,128)S(1)}, f32[10,8,6,8]{2,0,3,1:T(8,128)S(1)}, u32[]{:S(2)}, u32[]{:S(2)}) collective-permute-start(f32[10,8,6,8]{2,0,3,1:T(8,128)S(1)} %get-tuple-element.929), channel_id=1, source_target_pairs={{0,8},{8,16},{16,24},{1,9},{9,17},{17,25},{2,10},{10,18},{18,26},{... | collective-permute-start | bytes 46088 | tf_op jit(solution)/shard_map/ppermute | solution.py:31
  183.1 11.7 %collective-permute-start.13 = (f32[10,8,6,8]{2,0,3,1:T(8,128)S(1)}, f32[10,8,6,8]{2,0,3,1:T(8,128)S(1)}, u32[]{:S(2)}, u32[]{:S(2)}) collective-permute-start(f32[10,8,6,8]{2,0,3,1:T(8,128)S(1)} %get-tuple-element.930), channel_id=1, source_target_pairs={{8,0},{16,8},{24,16},{9,1},{17,9},{25,17},{10,2},{18,10},{26,18},{... | collective-permute-start | bytes 46088 | tf_op jit(solution)/shard_map/ppermute | solution.py:33
  200.2 116.1 %all-to-all-start = ((f32[8,1,640]{2,1,0:T(1,128)}), f32[8,1,640]{2,1,0:T(1,128)S(1)}, u32[]{:S(2)}, u32[]{:S(2)}) async-start(f32[8,1,640]{2,1,0:T(1,128)} %reshape.490), calls=%async_computation | async-start | bytes 40960 | tf_op jit(solution)/shard_map/all_to_all | solution.py:157
  319.3 6.4 %collective-permute-start.14 = (f32[10,6,1,64]{3,0,1,2:T(8,128)S(1)}, f32[10,6,1,64]{3,0,1,2:T(8,128)S(1)}, u32[]{:S(2)}, u32[]{:S(2)}) collective-permute-start(f32[10,6,1,64]{3,0,1,2:T(8,128)S(1)} %get-tuple-element.931), channel_id=1, source_target_pairs={{0,32},{32,64},{64,96},{96,128},{128,160},{160,192},{192,224},{224... | collective-permute-start | bytes 46088 | tf_op jit(solution)/shard_map/ppermute | solution.py:31
  320.6 5.1 %collective-permute-start.15 = (f32[10,6,1,64]{3,0,1,2:T(8,128)S(1)}, f32[10,6,1,64]{3,0,1,2:T(8,128)S(1)}, u32[]{:S(2)}, u32[]{:S(2)}) collective-permute-start(f32[10,6,1,64]{3,0,1,2:T(8,128)S(1)} %get-tuple-element.932), channel_id=1, source_target_pairs={{32,0},{64,32},{96,64},{128,96},{160,128},{192,160},{224,192},{256... | collective-permute-start | bytes 46088 | tf_op jit(solution)/shard_map/ppermute | solution.py:33
where the time goes:
time: 330 us; the launch traced here: 328 us
  blocking collectives  107 us (32%)
  other arithmetic  91.7 us (28%)
  starting transfers between devices  49.2 us (15%)
  waiting for transfers between devices  35.7 us (11%)
  local copies, waits for them, and re-layouts  35.1 us (11%)
  matrix products  6.19 us (2%)
    psum x1, blocking collectives, shards(): lax.psum((jnp.sum(kinetic), jnp.sum(contact), jnp.sum(bonding)), ('gx', '...  107 us
    ppermute x8, starting transfers between devices, extended(): lax.ppermute(tail, axis, [(i, (i + 1) % count) for i in range(ends)])  29.6 us
    ppermute x8, waiting for transfers between devices, extended(): lax.ppermute(head, axis, [((i + 1) % count, i) for i in range(ends)])  27.8 us
    reduce_sum x6, other arithmetic, pair_terms(): bond_energy = jnp.sum(0.5 * KB * stretch * stretch * window, axis=2)  17 us
    gather x12, local copies, waits for them, and re-layouts, visit(): partner = jnp.take(tiles, picked, axis=1)  13.6 us
    ppermute x8, starting transfers between devices, extended(): lax.ppermute(head, axis, [((i + 1) % count, i) for i in range(ends)])  11.6 us
    reduce_sum x6, other arithmetic, pair_terms(): jnp.sum(scaled * offsets[first] * offsets[second], axis=2)  11.6 us
    reduce_sum x12, other arithmetic, pair_terms(): force = jnp.sum(magnitude[None] * direction, axis=3)  10.8 us
  transfers between devices with their start and end apart: 17, of which 11 were waited for; matrix products, arithmetic and copies ran while one was open for 2% of the time, Pallas kernels for 0%

commit v1 on v0

v1 whole, which is shorter than its diff:
```python
import math

import jax
import jax.numpy as jnp
from jax import lax
from jax.experimental import pallas as pl
from jax.experimental.pallas import tpu as pltpu
from jax.sharding import PartitionSpec as P

STEPS = 2
CX = 8
CY = 8
CZ = 8
SIGMA = 2
HW = 6
KN = 1.0
GAMMA = 1.0
KB = 2.0
REACH = 1.5
STEP_DT = 0.02
DENS = 4.0
SOFT = 0.0001

NT = 8
K = 6
FAR = -1.0e9
LIVE = 1024
INSIDE = 2048
ITSELF = 4096
COMPS = 10
VMEM = pl.BlockSpec(memory_space=pltpu.VMEM)
SMEM = pl.BlockSpec(memory_space=pltpu.SMEM)

RAW = [math.exp(-d * d / (2.0 * SIGMA * SIGMA)) for d in range(HW + 1)]
TOTAL = RAW[0] + 2.0 * sum(RAW[1:])
GAUSS = [w / TOTAL for w in RAW]


def row(tile, index):
    return jnp.broadcast_to(tile[index : index + 1, :], (8, 128))


def pair_sums(tiles, meta, base, own, second):
    xi, yi, zi = row(own, 0), row(own, 1), row(own, 2)
    ui, vi, wi = row(own, 3), row(own, 4), row(own, 5)
    ri = row(own, 6)
    sub = lax.broadcasted_iota(jnp.int32, (8, 128), 0)
    lane = lax.broadcasted_iota(jnp.int32, (8, 128), 1)
    zero = jnp.zeros((8, 128), jnp.float32)
    count = 10 if second else 3
    sums = [zero] * count
    for slot in range(K):
        entry = meta[base + slot]
        partner = tiles[lax.bitwise_and(entry, 1023)]
        live = lax.bitwise_and(entry, LIVE) > 0
        dead = jnp.logical_and(sub == 6, jnp.logical_or(partner <= 0.0, jnp.logical_not(live)))
        partner = jnp.where(dead, FAR, partner)
        columns = partner.T
        if second:
            selfrow = jnp.where(lax.bitwise_and(entry, ITSELF) > 0, lane, -1)
        for chunk in range(16):
            part = columns[8 * chunk : 8 * chunk + 8, :]
            col = [jnp.broadcast_to(part[:, c : c + 1], (8, 128)) for c in range(7)]
            dx, dy, dz = col[0] - xi, col[1] - yi, col[2] - zi
            square = dx * dx + dy * dy + (dz * dz + SOFT)
            inverse = lax.rsqrt(square)
            inter = jnp.maximum((col[6] + ri) - square * inverse, 0.0)
            root = inter * lax.rsqrt(jnp.maximum(inter, 1e-30))
            closing = ((col[3] - ui) * dx + (col[4] - vi) * dy + (col[5] - wi) * dz) * inverse
            scaled = root * (GAMMA * closing - KN * inter) * inverse
            fx, fy, fz = scaled * dx, scaled * dy, scaled * dz
            sums[0] = sums[0] + fx
            sums[1] = sums[1] + fy
            sums[2] = sums[2] + fz
            if second:
                sums[3] = sums[3] + fx * dx
                sums[4] = sums[4] + fy * dy
                sums[5] = sums[5] + fz * dz
                sums[6] = sums[6] + fx * dy
                sums[7] = sums[7] + fx * dz
                sums[8] = sums[8] + fy * dz
                energy = inter * inter * root
                sums[9] = sums[9] + jnp.where(sub + 8 * chunk == selfrow, 0.0, energy)
    return sums


def bond_sums(tiles, entry, own, second, sums):
    xi, yi, zi, ri = row(own, 0), row(own, 1), row(own, 2), row(own, 6)
    code = row(own, 7)
    code = jnp.where(code < 0.0, -5.0, code)
    sub = lax.broadcasted_iota(jnp.int32, (8, 128), 0)
    lane = lax.broadcasted_iota(jnp.int32, (8, 128), 1)
    partner = tiles[lax.bitwise_and(entry, 1023)]
    columns = partner.T
    selfrow = jnp.where(lax.bitwise_and(entry, ITSELF) > 0, lane, -1)
    held = [sums[i] for i in range(11 if second else 3)]
    for chunk in range(16):
        part = columns[8 * chunk : 8 * chunk + 8, :]
        xj, yj, zj, rj, cj = [
            jnp.broadcast_to(part[:, c : c + 1], (8, 128)) for c in (0, 1, 2, 6, 7)
        ]
        dx, dy, dz = xj - xi, yj - yi, zj - zi
        square = dx * dx + dy * dy + (dz * dz + SOFT)
        inverse = lax.rsqrt(square)
        distance = square * inverse
        reach = rj + ri
        bonded = jnp.logical_and(cj == code, sub + 8 * chunk != selfrow)
        bonded = jnp.logical_and(bonded, rj > 0.0)
        window = jnp.maximum(1.0 - distance / (REACH * reach), 0.0)
        window = jnp.where(bonded, window * window, 0.0)
        stretch = distance - reach
        pull = stretch * window
        scaled = KB * pull * inverse
        fx, fy, fz = scaled * dx, scaled * dy, scaled * dz
        held[0] = held[0] + fx
        held[1] = held[1] + fy
        held[2] = held[2] + fz
        if second:
            held[3] = held[3] + fx * dx
            held[4] = held[4] + fy * dy
            held[5] = held[5] + fz * dz
            held[6] = held[6] + fx * dy
            held[7] = held[7] + fx * dz
            held[8] = held[8] + fy * dz
            held[10] = held[10] + pull * stretch
    for i, value in enumerate(held):
        sums[i] = value


def tile_sums(tiles, meta, base, own, second, sums):
    for i, value in enumerate(pair_sums(tiles, meta, base, own, second)):
        sums[i] = value
    if second:
        sums[10] = jnp.zeros((8, 128), jnp.float32)

    @pl.loop(0, K)
    def _(slot):
        entry = meta[base + slot]

        @pl.when(lax.bitwise_and(entry, INSIDE) > 0)
        def _():
            bond_sums(tiles, entry, own, second, sums)


def folded(value):
    return jnp.sum(value, axis=0, keepdims=True)


def fill(tiles, low, middle, high, size):
    for part, ref in enumerate((low, middle, high)):
        for i in range(size):
            tiles[part * size + i] = ref[i]


def first_kernel(meta, low, middle, high, out, tiles, sums):
    width = middle.shape[0] // 3
    fill(tiles, low, middle, high, 3 * width)
    sub = lax.broadcasted_iota(jnp.int32, (8, 128), 0)

    @pl.loop(0, width - 2)
    def _(t):
        own = tiles[4 * width + t + 1]
        tile_sums(tiles, meta, t * 8, own, False, sums)
        radius = own[6:7, :]
        gain = STEP_DT / (DENS * radius * radius * radius)
        fresh = own
        for axis in range(3):
            speed = own[3 + axis : 4 + axis, :] + gain * folded(sums[axis])
            place = own[axis : axis + 1, :] + STEP_DT * speed
            fresh = jnp.where(sub == axis, place, fresh)
            fresh = jnp.where(sub == 3 + axis, speed, fresh)
        out[t] = fresh


def second_kernel(
    meta, cell, low, middle, high, place_out, speed_out, grid_out, energy_out, tiles, sums, left, right, total
):
    width = middle.shape[0] // 3
    fill(tiles, low, middle, high, 3 * width)
    sub = lax.broadcasted_iota(jnp.int32, (8, 128), 0)
    line = lax.broadcasted_iota(jnp.int32, (64, 128), 0)
    total[...] = jnp.zeros((8, 128), jnp.float32)
    right[...] = jnp.zeros(right.shape, jnp.bfloat16)

    for t in range(NT):
        own = tiles[4 * width + t + 1]
        tile_sums(tiles, meta, t * 8, own, True, sums)
        radius = own[6:7, :]
        mass = DENS * radius * radius * radius
        gain = STEP_DT / mass
        values = [-0.5 * folded(sums[3 + i]) for i in range(6)]
        squares = jnp.zeros((1, 128), jnp.float32)
        for axis in range(3):
            speed = own[3 + axis : 4 + axis, :] + gain * folded(sums[axis])
            speed_out[axis, t : t + 1, :] = speed
            place_out[axis, t : t + 1, :] = own[axis : axis + 1, :] + STEP_DT * speed
            squares = squares + speed * speed
            values.append(mass * speed)
        kinetic = 0.5 * mass * squares
        values.append(kinetic)
        contact = 0.4 * KN * folded(sums[9])
        bond = 0.5 * KB * folded(sums[10])
        added = jnp.where(sub == 0, kinetic, jnp.where(sub == 1, contact, jnp.where(sub == 2, bond, 0.0)))
        total[...] = total[...] + added
        where = cell[t : t + 1, :]
        span = slice(128 * t, 128 * t + 128)
        in_plane = sub == lax.shift_right_logical(where, 6)
        for c in range(0, COMPS, 2):
            pair = jnp.concatenate(
                [jnp.where(in_plane, values[c], 0.0), jnp.where(in_plane, values[c + 1], 0.0)], axis=0
            )
            coarse = pair.astype(jnp.bfloat16)
            fine = (pair - coarse.astype(jnp.float32)).astype(jnp.bfloat16)
            right[8 * c : 8 * c + 16, span] = coarse
            right[128 + 8 * c : 128 + 8 * c + 16, span] = fine
        left[:, span] = jnp.where(line == lax.bitwise_and(where, 63), 1.0, 0.0).astype(jnp.bfloat16)

    both = lax.dot_general(
        left[...], right[...], (((1,), (1,)), ((), ())), preferred_element_type=jnp.float32
    )
    scale = float(CX * CY * CZ) / float(NT * 128)
    grid_out[...] = (both[:, 0:128] + both[:, 128:256]) * scale
    for i in range(energy_out.shape[0]):
        energy_out[i] = total[...]


def plane_kernel(coords, own, before, after, energy, out):
    lane = lax.broadcasted_iota(jnp.int32, (8, 128), 1)
    inner = lax.bitwise_and(lane, 7)
    sums = energy[0]
    for i in range(1, energy.shape[0]):
        sums = sums + energy[i]
    sums = jnp.where(lane == 8 * COMPS, jnp.sum(sums, axis=1, keepdims=True), 0.0)
    planes = []
    for y in range(CY):
        block = slice(8 * y, 8 * y + 8)
        here = own[block, :]
        low = pltpu.roll(before[block, :], 120, 1)
        high = pltpu.roll(after[block, :], 8, 1)
        smooth = GAUSS[0] * here
        for d in range(1, HW + 1):
            ahead = pltpu.roll(jnp.where(inner >= d, here, high), 128 - d, 1)
            behind = pltpu.roll(jnp.where(inner < 8 - d, here, low), d, 1)
            smooth = smooth + GAUSS[d] * (ahead + behind)
        planes.append(smooth)
    rows = out.shape[0]
    for j in range(rows):
        out[j] = sums
    start = coords[1] * CY
    for r in range(-HW, CY + HW):
        mixed = sums
        for y in range(CY):
            if abs(r - y) <= HW:
                mixed = mixed + GAUSS[abs(r - y)] * planes[y]

        @pl.when(jnp.logical_and(start + r >= 0, start + r < rows))
        def _():
            out[start + r] = mixed


def line_kernel(parts, stress, motion, energies):
    count = parts.shape[0] // 8
    lane = lax.broadcasted_iota(jnp.int32, (8, 128), 1)
    sub = lax.broadcasted_iota(jnp.int32, (8, 128), 0)
    lines = []
    for block in range(8):
        line = parts[block]
        for other in range(1, count):
            line = line + parts[8 * other + block]
        lines.append(line)
    whole = lines[0]
    for line in lines[1:]:
        whole = whole + line
    for i in range(3):
        energies[i] = jnp.sum(jnp.where(jnp.logical_and(sub == i, lane == 8 * COMPS), whole, 0.0))
    empty = jnp.zeros((8, 128), jnp.float32)
    out = []
    for block in range(8):
        here = lines[block]
        low = lines[block - 1] if block > 0 else empty
        high = lines[block + 1] if block < 7 else empty
        smooth = GAUSS[0] * here
        for d in range(1, HW + 1):
            ahead = pltpu.roll(jnp.where(sub >= d, here, high), 8 - d, 0)
            behind = pltpu.roll(jnp.where(sub < 8 - d, here, low), d, 0)
            smooth = smooth + GAUSS[d] * (ahead + behind)
        out.append(smooth)
    turned = jnp.concatenate(out, axis=0).T
    for c in range(6):
        stress[c] = turned[8 * c : 8 * c + 8, :]
    for c in range(4):
        motion[c] = turned[48 + 8 * c : 56 + 8 * c, :]


def pack_kernel(place, speed, radius, group, broken, lists, counts, out, to_left, to_right):
    code = jnp.where(broken[...] == 0, group[...].astype(jnp.float32), -1.0)
    for t in range(NT):
        for axis in range(3):
            out[t, axis : axis + 1, :] = place[axis, t : t + 1, :]
            out[t, 3 + axis : 4 + axis, :] = speed[axis, t : t + 1, :]
        out[t, 6:7, :] = radius[t : t + 1, :]
        out[t, 7:8, :] = code[t : t + 1, :]
    for ref, edge, first in ((to_left, 0, 0), (to_right, NT - 1, NT - 2)):
        ref[0] = out[first]
        ref[1] = out[first + 1]
        ref[2] = jnp.zeros((8, 128), jnp.float32)
        ref[2, 0:1, 0:K] = lists[edge : edge + 1, :].astype(jnp.float32)
        ref[2, 1:2, 0:NT] = counts[...].astype(jnp.float32)


def shifted(value, axis, step, wrap):
    count = lax.axis_size(axis)
    pairs = [(i, (i + step) % count) for i in range(count) if wrap or 0 <= i + step < count]
    return lax.ppermute(value, axis, pairs)


def list_entries(lists, counts, home, shift, width, margin):
    offset = lists // NT
    along = offset // 9 - 1
    across = offset // 3 % 3
    up = offset % 3
    spot = jnp.clip((along + shift) * NT + lists % NT + margin, 0, width - 1)

    def within(axis, step):
        moved = lax.axis_index(axis) + step
        return (moved >= 0) & (moved < lax.axis_size(axis))

    live = lax.broadcasted_iota(jnp.int32, lists.shape, 1) < counts
    live = live & within("gx", shift) & within("gx", shift + along)
    live = live & within("gy", across - 1) & within("gz", up - 1)
    inside = live & (offset == 13)
    itself = inside & (spot == home)
    entry = up * (3 * width) + across * width + spot
    entry = entry + LIVE * live.astype(jnp.int32) + INSIDE * inside.astype(jnp.int32)
    entry = entry + ITSELF * itself.astype(jnp.int32)
    return jnp.pad(entry, ((0, 0), (0, 8 - K))).reshape(-1)


def shards(positions, velocities, radius, group, broken, cell, neighbours, counts):
    lists = neighbours.reshape(NT, K)
    listed = counts.reshape(1, NT)
    tile = jax.ShapeDtypeStruct((NT, 8, 128), jnp.float32)
    edge = jax.ShapeDtypeStruct((3, 8, 128), jnp.float32)
    own, to_left, to_right = pl.pallas_call(
        pack_kernel,
        out_shape=(tile, edge, edge),
        in_specs=[VMEM] * 7,
        out_specs=(VMEM, VMEM, VMEM),
        name="pack",
    )(
        positions.reshape(3, NT, 128),
        velocities.reshape(3, NT, 128),
        radius.reshape(NT, 128),
        group.reshape(NT, 128),
        broken.reshape(NT, 128),
        lists,
        listed,
    )
    from_left = shifted(to_right, "gx", 1, True)
    from_right = shifted(to_left, "gx", -1, True)
    line = jnp.concatenate([from_left[0:2], own, from_right[0:2]], axis=0)
    width = NT + 4

    def extended(tiles):
        up = shifted(tiles, "gy", 1, False)
        down = shifted(tiles, "gy", -1, False)
        middle = jnp.concatenate([up, tiles, down], axis=0)
        low = shifted(middle, "gz", 1, True)
        high = shifted(middle, "gz", -1, True)
        return low, middle, high

    low, middle, high = extended(line)
    all_lists = jnp.concatenate(
        [from_left[2, 0:1, 0:K].astype(jnp.int32), lists, from_right[2, 0:1, 0:K].astype(jnp.int32)], axis=0
    )
    all_counts = jnp.concatenate(
        [from_left[2, 1, NT - 1 : NT].astype(jnp.int32), listed[0], from_right[2, 1, 0:1].astype(jnp.int32)]
    )
    spots = lax.broadcasted_iota(jnp.int32, (NT + 2, 1), 0)
    shift = jnp.where(spots == 0, -1, jnp.where(spots == NT + 1, 1, 0))
    first_meta = list_entries(all_lists, all_counts[:, None], spots + 1, shift, width, 2)
    spots = lax.broadcasted_iota(jnp.int32, (NT, 1), 0)
    second_meta = list_entries(lists, listed.reshape(NT, 1), spots + 1, 0, width - 2, 1)

    line = pl.pallas_call(
        first_kernel,
        out_shape=jax.ShapeDtypeStruct((width - 2, 8, 128), jnp.float32),
        in_specs=[SMEM] + [VMEM] * 3,
        out_specs=VMEM,
        scratch_shapes=[
            pltpu.VMEM((9 * width, 8, 128), jnp.float32),
            pltpu.VMEM((11, 8, 128), jnp.float32),
        ],
        name="first_step",
    )(first_meta, low, middle, high)
    low, middle, high = extended(line)
    width = width - 2
    peers = lax.axis_size("gx")
    block = jax.ShapeDtypeStruct((3, NT, 128), jnp.float32)
    places, speeds, grid, energy = pl.pallas_call(
        second_kernel,
        out_shape=(
            block,
            block,
            jax.ShapeDtypeStruct((64, 128), jnp.float32),
            jax.ShapeDtypeStruct((peers, 8, 128), jnp.float32),
        ),
        in_specs=[SMEM] + [VMEM] * 4,
        out_specs=(VMEM,) * 4,
        scratch_shapes=[
            pltpu.VMEM((9 * width, 8, 128), jnp.float32),
            pltpu.VMEM((11, 8, 128), jnp.float32),
            pltpu.VMEM((64, NT * 128), jnp.bfloat16),
            pltpu.VMEM((256, NT * 128), jnp.bfloat16),
            pltpu.VMEM((8, 128), jnp.float32),
        ],
        name="second_step",
    )(second_meta, cell.reshape(NT, 128), low, middle, high)
    energy = lax.all_to_all(energy, "gx", 0, 0, tiled=True)
    before = shifted(grid, "gx", 1, False)
    after = shifted(grid, "gx", -1, False)
    coords = jnp.stack([lax.axis_index(a) for a in ("gx", "gy", "gz")])
    rows = lax.axis_size("gy") * lax.axis_size("gz")
    parts = pl.pallas_call(
        plane_kernel,
        out_shape=jax.ShapeDtypeStruct((rows, 8, 128), jnp.float32),
        in_specs=[SMEM] + [VMEM] * 4,
        out_specs=VMEM,
        name="planes",
    )(coords, grid, before, after, energy)
    parts = lax.all_to_all(parts, ("gy", "gz"), 0, 0, tiled=True)
    stress, motion, energies = pl.pallas_call(
        line_kernel,
        out_shape=(
            jax.ShapeDtypeStruct((6, 8, 64), jnp.float32),
            jax.ShapeDtypeStruct((4, 8, 64), jnp.float32),
            jax.ShapeDtypeStruct((3,), jnp.float32),
        ),
        in_specs=[VMEM],
        out_specs=(VMEM, VMEM, SMEM),
        name="lines",
    )(parts)
    return (
        places.reshape(positions.shape),
        speeds.reshape(velocities.shape),
        stress.reshape(6, CX, 1, 64),
        motion.reshape(4, CX, 1, 64),
        energies,
    )


def solution(mesh):
    placed = (
        P(None, "gx", "gy", "gz", None),
        P(None, "gx", "gy", "gz", None),
        P("gx", "gy", "gz", None),
        P("gx", "gy", "gz", None),
        P("gx", "gy", "gz", None),
        P("gx", "gy", "gz", None),
        P("gx", "gy", "gz", None, None),
        P("gx", "gy", "gz", None),
    )
    return jax.shard_map(
        shards,
        mesh=mesh,
        in_specs=placed,
        out_specs=(
            P(None, "gx", "gy", "gz", None),
            P(None, "gx", "gy", "gz", None),
            P(None, "gx", ("gy", "gz"), None),
            P(None, "gx", ("gy", "gz"), None),
            P(),
        ),
        check_vma=False,
    )
```

time: 330 us -> 127 us (0.38)
  other arithmetic: 91.7 us -> 1.64 us
  blocking collectives: 107 us -> 19.5 us
  Pallas kernels: 0 us -> 37.5 us
  local copies, waits for them, and re-layouts: 35.1 us -> 8.21 us
  waiting for transfers between devices: 35.7 us -> 10.7 us
  matrix products: 6.19 us -> 0 us
    psum x1 -> x0, blocking collectives: 107 us -> none  [shards(): lax.psum((jnp.sum(kinetic), jnp.sum(contact), jnp.sum(bonding)), ('gx', '...]
    reduce_sum x47 -> x0, other arithmetic: 53.6 us -> none  [the longest x6 17 us: pair_terms(): bond_energy = jnp.sum(0.5 * KB * stretch * stretch * window, axis=2)]
    pallas_call x0 -> x5, Pallas kernels: none -> 37.5 us  [the longest x1 17.6 us: shards(): pl.pallas_call(first_kernel, out_shape=jax.ShapeDtypeStruct((width - 2, 8...]
    ppermute x16 -> x12, waiting for transfers between devices: 35.7 us -> 5.46 us  [shifted(): return lax.ppermute(value, axis, pairs)]
    gather x36 -> x0, local copies, waits for them, and re-layouts: 26.9 us -> none  [the longest x12 13.6 us: visit(): partner = jnp.take(tiles, picked, axis=1)]
    all_to_all x0 -> x1, blocking collectives: none -> 19.5 us  [shards(): parts = lax.all_to_all(parts, ('gy', 'gz'), 0, 0, tiled=True)]
    sub x7 -> x0, other arithmetic: 10.8 us -> none  [the longest x6 10.1 us: pair_terms(): offsets = partner[0:3, :, None, :] - own_tile[0:3, :, :, None]]
    scatter-add x1 -> x0, other arithmetic: 6.39 us -> none  [shards(): jax.ops.segment_sum(values.T, cell.reshape(width), num_segments=CX * CY *...]
  transfers between devices with their start and end apart: 17 -> 13, of which waited for: 11 -> 7; matrix products, arithmetic and copies ran while one was open for 2% -> 3% of each run, Pallas kernels for 0% -> 0%
where the time goes in v1:
time: 127 us; the launch traced here: 126 us
  starting transfers between devices  46.5 us (37%)
  Pallas kernels  37.5 us (30%)
  blocking collectives  19.5 us (15%)
  waiting for transfers between devices  10.7 us (8%)
  local copies, waits for them, and re-layouts  8.21 us (6%)
  between operations  2.37 us (2%)
  other arithmetic  1.64 us (1%)
    ppermute x12, starting transfers between devices, shifted(): return lax.ppermute(value, axis, pairs)  37.8 us
    all_to_all x1, blocking collectives, shards(): parts = lax.all_to_all(parts, ('gy', 'gz'), 0, 0, tiled=True)  19.5 us
    pallas_call x1, Pallas kernels, shards(): pl.pallas_call(first_kernel, out_shape=jax.ShapeDtypeStruct((width - 2, 8...  17.6 us
    pallas_call x1, Pallas kernels, shards(): pl.pallas_call(second_kernel, out_shape=(block, block, jax.ShapeDtypeStru...  14.9 us
    all_to_all x1, starting transfers between devices, shards(): energy = lax.all_to_all(energy, 'gx', 0, 0, tiled=True)  8.67 us
    ppermute x12, waiting for transfers between devices, shifted(): return lax.ppermute(value, axis, pairs)  5.46 us
    all_to_all x1, waiting for transfers between devices, shards(): energy = lax.all_to_all(energy, 'gx', 0, 0, tiled=True)  5.25 us
    unnamed x35, local copies, waits for them, and re-layouts  5.21 us
  transfers between devices with their start and end apart: 13, of which 7 were waited for; matrix products, arithmetic and copies ran while one was open for 3% of the time, Pallas kernels for 0%

profile of v1, /device:TPU:1, one launch (start us, length us, event | category | flops | bytes accessed | tf_op | source)
XLA Modules:
  0.0 126.4 jit_solution(351923280890739519)
XLA Ops:
  0.6 1.4 %copy.18 = s32[1,1,1,8,6]{4,3,2,1,0:T(8,128)} copy(s32[1,1,1,8,6]{3,2,4,1,0:T(1,128)} %param.14) | data formatting | bytes 384 | tf_op args[6]
  2.0 1.4 %pack.1 = (f32[8,8,128]{2,1,0:T(8,128)}, f32[3,8,128]{2,1,0:T(8,128)}, f32[3,8,128]{2,1,0:T(8,128)}) custom-call(f32[3,8,128]{2,1,0:T(8,128)} %bitcast.29, f32[3,8,128]{2,1,0:T(8,128)} %bitcast.30, f32[8,128]{1,0:T(8,128)} %bitcast.35, s32[8,128]{1,0:T(8,128)} %bitcast.36, s32[8,128]{1,0:T(8,128)} %bitcast.37, s32[8,6]{1,0:T(8,128)} %bitcast.27, s32[1,8]{1,0:T(1,128)} %bitcast.31), custom_call_target="tpu_custom_call" | custom-call | tf_op jit(solution)/shard_map/pack/pallas_call | solution.py:344
  3.4 4.5 %collective-permute-start = (f32[3,8,128]{2,1,0:T(8,128)}, f32[3,8,128]{2,1,0:T(8,128)S(1)}, u32[]{:S(2)}, u32[]{:S(2)}) collective-permute-start(f32[3,8,128]{2,1,0:T(8,128)} %get-tuple-element.15), channel_id=1, source_target_pairs={{0,32},{32,64},{64,96},{96,128},{128,160},{160,192},{192,224},{224... | collective-permute-start | bytes 36872 | tf_op jit(solution)/shard_map/ppermute | solution.py:314
  7.9 9.5 %collective-permute-start.1 = (f32[3,8,128]{2,1,0:T(8,128)}, f32[3,8,128]{2,1,0:T(8,128)S(1)}, u32[]{:S(2)}, u32[]{:S(2)}) collective-permute-start(f32[3,8,128]{2,1,0:T(8,128)} %get-tuple-element.16), channel_id=1, source_target_pairs={{0,480},{32,0},{64,32},{96,64},{128,96},{160,128},{192,160},{224,1... | collective-permute-start | bytes 36872 | tf_op jit(solution)/shard_map/ppermute | solution.py:314
  17.4 0.0 collective-permute-done
  17.5 0.0 copy-start.12
  17.5 0.6 copy-done.12
  18.1 0.4 collective-permute-done.1
  18.4 0.7 slice-done
  19.1 1.4 %collective-permute-start.3 = (f32[12,8,128]{2,1,0:T(8,128)S(1)}, f32[12,8,128]{2,1,0:T(8,128)S(1)}, u32[]{:S(2)}, u32[]{:S(2)}) collective-permute-start(f32[12,8,128]{2,1,0:T(8,128)S(1)} %pad_maximum_fusion.1), channel_id=1, source_target_pairs={{8,0},{16,8},{24,16},{9,1},{17,9},{25,17},{10,2},{18,10},{26,18},{... | collective-permute-start | bytes 147464 | tf_op jit(solution)/shard_map/ppermute | solution.py:314
  20.5 4.0 %collective-permute-start.2 = (f32[12,8,128]{2,1,0:T(8,128)S(1)}, f32[12,8,128]{2,1,0:T(8,128)S(1)}, u32[]{:S(2)}, u32[]{:S(2)}) collective-permute-start(f32[12,8,128]{2,1,0:T(8,128)S(1)} %pad_maximum_fusion.1), channel_id=1, source_target_pairs={{0,8},{8,16},{16,24},{1,9},{9,17},{17,25},{2,10},{10,18},{18,26},{... | collective-permute-start | bytes 147464 | tf_op jit(solution)/shard_map/ppermute | solution.py:314
  24.6 0.6 slice.26
  25.8 0.5 slice.27
  27.0 0.0 copy-start.14
  27.0 0.6 copy-done.14
  27.6 0.1 pad_add_fusion.1
  27.7 0.0 collective-permute-done.2
  27.8 0.0 copy-start.8
  27.8 2.1 %collective-permute-start.5 = (f32[36,8,128]{2,1,0:T(8,128)S(1)}, f32[36,8,128]{2,1,0:T(8,128)S(1)}, u32[]{:S(2)}, u32[]{:S(2)}) collective-permute-start(f32[36,8,128]{2,1,0:T(8,128)S(1)} %constant_dynamic-update-slice_fusion.middle), channel_id=1, source_target_pairs={{0,7},{1,0},{2,1},{3,2},{4,3},{5,4},{6,5},{7,6},{8,15},{9,8},{10,9... | collective-permute-start | bytes 442376 | tf_op jit(solution)/shard_map/ppermute | solution.py:314
  29.9 1.2 collective-permute-start.4
  31.1 0.1 select_add_fusion
  31.2 0.6 reshape.123.meta
  31.8 2.1 %collective-permute-done.5.high = f32[36,8,128]{2,1,0:T(8,128)S(1)} collective-permute-done((f32[36,8,128]{2,1,0:T(8,128)S(1)}, f32[36,8,128]{2,1,0:T(8,128)S(1)}, u32[]{:S(2)}, u32[]{:S(2)}) %collective-permute-start.5) | collective-permute-done | bytes 147488 | tf_op jit(solution)/shard_map/ppermute | solution.py:314
  33.9 0.0 collective-permute-done.4.low
  33.9 0.6 copy-done.3
  34.6 0.6 copy-done.4
  35.2 17.6 %first_step.1 = f32[10,8,128]{2,1,0:T(8,128)} custom-call(s32[80]{0:T(128)} %reshape.123.meta, f32[36,8,128]{2,1,0:T(8,128)} %copy-done.4, f32[36,8,128]{2,1,0:T(8,128)} %copy-done.1, f32[36,8,128]{2,1,0:T(8,128)} %copy-done.3), custom_call_target="tpu_custom_call" | custom-call | tf_op jit(solution)/shard_map/first_step/pallas_call | solution.py:385
  52.9 1.3 %collective-permute-start.7 = (f32[10,8,128]{2,1,0:T(8,128)}, f32[10,8,128]{2,1,0:T(8,128)S(1)}, u32[]{:S(2)}, u32[]{:S(2)}) collective-permute-start(f32[10,8,128]{2,1,0:T(8,128)} %first_step.1), channel_id=1, source_target_pairs={{8,0},{16,8},{24,16},{9,1},{17,9},{25,17},{10,2},{18,10},{26,18},{... | collective-permute-start | bytes 122888 | tf_op jit(solution)/shard_map/ppermute | solution.py:314
  54.2 4.0 %collective-permute-start.6 = (f32[10,8,128]{2,1,0:T(8,128)}, f32[10,8,128]{2,1,0:T(8,128)S(1)}, u32[]{:S(2)}, u32[]{:S(2)}) collective-permute-start(f32[10,8,128]{2,1,0:T(8,128)} %first_step.1), channel_id=1, source_target_pairs={{0,8},{8,16},{16,24},{1,9},{9,17},{17,25},{2,10},{10,18},{18,26},{... | collective-permute-start | bytes 122888 | tf_op jit(solution)/shard_map/ppermute | solution.py:314
  58.2 1.4 %collective-permute-done.6 = f32[10,8,128]{2,1,0:T(8,128)S(1)} collective-permute-done((f32[10,8,128]{2,1,0:T(8,128)}, f32[10,8,128]{2,1,0:T(8,128)S(1)}, u32[]{:S(2)}, u32[]{:S(2)}) %collective-permute-start.6) | collective-permute-done | bytes 40992 | tf_op jit(solution)/shard_map/ppermute | solution.py:314
  59.5 0.8 pad_maximum_fusion.middle
  60.3 4.5 %collective-permute-start.9 = (f32[30,8,128]{2,1,0:T(8,128)S(1)}, f32[30,8,128]{2,1,0:T(8,128)S(1)}, u32[]{:S(2)}, u32[]{:S(2)}) collective-permute-start(f32[30,8,128]{2,1,0:T(8,128)S(1)} %pad_maximum_fusion.middle), channel_id=1, source_target_pairs={{0,7},{1,0},{2,1},{3,2},{4,3},{5,4},{6,5},{7,6},{8,15},{9,8},{10,9... | collective-permute-start | bytes 368648 | tf_op jit(solution)/shard_map/ppermute | solution.py:314
  64.9 0.1 select_add_fusion.1
  65.0 0.6 reshape.115.meta
  65.6 0.3 collective-permute-done.9.high
  65.9 0.9 collective-permute-done.8.low
  66.8 0.6 copy-done.7
  67.4 14.9 %second_step.1 = (f32[3,8,128]{2,1,0:T(8,128)}, f32[3,8,128]{2,1,0:T(8,128)}, f32[64,128]{1,0:T(8,128)}, f32[16,8,128]{2,1,0:T(8,128)}) custom-call(s32[64]{0:T(128)} %reshape.115.meta, s32[8,128]{1,0:T(8,128)} %bitcast.34, f32[30,8,128]{2,1,0:T(8,128)} %copy-done.7, f32[30,8,128]{2,1,0:T(8,128)} %copy-done, f32[30,8,128]{2,1,0:T(8,128)} %copy-done.6), custom_call_target="tpu_custom_call" | custom-call | tf_op jit(solution)/shard_map/second_step/pallas_call | solution.py:400
  82.3 8.7 %all-to-all-start = ((f32[16,8,128]{2,1,0:T(8,128)}), f32[16,8,128]{2,1,0:T(8,128)S(1)}, u32[]{:S(2)}, u32[]{:S(2)}) async-start(f32[16,8,128]{2,1,0:T(8,128)} %get-tuple-element.21), calls=%async_computation | async-start | bytes 131072 | tf_op jit(solution)/shard_map/all_to_all | solution.py:419
  91.0 1.3 %collective-permute-start.11 = (f32[64,128]{1,0:T(8,128)S(1)}, f32[64,128]{1,0:T(8,128)S(1)}, u32[]{:S(2)}, u32[]{:S(2)}) collective-permute-start(f32[64,128]{1,0:T(8,128)S(1)} %copy-done.9), channel_id=1, source_target_pairs={{32,0},{64,32},{96,64},{128,96},{160,128},{192,160},{224,192},{256... | collective-permute-start | bytes 98312 | tf_op jit(solution)/shard_map/ppermute | solution.py:314
  92.3 4.0 %collective-permute-start.10 = (f32[64,128]{1,0:T(8,128)S(1)}, f32[64,128]{1,0:T(8,128)S(1)}, u32[]{:S(2)}, u32[]{:S(2)}) collective-permute-start(f32[64,128]{1,0:T(8,128)S(1)} %copy-done.9), channel_id=1, source_target_pairs={{0,32},{32,64},{64,96},{96,128},{128,160},{160,192},{192,224},{224... | collective-permute-start | bytes 98312 | tf_op jit(solution)/shard_map/ppermute | solution.py:314
  96.3 0.6 pad_add_fusion.2.coords
  96.9 0.4 collective-permute-done.10.before
  97.3 5.3 %all-to-all-done.energy = f32[16,8,128]{2,1,0:T(8,128)S(1)} async-done(((f32[16,8,128]{2,1,0:T(8,128)}), f32[16,8,128]{2,1,0:T(8,128)S(1)}, u32[]{:S(2)}, u32[]{:S(2)}) %all-to-all-start) | async-done | bytes 65568 | tf_op jit(solution)/shard_map/all_to_all | solution.py:419
  102.5 0.6 copy-done.2
  103.2 1.9 %planes.1 = f32[32,8,128]{2,1,0:T(8,128)} custom-call(s32[3]{0:T(128)} %pad_add_fusion.2.coords, f32[64,128]{1,0:T(8,128)} %get-tuple-element.20.own, f32[64,128]{1,0:T(8,128)} %copy-done.11, f32[64,128]{1,0:T(8,128)} %copy-done.10, f32[16,8,128]{2,1,0:T(8,128)} %copy-done.2), custom_call_target="tpu_custom_call" | custom-call | tf_op jit(solution)/shard_map/planes/pallas_call | solution.py:424
  105.1 19.5 %all_to_all.10.parts = f32[32,8,128]{2,1,0:T(8,128)} all-to-all(f32[32,8,128]{2,1,0:T(8,128)} %planes.1), channel_id=1, replica_groups=mesh['gx'=16,'gy'=4,'gz'=8] {'gy','gz'}, dimensions={0} | all-to-all | bytes 262144 | tf_op jit(solution)/shard_map/all_to_all | solution.py:431
  124.6 1.7 %lines.1 = (f32[6,8,64]{2,1,0:T(8,128)}, f32[4,8,64]{2,1,0:T(8,128)}, f32[3]{0:T(128)}) custom-call(f32[32,8,128]{2,1,0:T(8,128)} %all_to_all.10.parts), custom_call_target="tpu_custom_call" | custom-call | tf_op jit(solution)/shard_map/lines/pallas_call | solution.py:432
  (40 shorter events, 0.1 us)
Async XLA Ops:
  3.4 15.0 %copy-start.5 = (f32[8,8,128]{2,1,0:T(8,128)S(1)}, f32[8,8,128]{2,1,0:T(8,128)}, u32[]{:S(2)}) copy-start(f32[8,8,128]{2,1,0:T(8,128)} %get-tuple-element.17) | copy-start | bytes 98308
  3.4 14.1 %collective-permute-start = (f32[3,8,128]{2,1,0:T(8,128)}, f32[3,8,128]{2,1,0:T(8,128)S(1)}, u32[]{:S(2)}, u32[]{:S(2)}) collective-permute-start(f32[3,8,128]{2,1,0:T(8,128)} %get-tuple-element.15), channel_id=1, source_target_pairs={{0,32},{32,64},{64,96},{96,128},{128,160},{160,192},{192,224},{224... | collective-permute-start | bytes 36872 | tf_op jit(solution)/shard_map/ppermute | solution.py:314
  7.9 10.5 %collective-permute-start.1 = (f32[3,8,128]{2,1,0:T(8,128)}, f32[3,8,128]{2,1,0:T(8,128)S(1)}, u32[]{:S(2)}, u32[]{:S(2)}) collective-permute-start(f32[3,8,128]{2,1,0:T(8,128)} %get-tuple-element.16), channel_id=1, source_target_pairs={{0,480},{32,0},{64,32},{96,64},{128,96},{160,128},{192,160},{224,1... | collective-permute-start | bytes 36872 | tf_op jit(solution)/shard_map/ppermute | solution.py:314
  17.5 0.6 copy-start.12
  18.4 0.7 slice-start
  19.1 5.4 %copy-start.13 = (f32[3,8,128]{2,1,0:T(8,128)S(1)}, f32[3,8,128]{2,1,0:T(8,128)}, u32[]{:S(2)}) copy-start(f32[3,8,128]{2,1,0:T(8,128)} %copy-done.12) | copy-start | bytes 36868
  19.1 8.6 %collective-permute-start.3 = (f32[12,8,128]{2,1,0:T(8,128)S(1)}, f32[12,8,128]{2,1,0:T(8,128)S(1)}, u32[]{:S(2)}, u32[]{:S(2)}) collective-permute-start(f32[12,8,128]{2,1,0:T(8,128)S(1)} %pad_maximum_fusion.1), channel_id=1, source_target_pairs={{8,0},{16,8},{24,16},{9,1},{17,9},{25,17},{10,2},{18,10},{26,18},{... | collective-permute-start | bytes 147464 | tf_op jit(solution)/shard_map/ppermute | solution.py:314
  20.5 7.2 %collective-permute-start.2 = (f32[12,8,128]{2,1,0:T(8,128)S(1)}, f32[12,8,128]{2,1,0:T(8,128)S(1)}, u32[]{:S(2)}, u32[]{:S(2)}) collective-permute-start(f32[12,8,128]{2,1,0:T(8,128)S(1)} %pad_maximum_fusion.1), channel_id=1, source_target_pairs={{0,8},{8,16},{16,24},{1,9},{9,17},{17,25},{2,10},{10,18},{18,26},{... | collective-permute-start | bytes 147464 | tf_op jit(solution)/shard_map/ppermute | solution.py:314
  27.0 0.7 copy-start.14
  27.8 3.3 %copy-start.8 = (s32[1,1,1,8,6]{4,3,2,1,0:T(8,128)S(1)}, s32[1,1,1,8,6]{4,3,2,1,0:T(8,128)}, u32[]{:S(2)}) copy-start(s32[1,1,1,8,6]{4,3,2,1,0:T(8,128)} %copy.18) | copy-start | bytes 580
  27.8 6.1 %copy-start.1 = (f32[36,8,128]{2,1,0:T(8,128)}, f32[36,8,128]{2,1,0:T(8,128)S(1)}, u32[]{:S(2)}) copy-start(f32[36,8,128]{2,1,0:T(8,128)S(1)} %constant_dynamic-update-slice_fusion.middle) | copy-start | bytes 442372
  27.8 6.1 %collective-permute-start.5 = (f32[36,8,128]{2,1,0:T(8,128)S(1)}, f32[36,8,128]{2,1,0:T(8,128)S(1)}, u32[]{:S(2)}, u32[]{:S(2)}) collective-permute-start(f32[36,8,128]{2,1,0:T(8,128)S(1)} %constant_dynamic-update-slice_fusion.middle), channel_id=1, source_target_pairs={{0,7},{1,0},{2,1},{3,2},{4,3},{5,4},{6,5},{7,6},{8,15},{9,8},{10,9... | collective-permute-start | bytes 442376 | tf_op jit(solution)/shard_map/ppermute | solution.py:314
  29.9 4.0 %collective-permute-start.4 = (f32[36,8,128]{2,1,0:T(8,128)S(1)}, f32[36,8,128]{2,1,0:T(8,128)S(1)}, u32[]{:S(2)}, u32[]{:S(2)}) collective-permute-start(f32[36,8,128]{2,1,0:T(8,128)S(1)} %constant_dynamic-update-slice_fusion.middle), channel_id=1, source_target_pairs={{0,1},{1,2},{2,3},{3,4},{4,5},{5,6},{6,7},{7,0},{8,9},{9,10},{10,1... | collective-permute-start | bytes 442376 | tf_op jit(solution)/shard_map/ppermute | solution.py:314
  33.9 0.7 copy-start.3
  34.6 0.7 copy-start.4
  52.9 5.3 %collective-permute-start.7 = (f32[10,8,128]{2,1,0:T(8,128)}, f32[10,8,128]{2,1,0:T(8,128)S(1)}, u32[]{:S(2)}, u32[]{:S(2)}) collective-permute-start(f32[10,8,128]{2,1,0:T(8,128)} %first_step.1), channel_id=1, source_target_pairs={{8,0},{16,8},{24,16},{9,1},{17,9},{25,17},{10,2},{18,10},{26,18},{... | collective-permute-start | bytes 122888 | tf_op jit(solution)/shard_map/ppermute | solution.py:314
  54.2 5.4 %collective-permute-start.6 = (f32[10,8,128]{2,1,0:T(8,128)}, f32[10,8,128]{2,1,0:T(8,128)S(1)}, u32[]{:S(2)}, u32[]{:S(2)}) collective-permute-start(f32[10,8,128]{2,1,0:T(8,128)} %first_step.1), channel_id=1, source_target_pairs={{0,8},{8,16},{16,24},{1,9},{9,17},{17,25},{2,10},{10,18},{18,26},{... | collective-permute-start | bytes 122888 | tf_op jit(solution)/shard_map/ppermute | solution.py:314
  60.3 6.4 %copy-start = (f32[30,8,128]{2,1,0:T(8,128)}, f32[30,8,128]{2,1,0:T(8,128)S(1)}, u32[]{:S(2)}) copy-start(f32[30,8,128]{2,1,0:T(8,128)S(1)} %pad_maximum_fusion.middle) | copy-start | bytes 368644
  60.3 5.5 %collective-permute-start.9 = (f32[30,8,128]{2,1,0:T(8,128)S(1)}, f32[30,8,128]{2,1,0:T(8,128)S(1)}, u32[]{:S(2)}, u32[]{:S(2)}) collective-permute-start(f32[30,8,128]{2,1,0:T(8,128)S(1)} %pad_maximum_fusion.middle), channel_id=1, source_target_pairs={{0,7},{1,0},{2,1},{3,2},{4,3},{5,4},{6,5},{7,6},{8,15},{9,8},{10,9... | collective-permute-start | bytes 368648 | tf_op jit(solution)/shard_map/ppermute | solution.py:314
  64.9 1.9 %collective-permute-start.8 = (f32[30,8,128]{2,1,0:T(8,128)S(1)}, f32[30,8,128]{2,1,0:T(8,128)S(1)}, u32[]{:S(2)}, u32[]{:S(2)}) collective-permute-start(f32[30,8,128]{2,1,0:T(8,128)S(1)} %pad_maximum_fusion.middle), channel_id=1, source_target_pairs={{0,1},{1,2},{2,3},{3,4},{4,5},{5,6},{6,7},{7,0},{8,9},{9,10},{10,1... | collective-permute-start | bytes 368648 | tf_op jit(solution)/shard_map/ppermute | solution.py:314
  65.9 0.9 copy-start.6
  66.8 0.6 copy-start.7
  82.3 8.7 %copy-start.9 = (f32[64,128]{1,0:T(8,128)S(1)}, f32[64,128]{1,0:T(8,128)}, u32[]{:S(2)}) copy-start(f32[64,128]{1,0:T(8,128)} %get-tuple-element.20.own) | copy-start | bytes 98308
  82.3 20.2 %all-to-all-start = ((f32[16,8,128]{2,1,0:T(8,128)}), f32[16,8,128]{2,1,0:T(8,128)S(1)}, u32[]{:S(2)}, u32[]{:S(2)}) async-start(f32[16,8,128]{2,1,0:T(8,128)} %get-tuple-element.21), calls=%async_computation | async-start | bytes 131072 | tf_op jit(solution)/shard_map/all_to_all | solution.py:419
  91.0 5.9 %collective-permute-start.11 = (f32[64,128]{1,0:T(8,128)S(1)}, f32[64,128]{1,0:T(8,128)S(1)}, u32[]{:S(2)}, u32[]{:S(2)}) collective-permute-start(f32[64,128]{1,0:T(8,128)S(1)} %copy-done.9), channel_id=1, source_target_pairs={{32,0},{64,32},{96,64},{128,96},{160,128},{192,160},{224,192},{256... | collective-permute-start | bytes 98312 | tf_op jit(solution)/shard_map/ppermute | solution.py:314
  92.3 5.0 %collective-permute-start.10 = (f32[64,128]{1,0:T(8,128)S(1)}, f32[64,128]{1,0:T(8,128)S(1)}, u32[]{:S(2)}, u32[]{:S(2)}) collective-permute-start(f32[64,128]{1,0:T(8,128)S(1)} %copy-done.9), channel_id=1, source_target_pairs={{0,32},{32,64},{64,96},{96,128},{128,160},{160,192},{192,224},{224... | collective-permute-start | bytes 98312 | tf_op jit(solution)/shard_map/ppermute | solution.py:314
  96.9 5.7 %copy-start.10 = (f32[64,128]{1,0:T(8,128)}, f32[64,128]{1,0:T(8,128)S(1)}, u32[]{:S(2)}) copy-start(f32[64,128]{1,0:T(8,128)S(1)} %collective-permute-done.11.after) | copy-start | bytes 98308
  97.3 5.3 %copy-start.11 = (f32[64,128]{1,0:T(8,128)}, f32[64,128]{1,0:T(8,128)S(1)}, u32[]{:S(2)}) copy-start(f32[64,128]{1,0:T(8,128)S(1)} %collective-permute-done.10.before) | copy-start | bytes 98308
  102.5 0.6 copy-start.2

commit v2 on v1

--- a/solution.py
+++ b/solution.py
@@ -36,114 +36,111 @@
 GAUSS = [w / TOTAL for w in RAW]
 
 
-def row(tile, index):
-    return jnp.broadcast_to(tile[index : index + 1, :], (8, 128))
-
-
-def pair_sums(tiles, meta, base, own, second):
-    xi, yi, zi = row(own, 0), row(own, 1), row(own, 2)
-    ui, vi, wi = row(own, 3), row(own, 4), row(own, 5)
-    ri = row(own, 6)
-    sub = lax.broadcasted_iota(jnp.int32, (8, 128), 0)
-    lane = lax.broadcasted_iota(jnp.int32, (8, 128), 1)
-    zero = jnp.zeros((8, 128), jnp.float32)
-    count = 10 if second else 3
-    sums = [zero] * count
+def twice(value):
+    return jnp.concatenate([value, value], axis=0)
+
+
+def parts_of(value, count):
+    parts = []
+    for _ in range(count):
+        part = value.astype(jnp.bfloat16)
+        parts.append(part)
+        value = value - part.astype(jnp.float32)
+    return parts
+
+
+def selector():
+    shape = (32, 8 * 128)
+    line = lax.broadcasted_iota(jnp.int32, shape, 0)
+    block = lax.shift_right_logical(lax.broadcasted_iota(jnp.int32, shape, 1), 7)
+    hit = jnp.logical_and(lax.bitwise_and(line, 7) == block, line < 24)
+    return jnp.where(hit, 1.0, 0.0).astype(jnp.bfloat16)
+
+
+def own_columns(own, select, mine):
+    stack = jnp.concatenate(
+        [part.astype(jnp.float32) for part in parts_of(own, 3)] + [jnp.zeros((8, 128), jnp.float32)], axis=0
+    ).astype(jnp.bfloat16)
+    wide = lax.dot_general(
+        stack, select[...], (((0,), (0,)), ((), ())), preferred_element_type=jnp.float32
+    )
+    for c in range(8):
+        mine[c] = wide[:, 128 * c : 128 * c + 128]
+
+
+def pair_sums(tiles, meta, base, own, second, select, rows, mine):
+    lane = lax.broadcasted_iota(jnp.int32, (8, 128), 1).astype(jnp.float32)
     for slot in range(K):
         entry = meta[base + slot]
-        partner = tiles[lax.bitwise_and(entry, 1023)]
+        index = lax.bitwise_and(entry, 1023)
         live = lax.bitwise_and(entry, LIVE) > 0
-        dead = jnp.logical_and(sub == 6, jnp.logical_or(partner <= 0.0, jnp.logical_not(live)))
-        partner = jnp.where(dead, FAR, partner)
-        columns = partner.T
-        if second:
-            selfrow = jnp.where(lax.bitwise_and(entry, ITSELF) > 0, lane, -1)
-        for chunk in range(16):
-            part = columns[8 * chunk : 8 * chunk + 8, :]
-            col = [jnp.broadcast_to(part[:, c : c + 1], (8, 128)) for c in range(7)]
-            dx, dy, dz = col[0] - xi, col[1] - yi, col[2] - zi
+        for c in range(8 if slot < 3 else 7):
+            value = jnp.broadcast_to(tiles[index, c : c + 1, :], (8, 128))
+            if c == 6:
+                value = jnp.where(jnp.logical_and(live, value > 0.0), value, FAR)
+            if c == 7:
+                value = jnp.where(lax.bitwise_and(entry, INSIDE) > 0, value, -7.0)
+            rows[9 * slot + c] = value
+        if second and slot < 3:
+            rows[9 * slot + 8] = jnp.where(lax.bitwise_and(entry, ITSELF) > 0, lane, -1.0)
+    own_columns(own, select, mine)
+    number = lax.broadcasted_iota(jnp.int32, (16, 128), 0).astype(jnp.float32)
+    whole_lane = twice(lane)
+    ones = jnp.ones((256, 128), jnp.bfloat16)
+    count = 11 if second else 3
+    totals = [jnp.zeros((16, 128), jnp.float32)] * count
+    for block in range(8):
+        xi, yi, zi, ui, vi, wi, ri, ci = [mine[c, 16 * block : 16 * block + 16, :] for c in range(8)]
+        ci = jnp.where(ci < 0.0, -5.0, ci)
+        here = number + float(16 * block)
+        added = [jnp.zeros((16, 128), jnp.float32)] * count
+        for slot in range(K):
+            xj, yj, zj, uj, vj, wj, rj = [twice(rows[9 * slot + c]) for c in range(7)]
+            dx, dy, dz = xj - xi, yj - yi, zj - zi
             square = dx * dx + dy * dy + (dz * dz + SOFT)
             inverse = lax.rsqrt(square)
-            inter = jnp.maximum((col[6] + ri) - square * inverse, 0.0)
+            distance = square * inverse
+            reach = rj + ri
+            inter = jnp.maximum(reach - distance, 0.0)
             root = inter * lax.rsqrt(jnp.maximum(inter, 1e-30))
-            closing = ((col[3] - ui) * dx + (col[4] - vi) * dy + (col[5] - wi) * dz) * inverse
-            scaled = root * (GAMMA * closing - KN * inter) * inverse
+            closing = ((uj - ui) * dx + (vj - vi) * dy + (wj - wi) * dz) * inverse
+            magnitude = root * (closing - inter)
+            if slot < 3:
+                ratio = lax.rsqrt(reach)
+                window = jnp.maximum(1.0 - distance * ((1.0 / REACH) * ratio * ratio), 0.0)
+                window = jnp.where(twice(rows[9 * slot + 7]) == ci, window * window, 0.0)
+                stretch = distance - reach
+                pull = stretch * window
+                magnitude = magnitude + KB * pull
+            scaled = magnitude * inverse
             fx, fy, fz = scaled * dx, scaled * dy, scaled * dz
-            sums[0] = sums[0] + fx
-            sums[1] = sums[1] + fy
-            sums[2] = sums[2] + fz
+            terms = [fx, fy, fz]
             if second:
-                sums[3] = sums[3] + fx * dx
-                sums[4] = sums[4] + fy * dy
-                sums[5] = sums[5] + fz * dz
-                sums[6] = sums[6] + fx * dy
-                sums[7] = sums[7] + fx * dz
-                sums[8] = sums[8] + fy * dz
+                terms += [fx * dx, fy * dy, fz * dz, fx * dy, fx * dz, fy * dz]
                 energy = inter * inter * root
-                sums[9] = sums[9] + jnp.where(sub + 8 * chunk == selfrow, 0.0, energy)
-    return sums
-
-
-def bond_sums(tiles, entry, own, second, sums):
-    xi, yi, zi, ri = row(own, 0), row(own, 1), row(own, 2), row(own, 6)
-    code = row(own, 7)
-    code = jnp.where(code < 0.0, -5.0, code)
-    sub = lax.broadcasted_iota(jnp.int32, (8, 128), 0)
-    lane = lax.broadcasted_iota(jnp.int32, (8, 128), 1)
-    partner = tiles[lax.bitwise_and(entry, 1023)]
-    columns = partner.T
-    selfrow = jnp.where(lax.bitwise_and(entry, ITSELF) > 0, lane, -1)
-    held = [sums[i] for i in range(11 if second else 3)]
-    for chunk in range(16):
-        part = columns[8 * chunk : 8 * chunk + 8, :]
-        xj, yj, zj, rj, cj = [
-            jnp.broadcast_to(part[:, c : c + 1], (8, 128)) for c in (0, 1, 2, 6, 7)
+                if slot < 3:
+                    itself = twice(rows[9 * slot + 8]) == here
+                    terms += [jnp.where(itself, 0.0, energy), jnp.where(itself, 0.0, pull * stretch)]
+                else:
+                    terms += [energy]
+            added = [a + b for a, b in zip(added, terms)] + added[len(terms) :]
+        stack = jnp.concatenate([jnp.concatenate(parts_of(value, 2), axis=1) for value in added], axis=0)
+        sums = jnp.dot(stack, ones, preferred_element_type=jnp.float32)
+        diagonal = whole_lane == here
+        totals = [
+            jnp.where(diagonal, sums[16 * i : 16 * i + 16, :], total) for i, total in enumerate(totals)
         ]
-        dx, dy, dz = xj - xi, yj - yi, zj - zi
-        square = dx * dx + dy * dy + (dz * dz + SOFT)
-        inverse = lax.rsqrt(square)
-        distance = square * inverse
-        reach = rj + ri
-        bonded = jnp.logical_and(cj == code, sub + 8 * chunk != selfrow)
-        bonded = jnp.logical_and(bonded, rj > 0.0)
-        window = jnp.maximum(1.0 - distance / (REACH * reach), 0.0)
-        window = jnp.where(bonded, window * window, 0.0)
-        stretch = distance - reach
-        pull = stretch * window
-        scaled = KB * pull * inverse
-        fx, fy, fz = scaled * dx, scaled * dy, scaled * dz
-        held[0] = held[0] + fx
-        held[1] = held[1] + fy
-        held[2] = held[2] + fz
-        if second:
-            held[3] = held[3] + fx * dx
-            held[4] = held[4] + fy * dy
-            held[5] = held[5] + fz * dz
-            held[6] = held[6] + fx * dy
-            held[7] = held[7] + fx * dz
-            held[8] = held[8] + fy * dz
-            held[10] = held[10] + pull * stretch
-    for i, value in enumerate(held):
-        sums[i] = value
-
-
-def tile_sums(tiles, meta, base, own, second, sums):
-    for i, value in enumerate(pair_sums(tiles, meta, base, own, second)):
-        sums[i] = value
-    if second:
-        sums[10] = jnp.zeros((8, 128), jnp.float32)
-
-    @pl.loop(0, K)
-    def _(slot):
-        entry = meta[base + slot]
-
-        @pl.when(lax.bitwise_and(entry, INSIDE) > 0)
-        def _():
-            bond_sums(tiles, entry, own, second, sums)
-
-
-def folded(value):
-    return jnp.sum(value, axis=0, keepdims=True)
+    return [jnp.sum(total, axis=0, keepdims=True) for total in totals]
+
+
+def work_space():
+    return (
+        pltpu.VMEM((32, 8 * 128), jnp.bfloat16),
+        pltpu.VMEM((9 * K, 8, 128), jnp.float32),
+        pltpu.VMEM((8, 128, 128), jnp.float32),
+        pltpu.VMEM((9 * K, 8, 128), jnp.float32),
+        pltpu.VMEM((8, 128, 128), jnp.float32),
+    )
 
 
 def fill(tiles, low, middle, high, size):
@@ -152,58 +149,65 @@
             tiles[part * size + i] = ref[i]
 
 
-def first_kernel(meta, low, middle, high, out, tiles, sums):
+def first_kernel(meta, low, middle, high, out, tiles, *work):
     width = middle.shape[0] // 3
     fill(tiles, low, middle, high, 3 * width)
+    work[0][...] = selector()
     sub = lax.broadcasted_iota(jnp.int32, (8, 128), 0)
 
-    @pl.loop(0, width - 2)
-    def _(t):
+    def one(t, *work):
         own = tiles[4 * width + t + 1]
-        tile_sums(tiles, meta, t * 8, own, False, sums)
+        sums = pair_sums(tiles, meta, t * 8, own, False, *work)
         radius = own[6:7, :]
         gain = STEP_DT / (DENS * radius * radius * radius)
         fresh = own
         for axis in range(3):
-            speed = own[3 + axis : 4 + axis, :] + gain * folded(sums[axis])
+            speed = own[3 + axis : 4 + axis, :] + gain * sums[axis]
             place = own[axis : axis + 1, :] + STEP_DT * speed
             fresh = jnp.where(sub == axis, place, fresh)
             fresh = jnp.where(sub == 3 + axis, speed, fresh)
         out[t] = fresh
 
+    @pl.loop(0, (width - 2) // 2)
+    def _(t):
+        one(2 * t, work[0], work[1], work[2])
+        one(2 * t + 1, work[0], work[3], work[4])
+
 
 def second_kernel(
-    meta, cell, low, middle, high, place_out, speed_out, grid_out, energy_out, tiles, sums, left, right, total
+    meta, cell, low, middle, high, place_out, speed_out, grid_out, energy_out, tiles, left, right, total, *work
 ):
     width = middle.shape[0] // 3
     fill(tiles, low, middle, high, 3 * width)
+    work[0][...] = selector()
     sub = lax.broadcasted_iota(jnp.int32, (8, 128), 0)
     line = lax.broadcasted_iota(jnp.int32, (64, 128), 0)
     total[...] = jnp.zeros((8, 128), jnp.float32)
     right[...] = jnp.zeros(right.shape, jnp.bfloat16)
 
-    for t in range(NT):
+    def one(t, *work):
         own = tiles[4 * width + t + 1]
-        tile_sums(tiles, meta, t * 8, own, True, sums)
+        sums = pair_sums(tiles, meta, t * 8, own, True, *work)
         radius = own[6:7, :]
         mass = DENS * radius * radius * radius
         gain = STEP_DT / mass
-        values = [-0.5 * folded(sums[3 + i]) for i in range(6)]
+        values = [-0.5 * sums[3 + i] for i in range(6)]
         squares = jnp.zeros((1, 128), jnp.float32)
+        this = pl.ds(t, 1)
         for axis in range(3):
-            speed = own[3 + axis : 4 + axis, :] + gain * folded(sums[axis])
-            speed_out[axis, t : t + 1, :] = speed
-            place_out[axis, t : t + 1, :] = own[axis : axis + 1, :] + STEP_DT * speed
+            speed = own[3 + axis : 4 + axis, :] + gain * sums[axis]
+            speed_out[axis, this, :] = speed
+            place_out[axis, this, :] = own[axis : axis + 1, :] + STEP_DT * speed
             squares = squares + speed * speed
             values.append(mass * speed)
         kinetic = 0.5 * mass * squares
         values.append(kinetic)
-        contact = 0.4 * KN * folded(sums[9])
-        bond = 0.5 * KB * folded(sums[10])
+        contact = 0.4 * KN * sums[9]
+        bond = 0.5 * KB * sums[10]
         added = jnp.where(sub == 0, kinetic, jnp.where(sub == 1, contact, jnp.where(sub == 2, bond, 0.0)))
         total[...] = total[...] + added
-        where = cell[t : t + 1, :]
-        span = slice(128 * t, 128 * t + 128)
+        where = cell[this, :]
+        span = pl.ds(pl.multiple_of(128 * t, 128), 128)
         in_plane = sub == lax.shift_right_logical(where, 6)
         for c in range(0, COMPS, 2):
             pair = jnp.concatenate(
@@ -214,6 +218,11 @@
             right[8 * c : 8 * c + 16, span] = coarse
             right[128 + 8 * c : 128 + 8 * c + 16, span] = fine
         left[:, span] = jnp.where(line == lax.bitwise_and(where, 63), 1.0, 0.0).astype(jnp.bfloat16)
+
+    @pl.loop(0, NT // 2)
+    def _(t):
+        one(2 * t, work[0], work[1], work[2])
+        one(2 * t + 1, work[0], work[3], work[4])
 
     both = lax.dot_general(
         left[...], right[...], (((1,), (1,)), ((), ())), preferred_element_type=jnp.float32
@@ -333,7 +342,13 @@
     entry = up * (3 * width) + across * width + spot
     entry = entry + LIVE * live.astype(jnp.int32) + INSIDE * inside.astype(jnp.int32)
     entry = entry + ITSELF * itself.astype(jnp.int32)
-    return jnp.pad(entry, ((0, 0), (0, 8 - K))).reshape(-1)
+    own = inside.astype(jnp.int32)
+    earlier = lax.broadcasted_iota(jnp.int32, (K, K), 0) < lax.broadcasted_iota(jnp.int32, (K, K), 1)
+    before = jnp.sum(jnp.where(earlier, own[:, :, None], 0), axis=1)
+    slot = lax.broadcasted_iota(jnp.int32, lists.shape, 1)
+    rank = jnp.where(inside, before, slot - before + jnp.sum(own, axis=1, keepdims=True))
+    to = lax.broadcasted_iota(jnp.int32, (1, 1, 8), 2)
+    return jnp.sum(jnp.where(rank[:, :, None] == to, entry[:, :, None], 0), axis=1).reshape(-1)
 
 
 def shards(positions, velocities, radius, group, broken, cell, neighbours, counts):
@@ -389,7 +404,7 @@
         out_specs=VMEM,
         scratch_shapes=[
             pltpu.VMEM((9 * width, 8, 128), jnp.float32),
-            pltpu.VMEM((11, 8, 128), jnp.float32),
+            *work_space(),
         ],
         name="first_step",
     )(first_meta, low, middle, high)
@@ -409,10 +424,10 @@
         out_specs=(VMEM,) * 4,
         scratch_shapes=[
             pltpu.VMEM((9 * width, 8, 128), jnp.float32),
-            pltpu.VMEM((11, 8, 128), jnp.float32),
             pltpu.VMEM((64, NT * 128), jnp.bfloat16),
             pltpu.VMEM((256, NT * 128), jnp.bfloat16),
             pltpu.VMEM((8, 128), jnp.float32),
+            *work_space(),
         ],
         name="second_step",
     )(second_meta, cell.reshape(NT, 128), low, middle, high)

time: 127 us -> 114 us (0.90)
  Pallas kernels: 37.5 us -> 26.4 us
  starting transfers between devices: 46.5 us -> 44.9 us
    pallas_call x1, Pallas kernels: 17.6 us -> 10.3 us  [shards(): pl.pallas_call(first_kernel, out_shape=jax.ShapeDtypeStruct((width - 2, 8...]
    pallas_call x1, Pallas kernels: 14.9 us -> 11.1 us  [shards(): pl.pallas_call(second_kernel, out_shape=(block, block, jax.ShapeDtypeStru...]
    ppermute x12, starting transfers between devices: 37.8 us -> 36.4 us  [shifted(): return lax.ppermute(value, axis, pairs)]
    unnamed x35 -> x37, local copies, waits for them, and re-layouts: 5.21 us -> 5.73 us
  transfers between devices with their start and end apart: 13 -> 13, of which waited for: 7 -> 6; matrix products, arithmetic and copies ran while one was open for 3% -> 4% of each run, Pallas kernels for 0% -> 0%
where the time goes in v2:
time: 114 us; the launch traced here: 113 us
  starting transfers between devices  44.9 us (39%)
  Pallas kernels  26.4 us (23%)
  blocking collectives  18.3 us (16%)
  waiting for transfers between devices  10 us (9%)
  local copies, waits for them, and re-layouts  9.23 us (8%)
  other arithmetic  2.23 us (2%)
  between operations  2.23 us (2%)
    ppermute x12, starting transfers between devices, shifted(): return lax.ppermute(value, axis, pairs)  36.4 us
    all_to_all x1, blocking collectives, shards(): parts = lax.all_to_all(parts, ('gy', 'gz'), 0, 0, tiled=True)  18.3 us
    pallas_call x1, Pallas kernels, shards(): pl.pallas_call(second_kernel, out_shape=(block, block, jax.ShapeDtypeStru...  11.1 us
    pallas_call x1, Pallas kernels, shards(): pl.pallas_call(first_kernel, out_shape=jax.ShapeDtypeStruct((width - 2, 8...  10.3 us
    all_to_all x1, starting transfers between devices, shards(): energy = lax.all_to_all(energy, 'gx', 0, 0, tiled=True)  8.51 us
    unnamed x37, local copies, waits for them, and re-layouts  5.73 us
    all_to_all x1, waiting for transfers between devices, shards(): energy = lax.all_to_all(energy, 'gx', 0, 0, tiled=True)  5.25 us
    ppermute x12, waiting for transfers between devices, shifted(): return lax.ppermute(value, axis, pairs)  4.77 us
  transfers between devices with their start and end apart: 13, of which 6 were waited for; matrix products, arithmetic and copies ran while one was open for 4% of the time, Pallas kernels for 0%

profile of v2, /device:TPU:1, one launch (start us, length us, event | category | flops | bytes accessed | tf_op | source)
XLA Modules:
  0.0 113.4 jit_solution(15980037661767709601)
XLA Ops:
  0.6 1.4 %copy.23 = s32[1,1,1,8,6]{4,3,2,1,0:T(8,128)} copy(s32[1,1,1,8,6]{3,2,4,1,0:T(1,128)} %param.14) | data formatting | bytes 384 | tf_op args[6]
  2.0 1.4 %pack.1 = (f32[8,8,128]{2,1,0:T(8,128)}, f32[3,8,128]{2,1,0:T(8,128)}, f32[3,8,128]{2,1,0:T(8,128)}) custom-call(f32[3,8,128]{2,1,0:T(8,128)} %bitcast.42, f32[3,8,128]{2,1,0:T(8,128)} %bitcast.43, f32[8,128]{1,0:T(8,128)} %bitcast.48, s32[8,128]{1,0:T(8,128)} %bitcast.49, s32[8,128]{1,0:T(8,128)} %bitcast.50, s32[8,6]{1,0:T(8,128)} %bitcast.39, s32[1,8]{1,0:T(1,128)} %bitcast.44), custom_call_target="tpu_custom_call" | custom-call | tf_op jit(solution)/shard_map/pack/pallas_call | solution.py:359
  3.4 4.4 %collective-permute-start = (f32[3,8,128]{2,1,0:T(8,128)}, f32[3,8,128]{2,1,0:T(8,128)S(1)}, u32[]{:S(2)}, u32[]{:S(2)}) collective-permute-start(f32[3,8,128]{2,1,0:T(8,128)} %get-tuple-element.15), channel_id=1, source_target_pairs={{0,32},{32,64},{64,96},{96,128},{128,160},{160,192},{192,224},{224... | collective-permute-start | bytes 36872 | tf_op jit(solution)/shard_map/ppermute | solution.py:323
  7.8 9.5 %collective-permute-start.1 = (f32[3,8,128]{2,1,0:T(8,128)}, f32[3,8,128]{2,1,0:T(8,128)S(1)}, u32[]{:S(2)}, u32[]{:S(2)}) collective-permute-start(f32[3,8,128]{2,1,0:T(8,128)} %get-tuple-element.16), channel_id=1, source_target_pairs={{0,480},{32,0},{64,32},{96,64},{128,96},{160,128},{192,160},{224,1... | collective-permute-start | bytes 36872 | tf_op jit(solution)/shard_map/ppermute | solution.py:323
  17.3 0.7 copy-done.8
  18.0 0.2 convert_reduce_fusion.1
  18.2 0.1 copy.24
  18.3 0.1 select_reduce_fusion.3
  18.4 0.5 copy-done.14
  18.9 0.6 copy-done.12
  19.5 0.7 slice-done
  20.2 1.4 %collective-permute-start.3 = (f32[12,8,128]{2,1,0:T(8,128)S(1)}, f32[12,8,128]{2,1,0:T(8,128)S(1)}, u32[]{:S(2)}, u32[]{:S(2)}) collective-permute-start(f32[12,8,128]{2,1,0:T(8,128)S(1)} %pad_maximum_fusion.1), channel_id=1, source_target_pairs={{8,0},{16,8},{24,16},{9,1},{17,9},{25,17},{10,2},{18,10},{26,18},{... | collective-permute-start | bytes 147464 | tf_op jit(solution)/shard_map/ppermute | solution.py:323
  21.6 4.0 %collective-permute-start.2 = (f32[12,8,128]{2,1,0:T(8,128)S(1)}, f32[12,8,128]{2,1,0:T(8,128)S(1)}, u32[]{:S(2)}, u32[]{:S(2)}) collective-permute-start(f32[12,8,128]{2,1,0:T(8,128)S(1)} %pad_maximum_fusion.1), channel_id=1, source_target_pairs={{0,8},{8,16},{16,24},{1,9},{9,17},{17,25},{2,10},{10,18},{18,26},{... | collective-permute-start | bytes 147464 | tf_op jit(solution)/shard_map/ppermute | solution.py:323
  25.6 0.6 slice.24
  26.9 0.1 copy.27
  26.9 0.5 slice.25
  28.1 0.1 copy.29
  28.3 0.1 convert_reduce_fusion
  28.6 1.5 %collective-permute-start.5 = (f32[36,8,128]{2,1,0:T(8,128)S(1)}, f32[36,8,128]{2,1,0:T(8,128)S(1)}, u32[]{:S(2)}, u32[]{:S(2)}) collective-permute-start(f32[36,8,128]{2,1,0:T(8,128)S(1)} %constant_dynamic-update-slice_fusion.middle), channel_id=1, source_target_pairs={{0,7},{1,0},{2,1},{3,2},{4,3},{5,4},{6,5},{7,6},{8,15},{9,8},{10,9... | collective-permute-start | bytes 442376 | tf_op jit(solution)/shard_map/ppermute | solution.py:323
  30.1 1.2 %collective-permute-start.4 = (f32[36,8,128]{2,1,0:T(8,128)S(1)}, f32[36,8,128]{2,1,0:T(8,128)S(1)}, u32[]{:S(2)}, u32[]{:S(2)}) collective-permute-start(f32[36,8,128]{2,1,0:T(8,128)S(1)} %constant_dynamic-update-slice_fusion.middle), channel_id=1, source_target_pairs={{0,1},{1,2},{2,3},{3,4},{4,5},{5,6},{6,7},{7,0},{8,9},{9,10},{10,1... | collective-permute-start | bytes 442376 | tf_op jit(solution)/shard_map/ppermute | solution.py:323
  31.3 0.1 add_select_fusion.12
  31.4 0.1 copy.30
  31.5 0.6 reshape.807.meta
  32.1 2.0 %collective-permute-done.5.high = f32[36,8,128]{2,1,0:T(8,128)S(1)} collective-permute-done((f32[36,8,128]{2,1,0:T(8,128)S(1)}, f32[36,8,128]{2,1,0:T(8,128)S(1)}, u32[]{:S(2)}, u32[]{:S(2)}) %collective-permute-start.5) | collective-permute-done | bytes 147488 | tf_op jit(solution)/shard_map/ppermute | solution.py:323
  34.1 0.6 copy-done.3
  34.8 0.7 copy-done.4
  35.5 10.3 %first_step.1 = f32[10,8,128]{2,1,0:T(8,128)} custom-call(s32[80]{0:T(128)} %reshape.807.meta, f32[36,8,128]{2,1,0:T(8,128)} %copy-done.4, f32[36,8,128]{2,1,0:T(8,128)} %copy-done.1, f32[36,8,128]{2,1,0:T(8,128)} %copy-done.3), custom_call_target="tpu_custom_call" | custom-call | tf_op jit(solution)/shard_map/first_step/pallas_call | solution.py:400
  45.8 1.3 %collective-permute-start.7 = (f32[10,8,128]{2,1,0:T(8,128)}, f32[10,8,128]{2,1,0:T(8,128)S(1)}, u32[]{:S(2)}, u32[]{:S(2)}) collective-permute-start(f32[10,8,128]{2,1,0:T(8,128)} %first_step.1), channel_id=1, source_target_pairs={{8,0},{16,8},{24,16},{9,1},{17,9},{25,17},{10,2},{18,10},{26,18},{... | collective-permute-start | bytes 122888 | tf_op jit(solution)/shard_map/ppermute | solution.py:323
  47.1 4.0 %collective-permute-start.6 = (f32[10,8,128]{2,1,0:T(8,128)}, f32[10,8,128]{2,1,0:T(8,128)S(1)}, u32[]{:S(2)}, u32[]{:S(2)}) collective-permute-start(f32[10,8,128]{2,1,0:T(8,128)} %first_step.1), channel_id=1, source_target_pairs={{0,8},{8,16},{16,24},{1,9},{9,17},{17,25},{2,10},{10,18},{18,26},{... | collective-permute-start | bytes 122888 | tf_op jit(solution)/shard_map/ppermute | solution.py:323
  51.1 1.4 %collective-permute-done.6 = f32[10,8,128]{2,1,0:T(8,128)S(1)} collective-permute-done((f32[10,8,128]{2,1,0:T(8,128)}, f32[10,8,128]{2,1,0:T(8,128)S(1)}, u32[]{:S(2)}, u32[]{:S(2)}) %collective-permute-start.6) | collective-permute-done | bytes 40992 | tf_op jit(solution)/shard_map/ppermute | solution.py:323
  52.5 0.8 pad_maximum_fusion.middle
  53.3 3.9 %collective-permute-start.9 = (f32[30,8,128]{2,1,0:T(8,128)S(1)}, f32[30,8,128]{2,1,0:T(8,128)S(1)}, u32[]{:S(2)}, u32[]{:S(2)}) collective-permute-start(f32[30,8,128]{2,1,0:T(8,128)S(1)} %pad_maximum_fusion.middle), channel_id=1, source_target_pairs={{0,7},{1,0},{2,1},{3,2},{4,3},{5,4},{6,5},{7,6},{8,15},{9,8},{10,9... | collective-permute-start | bytes 368648 | tf_op jit(solution)/shard_map/ppermute | solution.py:323
  57.2 0.1 copy.25
  57.4 0.1 select_reduce_fusion.2
  57.5 0.6 reshape.799.meta
  58.1 0.9 collective-permute-done.8.low
  59.0 0.6 copy-done.7
  59.7 11.1 %second_step.1 = (f32[3,8,128]{2,1,0:T(8,128)}, f32[3,8,128]{2,1,0:T(8,128)}, f32[64,128]{1,0:T(8,128)}, f32[16,8,128]{2,1,0:T(8,128)}) custom-call(s32[64]{0:T(128)} %reshape.799.meta, s32[8,128]{1,0:T(8,128)} %bitcast.47, f32[30,8,128]{2,1,0:T(8,128)} %copy-done.7, f32[30,8,128]{2,1,0:T(8,128)} %copy-done, f32[30,8,128]{2,1,0:T(8,128)} %copy-done.6), custom_call_target="tpu_custom_call" | custom-call | tf_op jit(solution)/shard_map/second_step/pallas_call | solution.py:415
  70.7 8.5 %all-to-all-start = ((f32[16,8,128]{2,1,0:T(8,128)}), f32[16,8,128]{2,1,0:T(8,128)S(1)}, u32[]{:S(2)}, u32[]{:S(2)}) async-start(f32[16,8,128]{2,1,0:T(8,128)} %get-tuple-element.21), calls=%async_computation | async-start | bytes 131072 | tf_op jit(solution)/shard_map/all_to_all | solution.py:434
  79.3 1.3 %collective-permute-start.11 = (f32[64,128]{1,0:T(8,128)S(1)}, f32[64,128]{1,0:T(8,128)S(1)}, u32[]{:S(2)}, u32[]{:S(2)}) collective-permute-start(f32[64,128]{1,0:T(8,128)S(1)} %copy-done.9), channel_id=1, source_target_pairs={{32,0},{64,32},{96,64},{128,96},{160,128},{192,160},{224,192},{256... | collective-permute-start | bytes 98312 | tf_op jit(solution)/shard_map/ppermute | solution.py:323
  80.6 4.0 %collective-permute-start.10 = (f32[64,128]{1,0:T(8,128)S(1)}, f32[64,128]{1,0:T(8,128)S(1)}, u32[]{:S(2)}, u32[]{:S(2)}) collective-permute-start(f32[64,128]{1,0:T(8,128)S(1)} %copy-done.9), channel_id=1, source_target_pairs={{0,32},{32,64},{64,96},{96,128},{128,160},{160,192},{192,224},{224... | collective-permute-start | bytes 98312 | tf_op jit(solution)/shard_map/ppermute | solution.py:323
  84.6 0.6 pad_add_fusion.2.coords
  85.2 0.4 collective-permute-done.10.before
  85.6 5.3 %all-to-all-done.energy = f32[16,8,128]{2,1,0:T(8,128)S(1)} async-done(((f32[16,8,128]{2,1,0:T(8,128)}), f32[16,8,128]{2,1,0:T(8,128)S(1)}, u32[]{:S(2)}, u32[]{:S(2)}) %all-to-all-start) | async-done | bytes 65568 | tf_op jit(solution)/shard_map/all_to_all | solution.py:434
  90.8 0.6 copy-done.2
  91.5 1.9 %planes.1 = f32[32,8,128]{2,1,0:T(8,128)} custom-call(s32[3]{0:T(128)} %pad_add_fusion.2.coords, f32[64,128]{1,0:T(8,128)} %get-tuple-element.20.own, f32[64,128]{1,0:T(8,128)} %copy-done.11, f32[64,128]{1,0:T(8,128)} %copy-done.10, f32[16,8,128]{2,1,0:T(8,128)} %copy-done.2), custom_call_target="tpu_custom_call" | custom-call | tf_op jit(solution)/shard_map/planes/pallas_call | solution.py:439
  93.4 18.3 %all_to_all.10.parts = f32[32,8,128]{2,1,0:T(8,128)} all-to-all(f32[32,8,128]{2,1,0:T(8,128)} %planes.1), channel_id=1, replica_groups=mesh['gx'=16,'gy'=4,'gz'=8] {'gy','gz'}, dimensions={0} | all-to-all | bytes 262144 | tf_op jit(solution)/shard_map/all_to_all | solution.py:446
  111.7 1.7 %lines.1 = (f32[6,8,64]{2,1,0:T(8,128)}, f32[4,8,64]{2,1,0:T(8,128)}, f32[3]{0:T(128)}) custom-call(f32[32,8,128]{2,1,0:T(8,128)} %all_to_all.10.parts), custom_call_target="tpu_custom_call" | custom-call | tf_op jit(solution)/shard_map/lines/pallas_call | solution.py:447
  (56 shorter events, 0.5 us)
Async XLA Ops:
  3.4 15.5 %collective-permute-start = (f32[3,8,128]{2,1,0:T(8,128)}, f32[3,8,128]{2,1,0:T(8,128)S(1)}, u32[]{:S(2)}, u32[]{:S(2)}) collective-permute-start(f32[3,8,128]{2,1,0:T(8,128)} %get-tuple-element.15), channel_id=1, source_target_pairs={{0,32},{32,64},{64,96},{96,128},{128,160},{160,192},{192,224},{224... | collective-permute-start | bytes 36872 | tf_op jit(solution)/shard_map/ppermute | solution.py:323
  7.8 11.7 %collective-permute-start.1 = (f32[3,8,128]{2,1,0:T(8,128)}, f32[3,8,128]{2,1,0:T(8,128)S(1)}, u32[]{:S(2)}, u32[]{:S(2)}) collective-permute-start(f32[3,8,128]{2,1,0:T(8,128)} %get-tuple-element.16), channel_id=1, source_target_pairs={{0,480},{32,0},{64,32},{96,64},{128,96},{160,128},{192,160},{224,1... | collective-permute-start | bytes 36872 | tf_op jit(solution)/shard_map/ppermute | solution.py:323
  17.3 0.7 copy-start.8
  17.3 0.7 copy-start.15
  18.2 0.7 copy-start.14
  18.2 1.3 %copy-start.5 = (f32[8,8,128]{2,1,0:T(8,128)S(1)}, f32[8,8,128]{2,1,0:T(8,128)}, u32[]{:S(2)}) copy-start(f32[8,8,128]{2,1,0:T(8,128)} %get-tuple-element.17) | copy-start | bytes 98308
  18.9 0.6 copy-start.12
  19.5 0.7 slice-start
  20.2 5.4 %copy-start.13 = (f32[3,8,128]{2,1,0:T(8,128)S(1)}, f32[3,8,128]{2,1,0:T(8,128)}, u32[]{:S(2)}) copy-start(f32[3,8,128]{2,1,0:T(8,128)} %copy-done.12) | copy-start | bytes 36868
  20.2 8.4 %collective-permute-start.3 = (f32[12,8,128]{2,1,0:T(8,128)S(1)}, f32[12,8,128]{2,1,0:T(8,128)S(1)}, u32[]{:S(2)}, u32[]{:S(2)}) collective-permute-start(f32[12,8,128]{2,1,0:T(8,128)S(1)} %pad_maximum_fusion.1), channel_id=1, source_target_pairs={{8,0},{16,8},{24,16},{9,1},{17,9},{25,17},{10,2},{18,10},{26,18},{... | collective-permute-start | bytes 147464 | tf_op jit(solution)/shard_map/ppermute | solution.py:323
  21.6 6.9 %collective-permute-start.2 = (f32[12,8,128]{2,1,0:T(8,128)S(1)}, f32[12,8,128]{2,1,0:T(8,128)S(1)}, u32[]{:S(2)}, u32[]{:S(2)}) collective-permute-start(f32[12,8,128]{2,1,0:T(8,128)S(1)} %pad_maximum_fusion.1), channel_id=1, source_target_pairs={{0,8},{8,16},{16,24},{1,9},{9,17},{17,25},{2,10},{10,18},{18,26},{... | collective-permute-start | bytes 147464 | tf_op jit(solution)/shard_map/ppermute | solution.py:323
  28.6 5.6 %copy-start.1 = (f32[36,8,128]{2,1,0:T(8,128)}, f32[36,8,128]{2,1,0:T(8,128)S(1)}, u32[]{:S(2)}) copy-start(f32[36,8,128]{2,1,0:T(8,128)S(1)} %constant_dynamic-update-slice_fusion.middle) | copy-start | bytes 442372
  28.6 5.5 %collective-permute-start.5 = (f32[36,8,128]{2,1,0:T(8,128)S(1)}, f32[36,8,128]{2,1,0:T(8,128)S(1)}, u32[]{:S(2)}, u32[]{:S(2)}) collective-permute-start(f32[36,8,128]{2,1,0:T(8,128)S(1)} %constant_dynamic-update-slice_fusion.middle), channel_id=1, source_target_pairs={{0,7},{1,0},{2,1},{3,2},{4,3},{5,4},{6,5},{7,6},{8,15},{9,8},{10,9... | collective-permute-start | bytes 442376 | tf_op jit(solution)/shard_map/ppermute | solution.py:323
  30.1 4.0 %collective-permute-start.4 = (f32[36,8,128]{2,1,0:T(8,128)S(1)}, f32[36,8,128]{2,1,0:T(8,128)S(1)}, u32[]{:S(2)}, u32[]{:S(2)}) collective-permute-start(f32[36,8,128]{2,1,0:T(8,128)S(1)} %constant_dynamic-update-slice_fusion.middle), channel_id=1, source_target_pairs={{0,1},{1,2},{2,3},{3,4},{4,5},{5,6},{6,7},{7,0},{8,9},{9,10},{10,1... | collective-permute-start | bytes 442376 | tf_op jit(solution)/shard_map/ppermute | solution.py:323
  34.1 0.7 copy-start.3
  34.8 0.7 copy-start.4
  45.8 5.3 %collective-permute-start.7 = (f32[10,8,128]{2,1,0:T(8,128)}, f32[10,8,128]{2,1,0:T(8,128)S(1)}, u32[]{:S(2)}, u32[]{:S(2)}) collective-permute-start(f32[10,8,128]{2,1,0:T(8,128)} %first_step.1), channel_id=1, source_target_pairs={{8,0},{16,8},{24,16},{9,1},{17,9},{25,17},{10,2},{18,10},{26,18},{... | collective-permute-start | bytes 122888 | tf_op jit(solution)/shard_map/ppermute | solution.py:323
  47.1 5.4 %collective-permute-start.6 = (f32[10,8,128]{2,1,0:T(8,128)}, f32[10,8,128]{2,1,0:T(8,128)S(1)}, u32[]{:S(2)}, u32[]{:S(2)}) collective-permute-start(f32[10,8,128]{2,1,0:T(8,128)} %first_step.1), channel_id=1, source_target_pairs={{0,8},{8,16},{16,24},{1,9},{9,17},{17,25},{2,10},{10,18},{18,26},{... | collective-permute-start | bytes 122888 | tf_op jit(solution)/shard_map/ppermute | solution.py:323
  53.3 5.8 %copy-start = (f32[30,8,128]{2,1,0:T(8,128)}, f32[30,8,128]{2,1,0:T(8,128)S(1)}, u32[]{:S(2)}) copy-start(f32[30,8,128]{2,1,0:T(8,128)S(1)} %pad_maximum_fusion.middle) | copy-start | bytes 368644
  53.3 4.9 %collective-permute-start.9 = (f32[30,8,128]{2,1,0:T(8,128)S(1)}, f32[30,8,128]{2,1,0:T(8,128)S(1)}, u32[]{:S(2)}, u32[]{:S(2)}) collective-permute-start(f32[30,8,128]{2,1,0:T(8,128)S(1)} %pad_maximum_fusion.middle), channel_id=1, source_target_pairs={{0,7},{1,0},{2,1},{3,2},{4,3},{5,4},{6,5},{7,6},{8,15},{9,8},{10,9... | collective-permute-start | bytes 368648 | tf_op jit(solution)/shard_map/ppermute | solution.py:323
  57.2 1.9 %collective-permute-start.8 = (f32[30,8,128]{2,1,0:T(8,128)S(1)}, f32[30,8,128]{2,1,0:T(8,128)S(1)}, u32[]{:S(2)}, u32[]{:S(2)}) collective-permute-start(f32[30,8,128]{2,1,0:T(8,128)S(1)} %pad_maximum_fusion.middle), channel_id=1, source_target_pairs={{0,1},{1,2},{2,3},{3,4},{4,5},{5,6},{6,7},{7,0},{8,9},{9,10},{10,1... | collective-permute-start | bytes 368648 | tf_op jit(solution)/shard_map/ppermute | solution.py:323
  58.1 0.9 copy-start.6
  59.0 0.6 copy-start.7
  70.7 8.5 %copy-start.9 = (f32[64,128]{1,0:T(8,128)S(1)}, f32[64,128]{1,0:T(8,128)}, u32[]{:S(2)}) copy-start(f32[64,128]{1,0:T(8,128)} %get-tuple-element.20.own) | copy-start | bytes 98308
  70.7 20.1 %all-to-all-start = ((f32[16,8,128]{2,1,0:T(8,128)}), f32[16,8,128]{2,1,0:T(8,128)S(1)}, u32[]{:S(2)}, u32[]{:S(2)}) async-start(f32[16,8,128]{2,1,0:T(8,128)} %get-tuple-element.21), calls=%async_computation | async-start | bytes 131072 | tf_op jit(solution)/shard_map/all_to_all | solution.py:434
  79.3 5.9 %collective-permute-start.11 = (f32[64,128]{1,0:T(8,128)S(1)}, f32[64,128]{1,0:T(8,128)S(1)}, u32[]{:S(2)}, u32[]{:S(2)}) collective-permute-start(f32[64,128]{1,0:T(8,128)S(1)} %copy-done.9), channel_id=1, source_target_pairs={{32,0},{64,32},{96,64},{128,96},{160,128},{192,160},{224,192},{256... | collective-permute-start | bytes 98312 | tf_op jit(solution)/shard_map/ppermute | solution.py:323
  80.6 5.0 %collective-permute-start.10 = (f32[64,128]{1,0:T(8,128)S(1)}, f32[64,128]{1,0:T(8,128)S(1)}, u32[]{:S(2)}, u32[]{:S(2)}) collective-permute-start(f32[64,128]{1,0:T(8,128)S(1)} %copy-done.9), channel_id=1, source_target_pairs={{0,32},{32,64},{64,96},{96,128},{128,160},{160,192},{192,224},{224... | collective-permute-start | bytes 98312 | tf_op jit(solution)/shard_map/ppermute | solution.py:323
  85.2 5.7 %copy-start.10 = (f32[64,128]{1,0:T(8,128)}, f32[64,128]{1,0:T(8,128)S(1)}, u32[]{:S(2)}) copy-start(f32[64,128]{1,0:T(8,128)S(1)} %collective-permute-done.11.after) | copy-start | bytes 98308
  85.6 5.3 %copy-start.11 = (f32[64,128]{1,0:T(8,128)}, f32[64,128]{1,0:T(8,128)S(1)}, u32[]{:S(2)}) copy-start(f32[64,128]{1,0:T(8,128)S(1)} %collective-permute-done.10.before) | copy-start | bytes 98308
  90.8 0.6 copy-start.2

commit v3 on v2

--- a/solution.py
+++ b/solution.py
@@ -29,6 +29,8 @@
 ITSELF = 4096
 COMPS = 10
 VMEM = pl.BlockSpec(memory_space=pltpu.VMEM)
+SMALL = pltpu.CompilerParams(vmem_limit_bytes=4 << 20)
+LARGE = pltpu.CompilerParams(vmem_limit_bytes=10 << 20)
 SMEM = pl.BlockSpec(memory_space=pltpu.SMEM)
 
 RAW = [math.exp(-d * d / (2.0 * SIGMA * SIGMA)) for d in range(HW + 1)]
@@ -156,7 +158,7 @@
     sub = lax.broadcasted_iota(jnp.int32, (8, 128), 0)
 
     def one(t, *work):
-        own = tiles[4 * width + t + 1]
+        own = tiles[4 * width + t + 2]
         sums = pair_sums(tiles, meta, t * 8, own, False, *work)
         radius = own[6:7, :]
         gain = STEP_DT / (DENS * radius * radius * radius)
@@ -168,7 +170,7 @@
             fresh = jnp.where(sub == 3 + axis, speed, fresh)
         out[t] = fresh
 
-    @pl.loop(0, (width - 2) // 2)
+    @pl.loop(0, (width - 4) // 2)
     def _(t):
         one(2 * t, work[0], work[1], work[2])
         one(2 * t + 1, work[0], work[3], work[4])
@@ -309,12 +311,13 @@
             out[t, 3 + axis : 4 + axis, :] = speed[axis, t : t + 1, :]
         out[t, 6:7, :] = radius[t : t + 1, :]
         out[t, 7:8, :] = code[t : t + 1, :]
-    for ref, edge, first in ((to_left, 0, 0), (to_right, NT - 1, NT - 2)):
-        ref[0] = out[first]
-        ref[1] = out[first + 1]
-        ref[2] = jnp.zeros((8, 128), jnp.float32)
-        ref[2, 0:1, 0:K] = lists[edge : edge + 1, :].astype(jnp.float32)
-        ref[2, 1:2, 0:NT] = counts[...].astype(jnp.float32)
+    for ref, notes, tile, first in ((to_left, 2, 0, 0), (to_right, 0, 1, NT - 2)):
+        ref[tile] = out[first]
+        ref[tile + 1] = out[first + 1]
+        ref[notes] = jnp.zeros((8, 128), jnp.float32)
+        for slot in range(K):
+            ref[notes, slot : slot + 1, 0:NT] = lists[slot].astype(jnp.float32)
+        ref[notes, K : K + 1, 0:NT] = counts[...].astype(jnp.float32)
 
 
 def shifted(value, axis, step, wrap):
@@ -353,7 +356,7 @@
 
 def shards(positions, velocities, radius, group, broken, cell, neighbours, counts):
     lists = neighbours.reshape(NT, K)
-    listed = counts.reshape(1, NT)
+    listed = counts.reshape(NT, 1)
     tile = jax.ShapeDtypeStruct((NT, 8, 128), jnp.float32)
     edge = jax.ShapeDtypeStruct((3, 8, 128), jnp.float32)
     own, to_left, to_right = pl.pallas_call(
@@ -361,6 +364,7 @@
         out_shape=(tile, edge, edge),
         in_specs=[VMEM] * 7,
         out_specs=(VMEM, VMEM, VMEM),
+        compiler_params=SMALL,
         name="pack",
     )(
         positions.reshape(3, NT, 128),
@@ -368,13 +372,13 @@
         radius.reshape(NT, 128),
         group.reshape(NT, 128),
         broken.reshape(NT, 128),
-        lists,
-        listed,
+        lists.T.reshape(K, 1, NT),
+        counts.reshape(1, NT),
     )
     from_left = shifted(to_right, "gx", 1, True)
     from_right = shifted(to_left, "gx", -1, True)
-    line = jnp.concatenate([from_left[0:2], own, from_right[0:2]], axis=0)
-    width = NT + 4
+    line = jnp.concatenate([from_left, own, from_right], axis=0)
+    width = NT + 6
 
     def extended(tiles):
         up = shifted(tiles, "gy", 1, False)
@@ -385,31 +389,30 @@
         return low, middle, high
 
     low, middle, high = extended(line)
-    all_lists = jnp.concatenate(
-        [from_left[2, 0:1, 0:K].astype(jnp.int32), lists, from_right[2, 0:1, 0:K].astype(jnp.int32)], axis=0
-    )
-    all_counts = jnp.concatenate(
-        [from_left[2, 1, NT - 1 : NT].astype(jnp.int32), listed[0], from_right[2, 1, 0:1].astype(jnp.int32)]
-    )
+    left_notes = from_left[0, 0:7, NT - 1].astype(jnp.int32)
+    right_notes = from_right[2, 0:7, 0].astype(jnp.int32)
+    all_lists = jnp.concatenate([left_notes[None, 0:K], lists, right_notes[None, 0:K]], axis=0)
+    all_counts = jnp.concatenate([left_notes[None, K:7], listed, right_notes[None, K:7]], axis=0)
     spots = lax.broadcasted_iota(jnp.int32, (NT + 2, 1), 0)
     shift = jnp.where(spots == 0, -1, jnp.where(spots == NT + 1, 1, 0))
-    first_meta = list_entries(all_lists, all_counts[:, None], spots + 1, shift, width, 2)
+    first_meta = list_entries(all_lists, all_counts, spots + 2, shift, width, 3)
     spots = lax.broadcasted_iota(jnp.int32, (NT, 1), 0)
-    second_meta = list_entries(lists, listed.reshape(NT, 1), spots + 1, 0, width - 2, 1)
+    second_meta = list_entries(lists, listed, spots + 1, 0, width - 4, 1)
 
     line = pl.pallas_call(
         first_kernel,
-        out_shape=jax.ShapeDtypeStruct((width - 2, 8, 128), jnp.float32),
+        out_shape=jax.ShapeDtypeStruct((width - 4, 8, 128), jnp.float32),
         in_specs=[SMEM] + [VMEM] * 3,
         out_specs=VMEM,
         scratch_shapes=[
             pltpu.VMEM((9 * width, 8, 128), jnp.float32),
             *work_space(),
         ],
+        compiler_params=LARGE,
         name="first_step",
     )(first_meta, low, middle, high)
     low, middle, high = extended(line)
-    width = width - 2
+    width = width - 4
     peers = lax.axis_size("gx")
     block = jax.ShapeDtypeStruct((3, NT, 128), jnp.float32)
     places, speeds, grid, energy = pl.pallas_call(
@@ -429,6 +432,7 @@
             pltpu.VMEM((8, 128), jnp.float32),
             *work_space(),
         ],
+        compiler_params=LARGE,
         name="second_step",
     )(second_meta, cell.reshape(NT, 128), low, middle, high)
     energy = lax.all_to_all(energy, "gx", 0, 0, tiled=True)
@@ -441,6 +445,7 @@
         out_shape=jax.ShapeDtypeStruct((rows, 8, 128), jnp.float32),
         in_specs=[SMEM] + [VMEM] * 4,
         out_specs=VMEM,
+        compiler_params=SMALL,
         name="planes",
     )(coords, grid, before, after, energy)
     parts = lax.all_to_all(parts, ("gy", "gz"), 0, 0, tiled=True)
@@ -453,6 +458,7 @@
         ),
         in_specs=[VMEM],
         out_specs=(VMEM, VMEM, SMEM),
+        compiler_params=SMALL,
         name="lines",
     )(parts)
     return (

time: 114 us -> 106 us (0.930)
  Pallas kernels: 26.4 us -> 21.3 us
  local copies, waits for them, and re-layouts: 9.23 us -> 5.07 us
  waiting for transfers between devices: 10 us -> 11.5 us
  starting transfers between devices: 44.9 us -> 46.3 us
  between operations: 2.23 us -> 0.91 us
    unnamed x37 -> x23, local copies, waits for them, and re-layouts: 5.73 us -> 2.83 us
    ppermute x12, waiting for transfers between devices: 4.77 us -> 6.24 us  [shifted(): return lax.ppermute(value, axis, pairs)]
    pallas_call x1, Pallas kernels: 1.41 us -> 0.03 us  [shards(): pl.pallas_call(pack_kernel, out_shape=(tile, edge, edge), in_specs=[VMEM]...]
    concatenate x2 -> x1, other arithmetic: 0.08 us -> 1.37 us  [shards(): jnp.concatenate([left_notes[None, K:7], listed, right_notes[None, K:7]],...]
    pallas_call x1, Pallas kernels: 10.3 us -> 9.2 us  [shards(): pl.pallas_call(first_kernel, out_shape=jax.ShapeDtypeStruct((width - 4, 8...]
  transfers between devices with their start and end apart: 13 -> 13, of which waited for: 6 -> 6; matrix products, arithmetic and copies ran while one was open for 4% -> 3% of each run, Pallas kernels for 0% -> 0%
where the time goes in v3:
time: 106 us
  starting transfers between devices  46.3 us (44%)
  Pallas kernels  21.3 us (20%)
  blocking collectives  18.1 us (17%)
  waiting for transfers between devices  11.5 us (11%)
  local copies, waits for them, and re-layouts  5.07 us (5%)
  other arithmetic  2.3 us (2%)
    ppermute x12, starting transfers between devices, shifted(): return lax.ppermute(value, axis, pairs)  37 us
    all_to_all x1, blocking collectives, shards(): parts = lax.all_to_all(parts, ('gy', 'gz'), 0, 0, tiled=True)  18.1 us
    pallas_call x1, Pallas kernels, shards(): pl.pallas_call(second_kernel, out_shape=(block, block, jax.ShapeDtypeStru...  10.4 us
    all_to_all x1, starting transfers between devices, shards(): energy = lax.all_to_all(energy, 'gx', 0, 0, tiled=True)  9.37 us
    pallas_call x1, Pallas kernels, shards(): pl.pallas_call(first_kernel, out_shape=jax.ShapeDtypeStruct((width - 4, 8...  9.2 us
    ppermute x12, waiting for transfers between devices, shifted(): return lax.ppermute(value, axis, pairs)  6.24 us
    all_to_all x1, waiting for transfers between devices, shards(): energy = lax.all_to_all(energy, 'gx', 0, 0, tiled=True)  5.27 us
    unnamed x23, local copies, waits for them, and re-layouts  2.83 us
  transfers between devices with their start and end apart: 13, of which 6 were waited for; matrix products, arithmetic and copies ran while one was open for 3% of the time, Pallas kernels for 0%

profile of v3, /device:TPU:1, one launch (start us, length us, event | category | flops | bytes accessed | tf_op | source)
XLA Modules:
  0.0 105.5 jit_solution(13123597500368367606)
XLA Ops:
  0.7 0.7 copy.51
  1.4 0.6 copy-done.2
  2.0 0.7 copy-done.4
  2.7 0.7 copy-done.5
  3.4 0.7 copy-done.6
  4.1 4.4 %collective-permute-start = (f32[3,8,128]{2,1,0:T(8,128)S(1)}, f32[3,8,128]{2,1,0:T(8,128)S(1)}, u32[]{:S(2)}, u32[]{:S(2)}) collective-permute-start(f32[3,8,128]{2,1,0:T(8,128)S(1)} %get-tuple-element.15), channel_id=1, source_target_pairs={{0,32},{32,64},{64,96},{96,128},{128,160},{160,192},{192,224},{224... | collective-permute-start | bytes 36872 | tf_op jit(solution)/shard_map/ppermute | solution.py:326
  8.5 0.0 copy-start.7
  8.5 9.5 %collective-permute-start.1 = (f32[3,8,128]{2,1,0:T(8,128)S(1)}, f32[3,8,128]{2,1,0:T(8,128)S(1)}, u32[]{:S(2)}, u32[]{:S(2)}) collective-permute-start(f32[3,8,128]{2,1,0:T(8,128)S(1)} %get-tuple-element.16), channel_id=1, source_target_pairs={{0,480},{32,0},{64,32},{96,64},{128,96},{160,128},{192,160},{224,1... | collective-permute-start | bytes 36872 | tf_op jit(solution)/shard_map/ppermute | solution.py:326
  18.0 0.1 copy.31
  18.1 0.2 convert_reduce_fusion.1
  18.3 0.1 copy.32
  18.4 0.1 select_reduce_fusion.3
  18.5 0.1 slice_convert_fusion.1
  18.6 0.5 slice.23
  19.1 0.5 slice.25
  19.6 1.3 %collective-permute-start.3 = (f32[14,8,128]{2,1,0:T(8,128)S(1)}, f32[14,8,128]{2,1,0:T(8,128)S(1)}, u32[]{:S(2)}, u32[]{:S(2)}) collective-permute-start(f32[14,8,128]{2,1,0:T(8,128)S(1)} %constant_dynamic-update-slice_fusion), channel_id=1, source_target_pairs={{8,0},{16,8},{24,16},{9,1},{17,9},{25,17},{10,2},{18,10},{26,18},{... | collective-permute-start | bytes 172040 | tf_op jit(solution)/shard_map/ppermute | solution.py:326
  20.9 4.0 %collective-permute-start.2 = (f32[14,8,128]{2,1,0:T(8,128)S(1)}, f32[14,8,128]{2,1,0:T(8,128)S(1)}, u32[]{:S(2)}, u32[]{:S(2)}) collective-permute-start(f32[14,8,128]{2,1,0:T(8,128)S(1)} %constant_dynamic-update-slice_fusion), channel_id=1, source_target_pairs={{0,8},{8,16},{16,24},{1,9},{9,17},{17,25},{2,10},{10,18},{18,26},{... | collective-permute-start | bytes 172040 | tf_op jit(solution)/shard_map/ppermute | solution.py:326
  24.9 1.4 %add_bitcast_fusion = s32[10]{0:T(128)S(1)} fusion(s32[1,1]{0,1:T(1,128)} %bitcast.16, s32[8,1]{0,1:T(1,128)S(1)} %bitcast.78, s32[1,1]{0,1:T(1,128)} %bitcast.13), kind=kLoop, calls=%fused_computation.93 | loop fusion | flops 20 | bytes 80 | tf_op jit(solution)/shard_map/concatenate | solution.py:395
  26.3 0.1 convert_reduce_fusion
  26.4 0.1 select_reduce_fusion.1
  26.6 2.0 %collective-permute-start.5 = (f32[42,8,128]{2,1,0:T(8,128)S(1)}, f32[42,8,128]{2,1,0:T(8,128)S(1)}, u32[]{:S(2)}, u32[]{:S(2)}) collective-permute-start(f32[42,8,128]{2,1,0:T(8,128)S(1)} %constant_dynamic-update-slice_fusion.3.middle), channel_id=1, source_target_pairs={{0,7},{1,0},{2,1},{3,2},{4,3},{5,4},{6,5},{7,6},{8,15},{9,8},{10,9... | collective-permute-start | bytes 516104 | tf_op jit(solution)/shard_map/ppermute | solution.py:326
  28.6 1.2 %collective-permute-start.4 = (f32[42,8,128]{2,1,0:T(8,128)S(1)}, f32[42,8,128]{2,1,0:T(8,128)S(1)}, u32[]{:S(2)}, u32[]{:S(2)}) collective-permute-start(f32[42,8,128]{2,1,0:T(8,128)S(1)} %constant_dynamic-update-slice_fusion.3.middle), channel_id=1, source_target_pairs={{0,1},{1,2},{2,3},{3,4},{4,5},{5,6},{6,7},{7,0},{8,9},{9,10},{10,1... | collective-permute-start | bytes 516104 | tf_op jit(solution)/shard_map/ppermute | solution.py:326
  29.8 0.1 add_select_fusion.12
  29.9 0.1 copy.42
  30.0 0.1 reshape.838.meta
  30.1 2.8 %collective-permute-done.5.high = f32[42,8,128]{2,1,0:T(8,128)S(1)} collective-permute-done((f32[42,8,128]{2,1,0:T(8,128)S(1)}, f32[42,8,128]{2,1,0:T(8,128)S(1)}, u32[]{:S(2)}, u32[]{:S(2)}) %collective-permute-start.5) | collective-permute-done | bytes 172064 | tf_op jit(solution)/shard_map/ppermute | solution.py:326
  32.9 9.2 %first_step.1 = f32[10,8,128]{2,1,0:T(8,128)S(1)} custom-call(s32[80]{0:T(128)S(1)} %reshape.838.meta, f32[42,8,128]{2,1,0:T(8,128)S(1)} %collective-permute-done.4.low, f32[42,8,128]{2,1,0:T(8,128)S(1)} %constant_dynamic-update-slice_fusion.3.middle, f32[42,8,128]{2,1,0:T(8,128)S(1)} %collective-permute-done.5.high), custom_call_target="tpu_custom_call" | custom-call | tf_op jit(solution)/shard_map/first_step/pallas_call | solution.py:402
  42.1 1.3 %collective-permute-start.7 = (f32[10,8,128]{2,1,0:T(8,128)S(1)}, f32[10,8,128]{2,1,0:T(8,128)S(1)}, u32[]{:S(2)}, u32[]{:S(2)}) collective-permute-start(f32[10,8,128]{2,1,0:T(8,128)S(1)} %first_step.1), channel_id=1, source_target_pairs={{8,0},{16,8},{24,16},{9,1},{17,9},{25,17},{10,2},{18,10},{26,18},{... | collective-permute-start | bytes 122888 | tf_op jit(solution)/shard_map/ppermute | solution.py:326
  43.4 4.9 %collective-permute-start.6 = (f32[10,8,128]{2,1,0:T(8,128)S(1)}, f32[10,8,128]{2,1,0:T(8,128)S(1)}, u32[]{:S(2)}, u32[]{:S(2)}) collective-permute-start(f32[10,8,128]{2,1,0:T(8,128)S(1)} %first_step.1), channel_id=1, source_target_pairs={{0,8},{8,16},{16,24},{1,9},{9,17},{17,25},{2,10},{10,18},{18,26},{... | collective-permute-start | bytes 122888 | tf_op jit(solution)/shard_map/ppermute | solution.py:326
  48.3 1.1 %collective-permute-done.6 = f32[10,8,128]{2,1,0:T(8,128)S(1)} collective-permute-done((f32[10,8,128]{2,1,0:T(8,128)S(1)}, f32[10,8,128]{2,1,0:T(8,128)S(1)}, u32[]{:S(2)}, u32[]{:S(2)}) %collective-permute-start.6) | collective-permute-done | bytes 40992 | tf_op jit(solution)/shard_map/ppermute | solution.py:326
  49.4 3.1 %collective-permute-start.9 = (f32[30,8,128]{2,1,0:T(8,128)S(1)}, f32[30,8,128]{2,1,0:T(8,128)S(1)}, u32[]{:S(2)}, u32[]{:S(2)}) collective-permute-start(f32[30,8,128]{2,1,0:T(8,128)S(1)} %pad_maximum_fusion.middle), channel_id=1, source_target_pairs={{0,7},{1,0},{2,1},{3,2},{4,3},{5,4},{6,5},{7,6},{8,15},{9,8},{10,9... | collective-permute-start | bytes 368648 | tf_op jit(solution)/shard_map/ppermute | solution.py:326
  52.5 0.1 add_select_fusion.13
  52.6 0.1 copy.33
  52.7 0.1 copy.34
  52.8 0.1 select_reduce_fusion.2
  52.9 0.1 reshape.828.meta
  53.0 1.4 %collective-permute-done.9.high = f32[30,8,128]{2,1,0:T(8,128)S(1)} collective-permute-done((f32[30,8,128]{2,1,0:T(8,128)S(1)}, f32[30,8,128]{2,1,0:T(8,128)S(1)}, u32[]{:S(2)}, u32[]{:S(2)}) %collective-permute-start.9) | collective-permute-done | bytes 122912 | tf_op jit(solution)/shard_map/ppermute | solution.py:326
  54.3 0.1 collective-permute-done.8.low
  54.4 10.4 %second_step.1 = (f32[3,8,128]{2,1,0:T(8,128)}, f32[3,8,128]{2,1,0:T(8,128)}, f32[64,128]{1,0:T(8,128)S(1)}, f32[16,8,128]{2,1,0:T(8,128)}) custom-call(s32[64]{0:T(128)S(1)} %reshape.828.meta, s32[8,128]{1,0:T(8,128)S(1)} %bitcast.79, f32[30,8,128]{2,1,0:T(8,128)S(1)} %collective-permute-done.8.low, f32[30,8,128]{2,1,0:T(8,128)S(1)} %pad_maximum_fusion.middle, ...), custom_call_target="tpu_custom_call" | custom-call | tf_op jit(solution)/shard_map/second_step/pallas_call | solution.py:418
  64.8 9.4 %all-to-all-start = ((f32[16,8,128]{2,1,0:T(8,128)}), f32[16,8,128]{2,1,0:T(8,128)S(1)}, u32[]{:S(2)}, u32[]{:S(2)}) async-start(f32[16,8,128]{2,1,0:T(8,128)} %get-tuple-element.21), calls=%async_computation | async-start | bytes 131072 | tf_op jit(solution)/shard_map/all_to_all | solution.py:438
  74.2 1.3 %collective-permute-start.11 = (f32[64,128]{1,0:T(8,128)S(1)}, f32[64,128]{1,0:T(8,128)S(1)}, u32[]{:S(2)}, u32[]{:S(2)}) collective-permute-start(f32[64,128]{1,0:T(8,128)S(1)} %get-tuple-element.20.own), channel_id=1, source_target_pairs={{32,0},{64,32},{96,64},{128,96},{160,128},{192,160},{224,192},{256... | collective-permute-start | bytes 98312 | tf_op jit(solution)/shard_map/ppermute | solution.py:326
  75.5 4.0 %collective-permute-start.10 = (f32[64,128]{1,0:T(8,128)S(1)}, f32[64,128]{1,0:T(8,128)S(1)}, u32[]{:S(2)}, u32[]{:S(2)}) collective-permute-start(f32[64,128]{1,0:T(8,128)S(1)} %get-tuple-element.20.own), channel_id=1, source_target_pairs={{0,32},{32,64},{64,96},{96,128},{128,160},{160,192},{192,224},{224... | collective-permute-start | bytes 98312 | tf_op jit(solution)/shard_map/ppermute | solution.py:326
  79.5 0.1 pad_add_fusion.1.coords
  79.6 0.9 collective-permute-done.10.before
  80.5 5.3 %all-to-all-done.energy = f32[16,8,128]{2,1,0:T(8,128)S(1)} async-done(((f32[16,8,128]{2,1,0:T(8,128)}), f32[16,8,128]{2,1,0:T(8,128)S(1)}, u32[]{:S(2)}, u32[]{:S(2)}) %all-to-all-start) | async-done | bytes 65568 | tf_op jit(solution)/shard_map/all_to_all | solution.py:438
  85.8 0.9 planes.1
  86.7 18.1 %all_to_all.10.parts = f32[32,8,128]{2,1,0:T(8,128)S(1)} all-to-all(f32[32,8,128]{2,1,0:T(8,128)S(1)} %planes.1), channel_id=1, replica_groups=mesh['gx'=16,'gy'=4,'gz'=8] {'gy','gz'}, dimensions={0} | all-to-all | bytes 262144 | tf_op jit(solution)/shard_map/all_to_all | solution.py:451
  104.8 0.8 lines.1
  (40 shorter events, 0.2 us)
Async XLA Ops:
  0.6 0.7 copy-start.1
  0.6 0.7 copy-start
  1.4 0.7 copy-start.2
  2.0 0.7 copy-start.4
  2.7 0.7 copy-start.5
  3.4 0.7 copy-start.6
  4.1 14.4 %collective-permute-start = (f32[3,8,128]{2,1,0:T(8,128)S(1)}, f32[3,8,128]{2,1,0:T(8,128)S(1)}, u32[]{:S(2)}, u32[]{:S(2)}) collective-permute-start(f32[3,8,128]{2,1,0:T(8,128)S(1)} %get-tuple-element.15), channel_id=1, source_target_pairs={{0,32},{32,64},{64,96},{96,128},{128,160},{160,192},{192,224},{224... | collective-permute-start | bytes 36872 | tf_op jit(solution)/shard_map/ppermute | solution.py:326
  8.5 9.5 %copy-start.7 = (s32[1,1,1,8,6]{3,2,4,1,0:T(1,128)S(1)}, s32[1,1,1,8,6]{3,2,4,1,0:T(1,128)}, u32[]{:S(2)}) copy-start(s32[1,1,1,8,6]{3,2,4,1,0:T(1,128)} %param.14) | copy-start | bytes 580
  8.5 10.6 %collective-permute-start.1 = (f32[3,8,128]{2,1,0:T(8,128)S(1)}, f32[3,8,128]{2,1,0:T(8,128)S(1)}, u32[]{:S(2)}, u32[]{:S(2)}) collective-permute-start(f32[3,8,128]{2,1,0:T(8,128)S(1)} %get-tuple-element.16), channel_id=1, source_target_pairs={{0,480},{32,0},{64,32},{96,64},{128,96},{160,128},{192,160},{224,1... | collective-permute-start | bytes 36872 | tf_op jit(solution)/shard_map/ppermute | solution.py:326
  19.6 6.9 %collective-permute-start.3 = (f32[14,8,128]{2,1,0:T(8,128)S(1)}, f32[14,8,128]{2,1,0:T(8,128)S(1)}, u32[]{:S(2)}, u32[]{:S(2)}) collective-permute-start(f32[14,8,128]{2,1,0:T(8,128)S(1)} %constant_dynamic-update-slice_fusion), channel_id=1, source_target_pairs={{8,0},{16,8},{24,16},{9,1},{17,9},{25,17},{10,2},{18,10},{26,18},{... | collective-permute-start | bytes 172040 | tf_op jit(solution)/shard_map/ppermute | solution.py:326
  20.9 5.6 %collective-permute-start.2 = (f32[14,8,128]{2,1,0:T(8,128)S(1)}, f32[14,8,128]{2,1,0:T(8,128)S(1)}, u32[]{:S(2)}, u32[]{:S(2)}) collective-permute-start(f32[14,8,128]{2,1,0:T(8,128)S(1)} %constant_dynamic-update-slice_fusion), channel_id=1, source_target_pairs={{0,8},{8,16},{16,24},{1,9},{9,17},{17,25},{2,10},{10,18},{18,26},{... | collective-permute-start | bytes 172040 | tf_op jit(solution)/shard_map/ppermute | solution.py:326
  26.6 6.3 %collective-permute-start.5 = (f32[42,8,128]{2,1,0:T(8,128)S(1)}, f32[42,8,128]{2,1,0:T(8,128)S(1)}, u32[]{:S(2)}, u32[]{:S(2)}) collective-permute-start(f32[42,8,128]{2,1,0:T(8,128)S(1)} %constant_dynamic-update-slice_fusion.3.middle), channel_id=1, source_target_pairs={{0,7},{1,0},{2,1},{3,2},{4,3},{5,4},{6,5},{7,6},{8,15},{9,8},{10,9... | collective-permute-start | bytes 516104 | tf_op jit(solution)/shard_map/ppermute | solution.py:326
  28.6 4.3 %collective-permute-start.4 = (f32[42,8,128]{2,1,0:T(8,128)S(1)}, f32[42,8,128]{2,1,0:T(8,128)S(1)}, u32[]{:S(2)}, u32[]{:S(2)}) collective-permute-start(f32[42,8,128]{2,1,0:T(8,128)S(1)} %constant_dynamic-update-slice_fusion.3.middle), channel_id=1, source_target_pairs={{0,1},{1,2},{2,3},{3,4},{4,5},{5,6},{6,7},{7,0},{8,9},{9,10},{10,1... | collective-permute-start | bytes 516104 | tf_op jit(solution)/shard_map/ppermute | solution.py:326
  42.1 6.2 %collective-permute-start.7 = (f32[10,8,128]{2,1,0:T(8,128)S(1)}, f32[10,8,128]{2,1,0:T(8,128)S(1)}, u32[]{:S(2)}, u32[]{:S(2)}) collective-permute-start(f32[10,8,128]{2,1,0:T(8,128)S(1)} %first_step.1), channel_id=1, source_target_pairs={{8,0},{16,8},{24,16},{9,1},{17,9},{25,17},{10,2},{18,10},{26,18},{... | collective-permute-start | bytes 122888 | tf_op jit(solution)/shard_map/ppermute | solution.py:326
  43.4 6.0 %collective-permute-start.6 = (f32[10,8,128]{2,1,0:T(8,128)S(1)}, f32[10,8,128]{2,1,0:T(8,128)S(1)}, u32[]{:S(2)}, u32[]{:S(2)}) collective-permute-start(f32[10,8,128]{2,1,0:T(8,128)S(1)} %first_step.1), channel_id=1, source_target_pairs={{0,8},{8,16},{16,24},{1,9},{9,17},{17,25},{2,10},{10,18},{18,26},{... | collective-permute-start | bytes 122888 | tf_op jit(solution)/shard_map/ppermute | solution.py:326
  49.4 4.9 %collective-permute-start.9 = (f32[30,8,128]{2,1,0:T(8,128)S(1)}, f32[30,8,128]{2,1,0:T(8,128)S(1)}, u32[]{:S(2)}, u32[]{:S(2)}) collective-permute-start(f32[30,8,128]{2,1,0:T(8,128)S(1)} %pad_maximum_fusion.middle), channel_id=1, source_target_pairs={{0,7},{1,0},{2,1},{3,2},{4,3},{5,4},{6,5},{7,6},{8,15},{9,8},{10,9... | collective-permute-start | bytes 368648 | tf_op jit(solution)/shard_map/ppermute | solution.py:326
  52.5 1.9 %collective-permute-start.8 = (f32[30,8,128]{2,1,0:T(8,128)S(1)}, f32[30,8,128]{2,1,0:T(8,128)S(1)}, u32[]{:S(2)}, u32[]{:S(2)}) collective-permute-start(f32[30,8,128]{2,1,0:T(8,128)S(1)} %pad_maximum_fusion.middle), channel_id=1, source_target_pairs={{0,1},{1,2},{2,3},{3,4},{4,5},{5,6},{6,7},{7,0},{8,9},{9,10},{10,1... | collective-permute-start | bytes 368648 | tf_op jit(solution)/shard_map/ppermute | solution.py:326
  52.9 1.5 %copy-start.3 = (s32[1,1,1,1024]{3,2,1,0:T(1,128)S(1)}, s32[1,1,1,1024]{3,2,1,0:T(1,128)}, u32[]{:S(2)}) copy-start(s32[1,1,1,1024]{3,2,1,0:T(1,128)} %param.13) | copy-start | bytes 12292
  64.8 20.9 %all-to-all-start = ((f32[16,8,128]{2,1,0:T(8,128)}), f32[16,8,128]{2,1,0:T(8,128)S(1)}, u32[]{:S(2)}, u32[]{:S(2)}) async-start(f32[16,8,128]{2,1,0:T(8,128)} %get-tuple-element.21), calls=%async_computation | async-start | bytes 131072 | tf_op jit(solution)/shard_map/all_to_all | solution.py:438
  74.2 5.4 %collective-permute-start.11 = (f32[64,128]{1,0:T(8,128)S(1)}, f32[64,128]{1,0:T(8,128)S(1)}, u32[]{:S(2)}, u32[]{:S(2)}) collective-permute-start(f32[64,128]{1,0:T(8,128)S(1)} %get-tuple-element.20.own), channel_id=1, source_target_pairs={{32,0},{64,32},{96,64},{128,96},{160,128},{192,160},{224,192},{256... | collective-permute-start | bytes 98312 | tf_op jit(solution)/shard_map/ppermute | solution.py:326
  75.5 5.0 %collective-permute-start.10 = (f32[64,128]{1,0:T(8,128)S(1)}, f32[64,128]{1,0:T(8,128)S(1)}, u32[]{:S(2)}, u32[]{:S(2)}) collective-permute-start(f32[64,128]{1,0:T(8,128)S(1)} %get-tuple-element.20.own), channel_id=1, source_target_pairs={{0,32},{32,64},{64,96},{96,128},{128,160},{160,192},{192,224},{224... | collective-permute-start | bytes 98312 | tf_op jit(solution)/shard_map/ppermute | solution.py:326

commit v4 on v3

--- a/solution.py
+++ b/solution.py
@@ -42,38 +42,16 @@
     return jnp.concatenate([value, value], axis=0)
 
 
-def parts_of(value, count):
-    parts = []
-    for _ in range(count):
-        part = value.astype(jnp.bfloat16)
-        parts.append(part)
-        value = value - part.astype(jnp.float32)
-    return parts
-
-
-def selector():
-    shape = (32, 8 * 128)
-    line = lax.broadcasted_iota(jnp.int32, shape, 0)
-    block = lax.shift_right_logical(lax.broadcasted_iota(jnp.int32, shape, 1), 7)
-    hit = jnp.logical_and(lax.bitwise_and(line, 7) == block, line < 24)
-    return jnp.where(hit, 1.0, 0.0).astype(jnp.bfloat16)
-
-
-def own_columns(own, select, mine):
-    stack = jnp.concatenate(
-        [part.astype(jnp.float32) for part in parts_of(own, 3)] + [jnp.zeros((8, 128), jnp.float32)], axis=0
-    ).astype(jnp.bfloat16)
-    wide = lax.dot_general(
-        stack, select[...], (((0,), (0,)), ((), ())), preferred_element_type=jnp.float32
-    )
+def own_columns(own, mine):
     for c in range(8):
-        mine[c] = wide[:, 128 * c : 128 * c + 128]
-
-
-def pair_sums(tiles, meta, base, own, second, select, rows, mine):
+        mine[c] = jnp.broadcast_to(own[c : c + 1, :], (128, 128)).T
+
+
+def pair_sums(tiles, meta, t, own, second, rows, mine):
     lane = lax.broadcasted_iota(jnp.int32, (8, 128), 1).astype(jnp.float32)
+    stride = meta.shape[0] // K
     for slot in range(K):
-        entry = meta[base + slot]
+        entry = meta[slot * stride + t]
         index = lax.bitwise_and(entry, 1023)
         live = lax.bitwise_and(entry, LIVE) > 0
         for c in range(8 if slot < 3 else 7):
@@ -85,12 +63,10 @@
             rows[9 * slot + c] = value
         if second and slot < 3:
             rows[9 * slot + 8] = jnp.where(lax.bitwise_and(entry, ITSELF) > 0, lane, -1.0)
-    own_columns(own, select, mine)
+    own_columns(own, mine)
     number = lax.broadcasted_iota(jnp.int32, (16, 128), 0).astype(jnp.float32)
-    whole_lane = twice(lane)
-    ones = jnp.ones((256, 128), jnp.bfloat16)
     count = 11 if second else 3
-    totals = [jnp.zeros((16, 128), jnp.float32)] * count
+    stacks = []
     for block in range(8):
         xi, yi, zi, ui, vi, wi, ri, ci = [mine[c, 16 * block : 16 * block + 16, :] for c in range(8)]
         ci = jnp.where(ci < 0.0, -5.0, ci)
@@ -126,18 +102,13 @@
                 else:
                     terms += [energy]
             added = [a + b for a, b in zip(added, terms)] + added[len(terms) :]
-        stack = jnp.concatenate([jnp.concatenate(parts_of(value, 2), axis=1) for value in added], axis=0)
-        sums = jnp.dot(stack, ones, preferred_element_type=jnp.float32)
-        diagonal = whole_lane == here
-        totals = [
-            jnp.where(diagonal, sums[16 * i : 16 * i + 16, :], total) for i, total in enumerate(totals)
-        ]
+        stacks.append(added)
+    totals = [jnp.concatenate([added[i] for added in stacks], axis=0).T for i in range(count)]
     return [jnp.sum(total, axis=0, keepdims=True) for total in totals]
 
 
 def work_space():
     return (
-        pltpu.VMEM((32, 8 * 128), jnp.bfloat16),
         pltpu.VMEM((9 * K, 8, 128), jnp.float32),
         pltpu.VMEM((8, 128, 128), jnp.float32),
         pltpu.VMEM((9 * K, 8, 128), jnp.float32),
@@ -154,12 +125,11 @@
 def first_kernel(meta, low, middle, high, out, tiles, *work):
     width = middle.shape[0] // 3
     fill(tiles, low, middle, high, 3 * width)
-    work[0][...] = selector()
     sub = lax.broadcasted_iota(jnp.int32, (8, 128), 0)
 
     def one(t, *work):
         own = tiles[4 * width + t + 2]
-        sums = pair_sums(tiles, meta, t * 8, own, False, *work)
+        sums = pair_sums(tiles, meta, t, own, False, *work)
         radius = own[6:7, :]
         gain = STEP_DT / (DENS * radius * radius * radius)
         fresh = own
@@ -172,8 +142,8 @@
 
     @pl.loop(0, (width - 4) // 2)
     def _(t):
-        one(2 * t, work[0], work[1], work[2])
-        one(2 * t + 1, work[0], work[3], work[4])
+        one(2 * t, work[0], work[1])
+        one(2 * t + 1, work[2], work[3])
 
 
 def second_kernel(
@@ -181,7 +151,6 @@
 ):
     width = middle.shape[0] // 3
     fill(tiles, low, middle, high, 3 * width)
-    work[0][...] = selector()
     sub = lax.broadcasted_iota(jnp.int32, (8, 128), 0)
     line = lax.broadcasted_iota(jnp.int32, (64, 128), 0)
     total[...] = jnp.zeros((8, 128), jnp.float32)
@@ -189,7 +158,7 @@
 
     def one(t, *work):
         own = tiles[4 * width + t + 1]
-        sums = pair_sums(tiles, meta, t * 8, own, True, *work)
+        sums = pair_sums(tiles, meta, t, own, True, *work)
         radius = own[6:7, :]
         mass = DENS * radius * radius * radius
         gain = STEP_DT / mass
@@ -223,8 +192,8 @@
 
     @pl.loop(0, NT // 2)
     def _(t):
-        one(2 * t, work[0], work[1], work[2])
-        one(2 * t + 1, work[0], work[3], work[4])
+        one(2 * t, work[0], work[1])
+        one(2 * t + 1, work[2], work[3])
 
     both = lax.dot_general(
         left[...], right[...], (((1,), (1,)), ((), ())), preferred_element_type=jnp.float32
@@ -303,7 +272,14 @@
         motion[c] = turned[48 + 8 * c : 56 + 8 * c, :]
 
 
-def pack_kernel(place, speed, radius, group, broken, lists, counts, out, to_left, to_right):
+def pack_kernel(*refs):
+    sources, (out, to_left, to_right, notes), held, done = refs[0:7], refs[7:11], refs[11:18], refs[18]
+    copies = [pltpu.make_async_copy(a, b, done.at[i]) for i, (a, b) in enumerate(zip(sources, held))]
+    for copy in copies:
+        copy.start()
+    for copy in copies:
+        copy.wait()
+    place, speed, radius, group, broken, lists, counts = held
     code = jnp.where(broken[...] == 0, group[...].astype(jnp.float32), -1.0)
     for t in range(NT):
         for axis in range(3):
@@ -311,13 +287,14 @@
             out[t, 3 + axis : 4 + axis, :] = speed[axis, t : t + 1, :]
         out[t, 6:7, :] = radius[t : t + 1, :]
         out[t, 7:8, :] = code[t : t + 1, :]
-    for ref, notes, tile, first in ((to_left, 2, 0, 0), (to_right, 0, 1, NT - 2)):
+    notes[...] = jnp.zeros((8, 128), jnp.float32)
+    for slot in range(K):
+        notes[slot : slot + 1, 0:NT] = lists[0, 0, slot].astype(jnp.float32)
+    notes[K : K + 1, 0:NT] = counts[...].astype(jnp.float32)
+    for ref, place, tile, first in ((to_left, 2, 0, 0), (to_right, 0, 1, NT - 2)):
         ref[tile] = out[first]
         ref[tile + 1] = out[first + 1]
-        ref[notes] = jnp.zeros((8, 128), jnp.float32)
-        for slot in range(K):
-            ref[notes, slot : slot + 1, 0:NT] = lists[slot].astype(jnp.float32)
-        ref[notes, K : K + 1, 0:NT] = counts[...].astype(jnp.float32)
+        ref[place] = notes[...]
 
 
 def shifted(value, axis, step, wrap):
@@ -337,8 +314,8 @@
         moved = lax.axis_index(axis) + step
         return (moved >= 0) & (moved < lax.axis_size(axis))
 
-    live = lax.broadcasted_iota(jnp.int32, lists.shape, 1) < counts
-    live = live & within("gx", shift) & within("gx", shift + along)
+    slot = lax.broadcasted_iota(jnp.int32, lists.shape, 0)
+    live = (slot < counts) & within("gx", shift) & within("gx", shift + along)
     live = live & within("gy", across - 1) & within("gz", up - 1)
     inside = live & (offset == 13)
     itself = inside & (spot == home)
@@ -346,35 +323,33 @@
     entry = entry + LIVE * live.astype(jnp.int32) + INSIDE * inside.astype(jnp.int32)
     entry = entry + ITSELF * itself.astype(jnp.int32)
     own = inside.astype(jnp.int32)
-    earlier = lax.broadcasted_iota(jnp.int32, (K, K), 0) < lax.broadcasted_iota(jnp.int32, (K, K), 1)
-    before = jnp.sum(jnp.where(earlier, own[:, :, None], 0), axis=1)
-    slot = lax.broadcasted_iota(jnp.int32, lists.shape, 1)
-    rank = jnp.where(inside, before, slot - before + jnp.sum(own, axis=1, keepdims=True))
-    to = lax.broadcasted_iota(jnp.int32, (1, 1, 8), 2)
-    return jnp.sum(jnp.where(rank[:, :, None] == to, entry[:, :, None], 0), axis=1).reshape(-1)
+    earlier = lax.broadcasted_iota(jnp.int32, (K, K, 1), 0) < lax.broadcasted_iota(jnp.int32, (K, K, 1), 1)
+    before = jnp.sum(jnp.where(earlier, own[:, None, :], 0), axis=0)
+    rank = jnp.where(inside, before, slot - before + jnp.sum(own, axis=0, keepdims=True))
+    to = lax.broadcasted_iota(jnp.int32, (1, K, 1), 1)
+    return jnp.sum(jnp.where(rank[:, None, :] == to, entry[:, None, :], 0), axis=0).reshape(-1)
 
 
 def shards(positions, velocities, radius, group, broken, cell, neighbours, counts):
-    lists = neighbours.reshape(NT, K)
-    listed = counts.reshape(NT, 1)
     tile = jax.ShapeDtypeStruct((NT, 8, 128), jnp.float32)
     edge = jax.ShapeDtypeStruct((3, 8, 128), jnp.float32)
-    own, to_left, to_right = pl.pallas_call(
-        pack_kernel,
-        out_shape=(tile, edge, edge),
-        in_specs=[VMEM] * 7,
-        out_specs=(VMEM, VMEM, VMEM),
-        compiler_params=SMALL,
-        name="pack",
-    )(
+    arguments = (
         positions.reshape(3, NT, 128),
         velocities.reshape(3, NT, 128),
         radius.reshape(NT, 128),
         group.reshape(NT, 128),
         broken.reshape(NT, 128),
-        lists.T.reshape(K, 1, NT),
+        jnp.transpose(neighbours, (0, 1, 4, 2, 3)),
         counts.reshape(1, NT),
     )
+    own, to_left, to_right, notes = pl.pallas_call(
+        pack_kernel,
+        out_shape=(tile, edge, edge, jax.ShapeDtypeStruct((8, 128), jnp.float32)),
+        in_specs=[pl.BlockSpec(memory_space=pltpu.HBM)] * 7,
+        out_specs=(VMEM,) * 4,
+        scratch_shapes=[pltpu.VMEM(a.shape, a.dtype) for a in arguments] + [pltpu.SemaphoreType.DMA((7,))],
+        name="pack",
+    )(*arguments)
     from_left = shifted(to_right, "gx", 1, True)
     from_right = shifted(to_left, "gx", -1, True)
     line = jnp.concatenate([from_left, own, from_right], axis=0)
@@ -389,15 +364,13 @@
         return low, middle, high
 
     low, middle, high = extended(line)
-    left_notes = from_left[0, 0:7, NT - 1].astype(jnp.int32)
-    right_notes = from_right[2, 0:7, 0].astype(jnp.int32)
-    all_lists = jnp.concatenate([left_notes[None, 0:K], lists, right_notes[None, 0:K]], axis=0)
-    all_counts = jnp.concatenate([left_notes[None, K:7], listed, right_notes[None, K:7]], axis=0)
-    spots = lax.broadcasted_iota(jnp.int32, (NT + 2, 1), 0)
+    listed = [from_left[0, 0 : K + 1, NT - 1 : NT], notes[0 : K + 1, 0:NT], from_right[2, 0 : K + 1, 0:1]]
+    listed = jnp.concatenate(listed, axis=1).astype(jnp.int32)
+    spots = lax.broadcasted_iota(jnp.int32, (1, NT + 2), 1)
     shift = jnp.where(spots == 0, -1, jnp.where(spots == NT + 1, 1, 0))
-    first_meta = list_entries(all_lists, all_counts, spots + 2, shift, width, 3)
-    spots = lax.broadcasted_iota(jnp.int32, (NT, 1), 0)
-    second_meta = list_entries(lists, listed, spots + 1, 0, width - 4, 1)
+    first_meta = list_entries(listed[0:K], listed[K:], spots + 2, shift, width, 3)
+    spots = lax.broadcasted_iota(jnp.int32, (1, NT), 1)
+    second_meta = list_entries(listed[0:K, 1 : NT + 1], listed[K:, 1 : NT + 1], spots + 1, 0, width - 4, 1)
 
     line = pl.pallas_call(
         first_kernel,

time: 106 us -> 101 us (0.953)
  local copies, waits for them, and re-layouts: 5.07 us -> 0.36 us
  waiting for transfers between devices: 11.5 us -> 14.3 us
  other arithmetic: 2.3 us -> 0.7 us
  Pallas kernels: 21.3 us -> 20 us
    ppermute x12, waiting for transfers between devices: 6.24 us -> 9.04 us  [shifted(): return lax.ppermute(value, axis, pairs)]
    unnamed x23 -> x12, local copies, waits for them, and re-layouts: 2.83 us -> 0.04 us
    pallas_call x1, Pallas kernels: 9.2 us -> 7.71 us  [shards(): pl.pallas_call(first_kernel, out_shape=jax.ShapeDtypeStruct((width - 4, 8...]
    pallas_call x1, Pallas kernels: 0.03 us -> 1.47 us  [shards(): pl.pallas_call(pack_kernel, out_shape=(tile, edge, edge, jax.ShapeDtypeSt...]
    concatenate x1 -> x0, other arithmetic: 1.37 us -> none  [shards(): jnp.concatenate([left_notes[None, K:7], listed, right_notes[None, K:7]],...]
    pallas_call x1, Pallas kernels: 10.4 us -> 9.12 us  [shards(): pl.pallas_call(second_kernel, out_shape=(block, block, jax.ShapeDtypeStru...]
  transfers between devices with their start and end apart: 13 -> 13, of which waited for: 6 -> 7; matrix products, arithmetic and copies ran while one was open for 3% -> 1% of each run, Pallas kernels for 0% -> 0%
where the time goes in v4:
time: 101 us
  starting transfers between devices  46.3 us (46%)
  Pallas kernels  20 us (20%)
  blocking collectives  18.1 us (18%)
  waiting for transfers between devices  14.3 us (14%)
    ppermute x12, starting transfers between devices, shifted(): return lax.ppermute(value, axis, pairs)  36.8 us
    all_to_all x1, blocking collectives, shards(): parts = lax.all_to_all(parts, ('gy', 'gz'), 0, 0, tiled=True)  18.1 us
    all_to_all x1, starting transfers between devices, shards(): energy = lax.all_to_all(energy, 'gx', 0, 0, tiled=True)  9.46 us
    pallas_call x1, Pallas kernels, shards(): pl.pallas_call(second_kernel, out_shape=(block, block, jax.ShapeDtypeStru...  9.12 us
    ppermute x12, waiting for transfers between devices, shifted(): return lax.ppermute(value, axis, pairs)  9.04 us
    pallas_call x1, Pallas kernels, shards(): pl.pallas_call(first_kernel, out_shape=jax.ShapeDtypeStruct((width - 4, 8...  7.71 us
    all_to_all x1, waiting for transfers between devices, shards(): energy = lax.all_to_all(energy, 'gx', 0, 0, tiled=True)  5.27 us
  transfers between devices with their start and end apart: 13, of which 7 were waited for; matrix products, arithmetic and copies ran while one was open for 1% of the time, Pallas kernels for 0%

profile of v4, /device:TPU:1, one launch (start us, length us, event | category | flops | bytes accessed | tf_op | source)
XLA Modules:
  0.0 100.6 jit_solution(7855907021136264104)
XLA Ops:
  0.6 1.5 %pack.1 = (f32[8,8,128]{2,1,0:T(8,128)}, f32[3,8,128]{2,1,0:T(8,128)}, f32[3,8,128]{2,1,0:T(8,128)}, f32[8,128]{1,0:T(8,128)}) custom-call(f32[3,8,128]{2,1,0:T(8,128)} %bitcast.29, f32[3,8,128]{2,1,0:T(8,128)} %bitcast.30, f32[8,128]{1,0:T(8,128)} %bitcast.31, s32[8,128]{1,0:T(8,128)} %bitcast.32, s32[8,128]{1,0:T(8,128)} %bitcast.33, ...), custom_call_target="tpu_custom_call" | custom-call | tf_op jit(solution)/shard_map/pack/pallas_call | solution.py:345
  2.1 4.4 %collective-permute-start = (f32[3,8,128]{2,1,0:T(8,128)}, f32[3,8,128]{2,1,0:T(8,128)S(1)}, u32[]{:S(2)}, u32[]{:S(2)}) collective-permute-start(f32[3,8,128]{2,1,0:T(8,128)} %get-tuple-element.16), channel_id=1, source_target_pairs={{0,32},{32,64},{64,96},{96,128},{128,160},{160,192},{192,224},{224... | collective-permute-start | bytes 36872 | tf_op jit(solution)/shard_map/ppermute | solution.py:303
  6.5 9.5 %collective-permute-start.1 = (f32[3,8,128]{2,1,0:T(8,128)}, f32[3,8,128]{2,1,0:T(8,128)S(1)}, u32[]{:S(2)}, u32[]{:S(2)}) collective-permute-start(f32[3,8,128]{2,1,0:T(8,128)} %get-tuple-element.18), channel_id=1, source_target_pairs={{0,480},{32,0},{64,32},{96,64},{128,96},{160,128},{192,160},{224,1... | collective-permute-start | bytes 36872 | tf_op jit(solution)/shard_map/ppermute | solution.py:303
  16.1 0.0 copy-start.2
  16.1 0.0 copy-start.1
  16.1 0.0 collective-permute-done
  16.1 0.1 slice_bitcast_fusion.1
  16.2 0.9 collective-permute-done.1
  17.0 0.0 copy-done.2
  17.0 0.1 maximum_convert_fusion
  17.1 0.1 slice_bitcast_fusion.3
  17.2 0.0 copy-done.1
  17.2 1.3 %collective-permute-start.3 = (f32[14,8,128]{2,1,0:T(8,128)S(1)}, f32[14,8,128]{2,1,0:T(8,128)S(1)}, u32[]{:S(2)}, u32[]{:S(2)}) collective-permute-start(f32[14,8,128]{2,1,0:T(8,128)S(1)} %constant_dynamic-update-slice_fusion), channel_id=1, source_target_pairs={{8,0},{16,8},{24,16},{9,1},{17,9},{25,17},{10,2},{18,10},{26,18},{... | collective-permute-start | bytes 172040 | tf_op jit(solution)/shard_map/ppermute | solution.py:303
  18.5 4.0 %collective-permute-start.2 = (f32[14,8,128]{2,1,0:T(8,128)S(1)}, f32[14,8,128]{2,1,0:T(8,128)S(1)}, u32[]{:S(2)}, u32[]{:S(2)}) collective-permute-start(f32[14,8,128]{2,1,0:T(8,128)S(1)} %constant_dynamic-update-slice_fusion), channel_id=1, source_target_pairs={{0,8},{8,16},{16,24},{1,9},{9,17},{17,25},{2,10},{10,18},{18,26},{... | collective-permute-start | bytes 172040 | tf_op jit(solution)/shard_map/ppermute | solution.py:303
  22.5 0.1 convert_reduce_fusion
  22.6 0.1 select_reduce_fusion.1
  22.7 0.1 reshape.105.meta
  22.8 1.0 collective-permute-done.2
  23.8 0.0 collective-permute-done.3
  23.8 2.7 %collective-permute-start.5 = (f32[42,8,128]{2,1,0:T(8,128)S(1)}, f32[42,8,128]{2,1,0:T(8,128)S(1)}, u32[]{:S(2)}, u32[]{:S(2)}) collective-permute-start(f32[42,8,128]{2,1,0:T(8,128)S(1)} %constant_dynamic-update-slice_fusion.3.middle), channel_id=1, source_target_pairs={{0,7},{1,0},{2,1},{3,2},{4,3},{5,4},{6,5},{7,6},{8,15},{9,8},{10,9... | collective-permute-start | bytes 516104 | tf_op jit(solution)/shard_map/ppermute | solution.py:303
  26.5 1.2 %collective-permute-start.4 = (f32[42,8,128]{2,1,0:T(8,128)S(1)}, f32[42,8,128]{2,1,0:T(8,128)S(1)}, u32[]{:S(2)}, u32[]{:S(2)}) collective-permute-start(f32[42,8,128]{2,1,0:T(8,128)S(1)} %constant_dynamic-update-slice_fusion.3.middle), channel_id=1, source_target_pairs={{0,1},{1,2},{2,3},{3,4},{4,5},{5,6},{6,7},{7,0},{8,9},{9,10},{10,1... | collective-permute-start | bytes 516104 | tf_op jit(solution)/shard_map/ppermute | solution.py:303
  27.7 0.1 convert_reduce_fusion.1
  27.8 3.2 %collective-permute-done.5.high = f32[42,8,128]{2,1,0:T(8,128)S(1)} collective-permute-done((f32[42,8,128]{2,1,0:T(8,128)S(1)}, f32[42,8,128]{2,1,0:T(8,128)S(1)}, u32[]{:S(2)}, u32[]{:S(2)}) %collective-permute-start.5) | collective-permute-done | bytes 172064 | tf_op jit(solution)/shard_map/ppermute | solution.py:303
  31.0 0.0 collective-permute-done.4.low
  31.0 7.7 %first_step.1 = f32[10,8,128]{2,1,0:T(8,128)S(1)} custom-call(s32[60]{0:T(128)S(1)} %reshape.105.meta, f32[42,8,128]{2,1,0:T(8,128)S(1)} %collective-permute-done.4.low, f32[42,8,128]{2,1,0:T(8,128)S(1)} %constant_dynamic-update-slice_fusion.3.middle, f32[42,8,128]{2,1,0:T(8,128)S(1)} %collective-permute-done.5.high), custom_call_target="tpu_custom_call" | custom-call | tf_op jit(solution)/shard_map/first_step/pallas_call | solution.py:375
  38.8 1.3 %collective-permute-start.7 = (f32[10,8,128]{2,1,0:T(8,128)S(1)}, f32[10,8,128]{2,1,0:T(8,128)S(1)}, u32[]{:S(2)}, u32[]{:S(2)}) collective-permute-start(f32[10,8,128]{2,1,0:T(8,128)S(1)} %first_step.1), channel_id=1, source_target_pairs={{8,0},{16,8},{24,16},{9,1},{17,9},{25,17},{10,2},{18,10},{26,18},{... | collective-permute-start | bytes 122888 | tf_op jit(solution)/shard_map/ppermute | solution.py:303
  40.1 4.6 %collective-permute-start.6 = (f32[10,8,128]{2,1,0:T(8,128)S(1)}, f32[10,8,128]{2,1,0:T(8,128)S(1)}, u32[]{:S(2)}, u32[]{:S(2)}) collective-permute-start(f32[10,8,128]{2,1,0:T(8,128)S(1)} %first_step.1), channel_id=1, source_target_pairs={{0,8},{8,16},{16,24},{1,9},{9,17},{17,25},{2,10},{10,18},{18,26},{... | collective-permute-start | bytes 122888 | tf_op jit(solution)/shard_map/ppermute | solution.py:303
  44.7 0.1 select_reduce_fusion.3
  44.8 0.0 collective-permute-done.7
  44.8 1.0 collective-permute-done.6
  45.8 2.6 %collective-permute-start.9 = (f32[30,8,128]{2,1,0:T(8,128)S(1)}, f32[30,8,128]{2,1,0:T(8,128)S(1)}, u32[]{:S(2)}, u32[]{:S(2)}) collective-permute-start(f32[30,8,128]{2,1,0:T(8,128)S(1)} %pad_maximum_fusion.middle), channel_id=1, source_target_pairs={{0,7},{1,0},{2,1},{3,2},{4,3},{5,4},{6,5},{7,6},{8,15},{9,8},{10,9... | collective-permute-start | bytes 368648 | tf_op jit(solution)/shard_map/ppermute | solution.py:303
  48.4 0.0 collective-permute-start.8
  48.4 0.1 add_select_fusion.13
  48.5 0.0 copy-start
  48.5 0.1 reshape.103.meta
  48.6 2.1 %collective-permute-done.9.high = f32[30,8,128]{2,1,0:T(8,128)S(1)} collective-permute-done((f32[30,8,128]{2,1,0:T(8,128)S(1)}, f32[30,8,128]{2,1,0:T(8,128)S(1)}, u32[]{:S(2)}, u32[]{:S(2)}) %collective-permute-start.9) | collective-permute-done | bytes 122912 | tf_op jit(solution)/shard_map/ppermute | solution.py:303
  50.7 0.0 collective-permute-done.8.low
  50.7 9.1 %second_step.1 = (f32[3,8,128]{2,1,0:T(8,128)}, f32[3,8,128]{2,1,0:T(8,128)}, f32[64,128]{1,0:T(8,128)S(1)}, f32[16,8,128]{2,1,0:T(8,128)}) custom-call(s32[48]{0:T(128)S(1)} %reshape.103.meta, s32[8,128]{1,0:T(8,128)S(1)} %bitcast.28, f32[30,8,128]{2,1,0:T(8,128)S(1)} %collective-permute-done.8.low, f32[30,8,128]{2,1,0:T(8,128)S(1)} %pad_maximum_fusion.middle, ...), custom_call_target="tpu_custom_call" | custom-call | tf_op jit(solution)/shard_map/second_step/pallas_call | solution.py:391
  59.8 9.5 %all-to-all-start = ((f32[16,8,128]{2,1,0:T(8,128)}), f32[16,8,128]{2,1,0:T(8,128)S(1)}, u32[]{:S(2)}, u32[]{:S(2)}) async-start(f32[16,8,128]{2,1,0:T(8,128)} %get-tuple-element.23), calls=%async_computation | async-start | bytes 131072 | tf_op jit(solution)/shard_map/all_to_all | solution.py:411
  69.3 1.3 %collective-permute-start.11 = (f32[64,128]{1,0:T(8,128)S(1)}, f32[64,128]{1,0:T(8,128)S(1)}, u32[]{:S(2)}, u32[]{:S(2)}) collective-permute-start(f32[64,128]{1,0:T(8,128)S(1)} %get-tuple-element.22.own), channel_id=1, source_target_pairs={{32,0},{64,32},{96,64},{128,96},{160,128},{192,160},{224,192},{256... | collective-permute-start | bytes 98312 | tf_op jit(solution)/shard_map/ppermute | solution.py:303
  70.6 4.0 %collective-permute-start.10 = (f32[64,128]{1,0:T(8,128)S(1)}, f32[64,128]{1,0:T(8,128)S(1)}, u32[]{:S(2)}, u32[]{:S(2)}) collective-permute-start(f32[64,128]{1,0:T(8,128)S(1)} %get-tuple-element.22.own), channel_id=1, source_target_pairs={{0,32},{32,64},{64,96},{96,128},{128,160},{160,192},{192,224},{224... | collective-permute-start | bytes 98312 | tf_op jit(solution)/shard_map/ppermute | solution.py:303
  74.6 0.1 pad_add_fusion.coords
  74.6 0.0 collective-permute-done.11.after
  74.6 0.9 collective-permute-done.10.before
  75.6 5.3 %all-to-all-done.energy = f32[16,8,128]{2,1,0:T(8,128)S(1)} async-done(((f32[16,8,128]{2,1,0:T(8,128)}), f32[16,8,128]{2,1,0:T(8,128)S(1)}, u32[]{:S(2)}, u32[]{:S(2)}) %all-to-all-start) | async-done | bytes 65568 | tf_op jit(solution)/shard_map/all_to_all | solution.py:411
  80.8 0.9 planes.1
  81.8 18.1 %all_to_all.10.parts = f32[32,8,128]{2,1,0:T(8,128)S(1)} all-to-all(f32[32,8,128]{2,1,0:T(8,128)S(1)} %planes.1), channel_id=1, replica_groups=mesh['gx'=16,'gy'=4,'gz'=8] {'gy','gz'}, dimensions={0} | all-to-all | bytes 262144 | tf_op jit(solution)/shard_map/all_to_all | solution.py:424
  99.9 0.8 lines.1
  (21 shorter events, 0.1 us)
Async XLA Ops:
  2.1 14.0 %collective-permute-start = (f32[3,8,128]{2,1,0:T(8,128)}, f32[3,8,128]{2,1,0:T(8,128)S(1)}, u32[]{:S(2)}, u32[]{:S(2)}) collective-permute-start(f32[3,8,128]{2,1,0:T(8,128)} %get-tuple-element.16), channel_id=1, source_target_pairs={{0,32},{32,64},{64,96},{96,128},{128,160},{160,192},{192,224},{224... | collective-permute-start | bytes 36872 | tf_op jit(solution)/shard_map/ppermute | solution.py:303
  6.5 10.5 %collective-permute-start.1 = (f32[3,8,128]{2,1,0:T(8,128)}, f32[3,8,128]{2,1,0:T(8,128)S(1)}, u32[]{:S(2)}, u32[]{:S(2)}) collective-permute-start(f32[3,8,128]{2,1,0:T(8,128)} %get-tuple-element.18), channel_id=1, source_target_pairs={{0,480},{32,0},{64,32},{96,64},{128,96},{160,128},{192,160},{224,1... | collective-permute-start | bytes 36872 | tf_op jit(solution)/shard_map/ppermute | solution.py:303
  16.1 1.0 copy-start.2
  16.1 1.1 %copy-start.1 = (f32[8,8,128]{2,1,0:T(8,128)S(1)}, f32[8,8,128]{2,1,0:T(8,128)}, u32[]{:S(2)}) copy-start(f32[8,8,128]{2,1,0:T(8,128)} %get-tuple-element.19) | copy-start | bytes 98308
  17.2 6.6 %collective-permute-start.3 = (f32[14,8,128]{2,1,0:T(8,128)S(1)}, f32[14,8,128]{2,1,0:T(8,128)S(1)}, u32[]{:S(2)}, u32[]{:S(2)}) collective-permute-start(f32[14,8,128]{2,1,0:T(8,128)S(1)} %constant_dynamic-update-slice_fusion), channel_id=1, source_target_pairs={{8,0},{16,8},{24,16},{9,1},{17,9},{25,17},{10,2},{18,10},{26,18},{... | collective-permute-start | bytes 172040 | tf_op jit(solution)/shard_map/ppermute | solution.py:303
  18.5 5.2 %collective-permute-start.2 = (f32[14,8,128]{2,1,0:T(8,128)S(1)}, f32[14,8,128]{2,1,0:T(8,128)S(1)}, u32[]{:S(2)}, u32[]{:S(2)}) collective-permute-start(f32[14,8,128]{2,1,0:T(8,128)S(1)} %constant_dynamic-update-slice_fusion), channel_id=1, source_target_pairs={{0,8},{8,16},{16,24},{1,9},{9,17},{17,25},{2,10},{10,18},{18,26},{... | collective-permute-start | bytes 172040 | tf_op jit(solution)/shard_map/ppermute | solution.py:303
  23.8 7.2 %collective-permute-start.5 = (f32[42,8,128]{2,1,0:T(8,128)S(1)}, f32[42,8,128]{2,1,0:T(8,128)S(1)}, u32[]{:S(2)}, u32[]{:S(2)}) collective-permute-start(f32[42,8,128]{2,1,0:T(8,128)S(1)} %constant_dynamic-update-slice_fusion.3.middle), channel_id=1, source_target_pairs={{0,7},{1,0},{2,1},{3,2},{4,3},{5,4},{6,5},{7,6},{8,15},{9,8},{10,9... | collective-permute-start | bytes 516104 | tf_op jit(solution)/shard_map/ppermute | solution.py:303
  26.5 4.6 %collective-permute-start.4 = (f32[42,8,128]{2,1,0:T(8,128)S(1)}, f32[42,8,128]{2,1,0:T(8,128)S(1)}, u32[]{:S(2)}, u32[]{:S(2)}) collective-permute-start(f32[42,8,128]{2,1,0:T(8,128)S(1)} %constant_dynamic-update-slice_fusion.3.middle), channel_id=1, source_target_pairs={{0,1},{1,2},{2,3},{3,4},{4,5},{5,6},{6,7},{7,0},{8,9},{9,10},{10,1... | collective-permute-start | bytes 516104 | tf_op jit(solution)/shard_map/ppermute | solution.py:303
  38.8 6.0 %collective-permute-start.7 = (f32[10,8,128]{2,1,0:T(8,128)S(1)}, f32[10,8,128]{2,1,0:T(8,128)S(1)}, u32[]{:S(2)}, u32[]{:S(2)}) collective-permute-start(f32[10,8,128]{2,1,0:T(8,128)S(1)} %first_step.1), channel_id=1, source_target_pairs={{8,0},{16,8},{24,16},{9,1},{17,9},{25,17},{10,2},{18,10},{26,18},{... | collective-permute-start | bytes 122888 | tf_op jit(solution)/shard_map/ppermute | solution.py:303
  40.1 5.7 %collective-permute-start.6 = (f32[10,8,128]{2,1,0:T(8,128)S(1)}, f32[10,8,128]{2,1,0:T(8,128)S(1)}, u32[]{:S(2)}, u32[]{:S(2)}) collective-permute-start(f32[10,8,128]{2,1,0:T(8,128)S(1)} %first_step.1), channel_id=1, source_target_pairs={{0,8},{8,16},{16,24},{1,9},{9,17},{17,25},{2,10},{10,18},{18,26},{... | collective-permute-start | bytes 122888 | tf_op jit(solution)/shard_map/ppermute | solution.py:303
  45.8 4.9 %collective-permute-start.9 = (f32[30,8,128]{2,1,0:T(8,128)S(1)}, f32[30,8,128]{2,1,0:T(8,128)S(1)}, u32[]{:S(2)}, u32[]{:S(2)}) collective-permute-start(f32[30,8,128]{2,1,0:T(8,128)S(1)} %pad_maximum_fusion.middle), channel_id=1, source_target_pairs={{0,7},{1,0},{2,1},{3,2},{4,3},{5,4},{6,5},{7,6},{8,15},{9,8},{10,9... | collective-permute-start | bytes 368648 | tf_op jit(solution)/shard_map/ppermute | solution.py:303
  48.4 2.3 %collective-permute-start.8 = (f32[30,8,128]{2,1,0:T(8,128)S(1)}, f32[30,8,128]{2,1,0:T(8,128)S(1)}, u32[]{:S(2)}, u32[]{:S(2)}) collective-permute-start(f32[30,8,128]{2,1,0:T(8,128)S(1)} %pad_maximum_fusion.middle), channel_id=1, source_target_pairs={{0,1},{1,2},{2,3},{3,4},{4,5},{5,6},{6,7},{7,0},{8,9},{9,10},{10,1... | collective-permute-start | bytes 368648 | tf_op jit(solution)/shard_map/ppermute | solution.py:303
  48.5 2.2 %copy-start = (s32[1,1,1,1024]{3,2,1,0:T(1,128)S(1)}, s32[1,1,1,1024]{3,2,1,0:T(1,128)}, u32[]{:S(2)}) copy-start(s32[1,1,1,1024]{3,2,1,0:T(1,128)} %param.13) | copy-start | bytes 12292
  59.8 21.0 %all-to-all-start = ((f32[16,8,128]{2,1,0:T(8,128)}), f32[16,8,128]{2,1,0:T(8,128)S(1)}, u32[]{:S(2)}, u32[]{:S(2)}) async-start(f32[16,8,128]{2,1,0:T(8,128)} %get-tuple-element.23), calls=%async_computation | async-start | bytes 131072 | tf_op jit(solution)/shard_map/all_to_all | solution.py:411
  69.3 5.4 %collective-permute-start.11 = (f32[64,128]{1,0:T(8,128)S(1)}, f32[64,128]{1,0:T(8,128)S(1)}, u32[]{:S(2)}, u32[]{:S(2)}) collective-permute-start(f32[64,128]{1,0:T(8,128)S(1)} %get-tuple-element.22.own), channel_id=1, source_target_pairs={{32,0},{64,32},{96,64},{128,96},{160,128},{192,160},{224,192},{256... | collective-permute-start | bytes 98312 | tf_op jit(solution)/shard_map/ppermute | solution.py:303
  70.6 5.0 %collective-permute-start.10 = (f32[64,128]{1,0:T(8,128)S(1)}, f32[64,128]{1,0:T(8,128)S(1)}, u32[]{:S(2)}, u32[]{:S(2)}) collective-permute-start(f32[64,128]{1,0:T(8,128)S(1)} %get-tuple-element.22.own), channel_id=1, source_target_pairs={{0,32},{32,64},{64,96},{96,128},{128,160},{160,192},{192,224},{224... | collective-permute-start | bytes 98312 | tf_op jit(solution)/shard_map/ppermute | solution.py:303

commit v5 on v4

--- a/solution.py
+++ b/solution.py
@@ -128,7 +128,7 @@
     sub = lax.broadcasted_iota(jnp.int32, (8, 128), 0)
 
     def one(t, *work):
-        own = tiles[4 * width + t + 2]
+        own = tiles[4 * width + t + 1]
         sums = pair_sums(tiles, meta, t, own, False, *work)
         radius = own[6:7, :]
         gain = STEP_DT / (DENS * radius * radius * radius)
@@ -140,21 +140,19 @@
             fresh = jnp.where(sub == 3 + axis, speed, fresh)
         out[t] = fresh
 
-    @pl.loop(0, (width - 4) // 2)
+    @pl.loop(0, (width - 2) // 2)
     def _(t):
         one(2 * t, work[0], work[1])
         one(2 * t + 1, work[2], work[3])
 
 
 def second_kernel(
-    meta, cell, low, middle, high, place_out, speed_out, grid_out, energy_out, tiles, left, right, total, *work
+    meta, low, middle, high, place_out, speed_out, values_out, energy_out, tiles, total, *work
 ):
     width = middle.shape[0] // 3
     fill(tiles, low, middle, high, 3 * width)
     sub = lax.broadcasted_iota(jnp.int32, (8, 128), 0)
-    line = lax.broadcasted_iota(jnp.int32, (64, 128), 0)
     total[...] = jnp.zeros((8, 128), jnp.float32)
-    right[...] = jnp.zeros(right.shape, jnp.bfloat16)
 
     def one(t, *work):
         own = tiles[4 * width + t + 1]
@@ -177,40 +175,44 @@
         bond = 0.5 * KB * sums[10]
         added = jnp.where(sub == 0, kinetic, jnp.where(sub == 1, contact, jnp.where(sub == 2, bond, 0.0)))
         total[...] = total[...] + added
-        where = cell[this, :]
-        span = pl.ds(pl.multiple_of(128 * t, 128), 128)
+        for c in range(COMPS):
+            values_out[t, c : c + 1, :] = values[c]
+
+    @pl.loop(0, NT // 2)
+    def _(t):
+        one(2 * t, work[0], work[1])
+        one(2 * t + 1, work[2], work[3])
+
+    for i in range(energy_out.shape[0]):
+        energy_out[i] = total[...]
+
+
+def deposit_kernel(values, cell, grid, left, right):
+    sub = lax.broadcasted_iota(jnp.int32, (8, 128), 0)
+    line = lax.broadcasted_iota(jnp.int32, (64, 128), 0)
+    right[...] = jnp.zeros(right.shape, jnp.bfloat16)
+    for t in range(NT):
+        where = cell[t : t + 1, :]
+        span = slice(128 * t, 128 * t + 128)
         in_plane = sub == lax.shift_right_logical(where, 6)
         for c in range(0, COMPS, 2):
-            pair = jnp.concatenate(
-                [jnp.where(in_plane, values[c], 0.0), jnp.where(in_plane, values[c + 1], 0.0)], axis=0
-            )
+            pair = [jnp.where(in_plane, values[t, c + i : c + i + 1, :], 0.0) for i in range(2)]
+            pair = jnp.concatenate(pair, axis=0)
             coarse = pair.astype(jnp.bfloat16)
             fine = (pair - coarse.astype(jnp.float32)).astype(jnp.bfloat16)
             right[8 * c : 8 * c + 16, span] = coarse
             right[128 + 8 * c : 128 + 8 * c + 16, span] = fine
         left[:, span] = jnp.where(line == lax.bitwise_and(where, 63), 1.0, 0.0).astype(jnp.bfloat16)
-
-    @pl.loop(0, NT // 2)
-    def _(t):
-        one(2 * t, work[0], work[1])
-        one(2 * t + 1, work[2], work[3])
-
     both = lax.dot_general(
         left[...], right[...], (((1,), (1,)), ((), ())), preferred_element_type=jnp.float32
     )
     scale = float(CX * CY * CZ) / float(NT * 128)
-    grid_out[...] = (both[:, 0:128] + both[:, 128:256]) * scale
-    for i in range(energy_out.shape[0]):
-        energy_out[i] = total[...]
-
-
-def plane_kernel(coords, own, before, after, energy, out):
+    grid[...] = (both[:, 0:128] + both[:, 128:256]) * scale
+
+
+def plane_kernel(coords, own, before, after, out):
     lane = lax.broadcasted_iota(jnp.int32, (8, 128), 1)
     inner = lax.bitwise_and(lane, 7)
-    sums = energy[0]
-    for i in range(1, energy.shape[0]):
-        sums = sums + energy[i]
-    sums = jnp.where(lane == 8 * COMPS, jnp.sum(sums, axis=1, keepdims=True), 0.0)
     planes = []
     for y in range(CY):
         block = slice(8 * y, 8 * y + 8)
@@ -225,10 +227,10 @@
         planes.append(smooth)
     rows = out.shape[0]
     for j in range(rows):
-        out[j] = sums
+        out[j] = jnp.zeros((8, 128), jnp.float32)
     start = coords[1] * CY
     for r in range(-HW, CY + HW):
-        mixed = sums
+        mixed = jnp.zeros((8, 128), jnp.float32)
         for y in range(CY):
             if abs(r - y) <= HW:
                 mixed = mixed + GAUSS[abs(r - y)] * planes[y]
@@ -236,6 +238,16 @@
         @pl.when(jnp.logical_and(start + r >= 0, start + r < rows))
         def _():
             out[start + r] = mixed
+
+
+def energy_kernel(parts, energy, out):
+    lane = lax.broadcasted_iota(jnp.int32, (8, 128), 1)
+    sums = energy[0]
+    for i in range(1, energy.shape[0]):
+        sums = sums + energy[i]
+    sums = jnp.where(lane == 8 * COMPS, jnp.sum(sums, axis=1, keepdims=True), 0.0)
+    for j in range(out.shape[0]):
+        out[j] = parts[j] + sums
 
 
 def line_kernel(parts, stress, motion, energies):
@@ -289,12 +301,23 @@
         out[t, 7:8, :] = code[t : t + 1, :]
     notes[...] = jnp.zeros((8, 128), jnp.float32)
     for slot in range(K):
-        notes[slot : slot + 1, 0:NT] = lists[0, 0, slot].astype(jnp.float32)
-    notes[K : K + 1, 0:NT] = counts[...].astype(jnp.float32)
-    for ref, place, tile, first in ((to_left, 2, 0, 0), (to_right, 0, 1, NT - 2)):
-        ref[tile] = out[first]
-        ref[tile + 1] = out[first + 1]
-        ref[place] = notes[...]
+        notes[slot : slot + 1, 1 : NT + 1] = lists[0, 0, slot].astype(jnp.float32)
+    notes[K : K + 1, 1 : NT + 1] = counts[...].astype(jnp.float32)
+    for ref, first in ((to_left, 0), (to_right, NT - 2)):
+        ref[0] = out[first]
+        ref[1] = out[first + 1]
+        ref[2] = notes[...]
+
+
+def join_kernel(left, own, right, mine, line, notes):
+    for i in range(2):
+        line[i] = left[i]
+        line[NT + 2 + i] = right[i]
+    for t in range(NT):
+        line[2 + t] = own[t]
+    lane = lax.broadcasted_iota(jnp.int32, (8, 128), 1)
+    edges = jnp.where(lane == 0, pltpu.roll(left[2], 128 - NT, 1), pltpu.roll(right[2], NT, 1))
+    notes[...] = jnp.where(jnp.logical_and(lane >= 1, lane <= NT), mine[...], edges)
 
 
 def shifted(value, axis, step, wrap):
@@ -352,8 +375,18 @@
     )(*arguments)
     from_left = shifted(to_right, "gx", 1, True)
     from_right = shifted(to_left, "gx", -1, True)
-    line = jnp.concatenate([from_left, own, from_right], axis=0)
-    width = NT + 6
+    width = NT + 4
+    line, listed = pl.pallas_call(
+        join_kernel,
+        out_shape=(
+            jax.ShapeDtypeStruct((width, 8, 128), jnp.float32),
+            jax.ShapeDtypeStruct((8, 128), jnp.float32),
+        ),
+        in_specs=[VMEM] * 4,
+        out_specs=(VMEM,) * 2,
+        compiler_params=SMALL,
+        name="join",
+    )(from_left, own, from_right, notes)
 
     def extended(tiles):
         up = shifted(tiles, "gy", 1, False)
@@ -364,17 +397,16 @@
         return low, middle, high
 
     low, middle, high = extended(line)
-    listed = [from_left[0, 0 : K + 1, NT - 1 : NT], notes[0 : K + 1, 0:NT], from_right[2, 0 : K + 1, 0:1]]
-    listed = jnp.concatenate(listed, axis=1).astype(jnp.int32)
+    listed = listed[0 : K + 1, 0 : NT + 2].astype(jnp.int32)
     spots = lax.broadcasted_iota(jnp.int32, (1, NT + 2), 1)
     shift = jnp.where(spots == 0, -1, jnp.where(spots == NT + 1, 1, 0))
-    first_meta = list_entries(listed[0:K], listed[K:], spots + 2, shift, width, 3)
+    first_meta = list_entries(listed[0:K], listed[K:], spots + 1, shift, width, 2)
     spots = lax.broadcasted_iota(jnp.int32, (1, NT), 1)
-    second_meta = list_entries(listed[0:K, 1 : NT + 1], listed[K:, 1 : NT + 1], spots + 1, 0, width - 4, 1)
+    second_meta = list_entries(listed[0:K, 1 : NT + 1], listed[K:, 1 : NT + 1], spots + 1, 0, width - 2, 1)
 
     line = pl.pallas_call(
         first_kernel,
-        out_shape=jax.ShapeDtypeStruct((width - 4, 8, 128), jnp.float32),
+        out_shape=jax.ShapeDtypeStruct((width - 2, 8, 128), jnp.float32),
         in_specs=[SMEM] + [VMEM] * 3,
         out_specs=VMEM,
         scratch_shapes=[
@@ -385,30 +417,40 @@
         name="first_step",
     )(first_meta, low, middle, high)
     low, middle, high = extended(line)
-    width = width - 4
+    width = width - 2
     peers = lax.axis_size("gx")
     block = jax.ShapeDtypeStruct((3, NT, 128), jnp.float32)
-    places, speeds, grid, energy = pl.pallas_call(
+    places, speeds, values, energy = pl.pallas_call(
         second_kernel,
         out_shape=(
             block,
             block,
-            jax.ShapeDtypeStruct((64, 128), jnp.float32),
+            jax.ShapeDtypeStruct((NT, 16, 128), jnp.float32),
             jax.ShapeDtypeStruct((peers, 8, 128), jnp.float32),
         ),
-        in_specs=[SMEM] + [VMEM] * 4,
+        in_specs=[SMEM] + [VMEM] * 3,
         out_specs=(VMEM,) * 4,
         scratch_shapes=[
             pltpu.VMEM((9 * width, 8, 128), jnp.float32),
-            pltpu.VMEM((64, NT * 128), jnp.bfloat16),
-            pltpu.VMEM((256, NT * 128), jnp.bfloat16),
             pltpu.VMEM((8, 128), jnp.float32),
             *work_space(),
         ],
         compiler_params=LARGE,
         name="second_step",
-    )(second_meta, cell.reshape(NT, 128), low, middle, high)
+    )(second_meta, low, middle, high)
     energy = lax.all_to_all(energy, "gx", 0, 0, tiled=True)
+    grid = pl.pallas_call(
+        deposit_kernel,
+        out_shape=jax.ShapeDtypeStruct((64, 128), jnp.float32),
+        in_specs=[VMEM] * 2,
+        out_specs=VMEM,
+        scratch_shapes=[
+            pltpu.VMEM((64, NT * 128), jnp.bfloat16),
+            pltpu.VMEM((256, NT * 128), jnp.bfloat16),
+        ],
+        compiler_params=SMALL,
+        name="deposit",
+    )(values, cell.reshape(NT, 128))
     before = shifted(grid, "gx", 1, False)
     after = shifted(grid, "gx", -1, False)
     coords = jnp.stack([lax.axis_index(a) for a in ("gx", "gy", "gz")])
@@ -416,11 +458,19 @@
     parts = pl.pallas_call(
         plane_kernel,
         out_shape=jax.ShapeDtypeStruct((rows, 8, 128), jnp.float32),
-        in_specs=[SMEM] + [VMEM] * 4,
+        in_specs=[SMEM] + [VMEM] * 3,
         out_specs=VMEM,
         compiler_params=SMALL,
         name="planes",
-    )(coords, grid, before, after, energy)
+    )(coords, grid, before, after)
+    parts = pl.pallas_call(
+        energy_kernel,
+        out_shape=jax.ShapeDtypeStruct((rows, 8, 128), jnp.float32),
+        in_specs=[VMEM] * 2,
+        out_specs=VMEM,
+        compiler_params=SMALL,
+        name="energies",
+    )(parts, energy)
     parts = lax.all_to_all(parts, ("gy", "gz"), 0, 0, tiled=True)
     stress, motion, energies = pl.pallas_call(
         line_kernel,

time: 101 us -> 100 us (0.990)
  waiting for transfers between devices: 14.3 us -> 12.8 us
    all_to_all x1, waiting for transfers between devices: 5.27 us -> 4.01 us  [shards(): energy = lax.all_to_all(energy, 'gx', 0, 0, tiled=True)]
    pallas_call x1 -> x4, Pallas kernels: 7.71 us -> 8.22 us  [the longest x1 7.72 us: shards(): pl.pallas_call(first_kernel, out_shape=jax.ShapeDtypeStruct((width - 2, 8...]
  transfers between devices with their start and end apart: 13 -> 13, of which waited for: 7 -> 7; matrix products, arithmetic and copies ran while one was open for 1% -> 1% of each run, Pallas kernels for 0% -> 1%
where the time goes in v5:
time: 100 us; the launch traced here: 99.5 us
  starting transfers between devices  46.4 us (46%)
  Pallas kernels  20.4 us (20%)
  blocking collectives  18.1 us (18%)
  waiting for transfers between devices  12.8 us (13%)
    ppermute x12, starting transfers between devices, shifted(): return lax.ppermute(value, axis, pairs)  36.8 us
    all_to_all x1, blocking collectives, shards(): parts = lax.all_to_all(parts, ('gy', 'gz'), 0, 0, tiled=True)  18.1 us
    all_to_all x1, starting transfers between devices, shards(): energy = lax.all_to_all(energy, 'gx', 0, 0, tiled=True)  9.61 us
    pallas_call x1, Pallas kernels, shards(): pl.pallas_call(second_kernel, out_shape=(block, block, jax.ShapeDtypeStru...  8.98 us
    ppermute x12, waiting for transfers between devices, shifted(): return lax.ppermute(value, axis, pairs)  8.79 us
    pallas_call x1, Pallas kernels, shards(): pl.pallas_call(first_kernel, out_shape=jax.ShapeDtypeStruct((width - 2, 8...  7.72 us
    all_to_all x1, waiting for transfers between devices, shards(): energy = lax.all_to_all(energy, 'gx', 0, 0, tiled=True)  4.01 us
  transfers between devices with their start and end apart: 13, of which 7 were waited for; matrix products, arithmetic and copies ran while one was open for 1% of the time, Pallas kernels for 1%

profile of v5, /device:TPU:1, one launch (start us, length us, event | category | flops | bytes accessed | tf_op | source)
XLA Modules:
  0.0 99.5 jit_solution(8074649508779797401)
XLA Ops:
  0.6 1.5 %pack.1 = (f32[8,8,128]{2,1,0:T(8,128)}, f32[3,8,128]{2,1,0:T(8,128)}, f32[3,8,128]{2,1,0:T(8,128)}, f32[8,128]{1,0:T(8,128)}) custom-call(f32[3,8,128]{2,1,0:T(8,128)} %bitcast.24, f32[3,8,128]{2,1,0:T(8,128)} %bitcast.25, f32[8,128]{1,0:T(8,128)} %bitcast.26, s32[8,128]{1,0:T(8,128)} %bitcast.27, s32[8,128]{1,0:T(8,128)} %bitcast.28, ...), custom_call_target="tpu_custom_call" | custom-call | tf_op jit(solution)/shard_map/pack/pallas_call | solution.py:368
  2.2 0.0 copy-start
  2.2 4.4 %collective-permute-start = (f32[3,8,128]{2,1,0:T(8,128)}, f32[3,8,128]{2,1,0:T(8,128)S(1)}, u32[]{:S(2)}, u32[]{:S(2)}) collective-permute-start(f32[3,8,128]{2,1,0:T(8,128)} %get-tuple-element.18), channel_id=1, source_target_pairs={{0,32},{32,64},{64,96},{96,128},{128,160},{160,192},{192,224},{224... | collective-permute-start | bytes 36872 | tf_op jit(solution)/shard_map/ppermute | solution.py:326
  6.6 9.5 %collective-permute-start.1 = (f32[3,8,128]{2,1,0:T(8,128)}, f32[3,8,128]{2,1,0:T(8,128)S(1)}, u32[]{:S(2)}, u32[]{:S(2)}) collective-permute-start(f32[3,8,128]{2,1,0:T(8,128)} %get-tuple-element.20), channel_id=1, source_target_pairs={{0,480},{32,0},{64,32},{96,64},{128,96},{160,128},{192,160},{224,1... | collective-permute-start | bytes 36872 | tf_op jit(solution)/shard_map/ppermute | solution.py:326
  16.1 0.0 copy-start.2
  16.1 0.0 collective-permute-done.left
  16.1 0.9 collective-permute-done.1.right
  17.1 0.0 copy-done
  17.1 0.0 copy-done.2
  17.1 0.1 join.1
  17.2 0.1 slice_bitcast_fusion.1
  17.2 1.3 %collective-permute-start.3 = (f32[12,8,128]{2,1,0:T(8,128)S(1)}, f32[12,8,128]{2,1,0:T(8,128)S(1)}, u32[]{:S(2)}, u32[]{:S(2)}) collective-permute-start(f32[12,8,128]{2,1,0:T(8,128)S(1)} %get-tuple-element.23), channel_id=1, source_target_pairs={{8,0},{16,8},{24,16},{9,1},{17,9},{25,17},{10,2},{18,10},{26,18},{... | collective-permute-start | bytes 147464 | tf_op jit(solution)/shard_map/ppermute | solution.py:326
  18.5 4.0 %collective-permute-start.2 = (f32[12,8,128]{2,1,0:T(8,128)S(1)}, f32[12,8,128]{2,1,0:T(8,128)S(1)}, u32[]{:S(2)}, u32[]{:S(2)}) collective-permute-start(f32[12,8,128]{2,1,0:T(8,128)S(1)} %get-tuple-element.23), channel_id=1, source_target_pairs={{0,8},{8,16},{16,24},{1,9},{9,17},{17,25},{2,10},{10,18},{18,26},{... | collective-permute-start | bytes 147464 | tf_op jit(solution)/shard_map/ppermute | solution.py:326
  22.5 0.1 convert_reduce_fusion
  22.6 0.1 select_reduce_fusion.1
  22.7 0.1 reshape.104.meta
  22.8 0.9 collective-permute-done.2
  23.7 0.0 collective-permute-done.3
  23.7 2.7 %collective-permute-start.5 = (f32[36,8,128]{2,1,0:T(8,128)S(1)}, f32[36,8,128]{2,1,0:T(8,128)S(1)}, u32[]{:S(2)}, u32[]{:S(2)}) collective-permute-start(f32[36,8,128]{2,1,0:T(8,128)S(1)} %constant_dynamic-update-slice_fusion.middle), channel_id=1, source_target_pairs={{0,7},{1,0},{2,1},{3,2},{4,3},{5,4},{6,5},{7,6},{8,15},{9,8},{10,9... | collective-permute-start | bytes 442376 | tf_op jit(solution)/shard_map/ppermute | solution.py:326
  26.4 1.2 %collective-permute-start.4 = (f32[36,8,128]{2,1,0:T(8,128)S(1)}, f32[36,8,128]{2,1,0:T(8,128)S(1)}, u32[]{:S(2)}, u32[]{:S(2)}) collective-permute-start(f32[36,8,128]{2,1,0:T(8,128)S(1)} %constant_dynamic-update-slice_fusion.middle), channel_id=1, source_target_pairs={{0,1},{1,2},{2,3},{3,4},{4,5},{5,6},{6,7},{7,0},{8,9},{9,10},{10,1... | collective-permute-start | bytes 442376 | tf_op jit(solution)/shard_map/ppermute | solution.py:326
  27.6 0.1 convert_reduce_fusion.1
  27.7 3.0 %collective-permute-done.5.high = f32[36,8,128]{2,1,0:T(8,128)S(1)} collective-permute-done((f32[36,8,128]{2,1,0:T(8,128)S(1)}, f32[36,8,128]{2,1,0:T(8,128)S(1)}, u32[]{:S(2)}, u32[]{:S(2)}) %collective-permute-start.5) | collective-permute-done | bytes 147488 | tf_op jit(solution)/shard_map/ppermute | solution.py:326
  30.7 0.0 collective-permute-done.4.low
  30.7 7.7 %first_step.1 = f32[10,8,128]{2,1,0:T(8,128)S(1)} custom-call(s32[60]{0:T(128)S(1)} %reshape.104.meta, f32[36,8,128]{2,1,0:T(8,128)S(1)} %collective-permute-done.4.low, f32[36,8,128]{2,1,0:T(8,128)S(1)} %constant_dynamic-update-slice_fusion.middle, f32[36,8,128]{2,1,0:T(8,128)S(1)} %collective-permute-done.5.high), custom_call_target="tpu_custom_call" | custom-call | tf_op jit(solution)/shard_map/first_step/pallas_call | solution.py:407
  38.4 1.3 %collective-permute-start.7 = (f32[10,8,128]{2,1,0:T(8,128)S(1)}, f32[10,8,128]{2,1,0:T(8,128)S(1)}, u32[]{:S(2)}, u32[]{:S(2)}) collective-permute-start(f32[10,8,128]{2,1,0:T(8,128)S(1)} %first_step.1), channel_id=1, source_target_pairs={{8,0},{16,8},{24,16},{9,1},{17,9},{25,17},{10,2},{18,10},{26,18},{... | collective-permute-start | bytes 122888 | tf_op jit(solution)/shard_map/ppermute | solution.py:326
  39.7 4.6 %collective-permute-start.6 = (f32[10,8,128]{2,1,0:T(8,128)S(1)}, f32[10,8,128]{2,1,0:T(8,128)S(1)}, u32[]{:S(2)}, u32[]{:S(2)}) collective-permute-start(f32[10,8,128]{2,1,0:T(8,128)S(1)} %first_step.1), channel_id=1, source_target_pairs={{0,8},{8,16},{16,24},{1,9},{9,17},{17,25},{2,10},{10,18},{18,26},{... | collective-permute-start | bytes 122888 | tf_op jit(solution)/shard_map/ppermute | solution.py:326
  44.3 0.1 select_reduce_fusion.3
  44.4 0.0 collective-permute-done.7
  44.4 1.0 collective-permute-done.6
  45.4 2.6 %collective-permute-start.9 = (f32[30,8,128]{2,1,0:T(8,128)S(1)}, f32[30,8,128]{2,1,0:T(8,128)S(1)}, u32[]{:S(2)}, u32[]{:S(2)}) collective-permute-start(f32[30,8,128]{2,1,0:T(8,128)S(1)} %pad_maximum_fusion.middle), channel_id=1, source_target_pairs={{0,7},{1,0},{2,1},{3,2},{4,3},{5,4},{6,5},{7,6},{8,15},{9,8},{10,9... | collective-permute-start | bytes 368648 | tf_op jit(solution)/shard_map/ppermute | solution.py:326
  48.0 0.0 collective-permute-start.8
  48.0 0.1 add_select_fusion.13
  48.2 0.1 reshape.103.meta
  48.2 2.1 %collective-permute-done.9.high = f32[30,8,128]{2,1,0:T(8,128)S(1)} collective-permute-done((f32[30,8,128]{2,1,0:T(8,128)S(1)}, f32[30,8,128]{2,1,0:T(8,128)S(1)}, u32[]{:S(2)}, u32[]{:S(2)}) %collective-permute-start.9) | collective-permute-done | bytes 122912 | tf_op jit(solution)/shard_map/ppermute | solution.py:326
  50.3 0.0 collective-permute-done.8.low
  50.3 9.0 %second_step.1 = (f32[3,8,128]{2,1,0:T(8,128)}, f32[3,8,128]{2,1,0:T(8,128)}, f32[8,16,128]{2,1,0:T(8,128)S(1)}, f32[16,8,128]{2,1,0:T(8,128)}) custom-call(s32[48]{0:T(128)S(1)} %reshape.103.meta, f32[30,8,128]{2,1,0:T(8,128)S(1)} %collective-permute-done.8.low, f32[30,8,128]{2,1,0:T(8,128)S(1)} %pad_maximum_fusion.middle, ...), custom_call_target="tpu_custom_call" | custom-call | tf_op jit(solution)/shard_map/second_step/pallas_call | solution.py:423
  59.3 9.6 %all-to-all-start = ((f32[16,8,128]{2,1,0:T(8,128)}), f32[16,8,128]{2,1,0:T(8,128)S(1)}, u32[]{:S(2)}, u32[]{:S(2)}) async-start(f32[16,8,128]{2,1,0:T(8,128)} %get-tuple-element.27), calls=%async_computation | async-start | bytes 131072 | tf_op jit(solution)/shard_map/all_to_all | solution.py:441
  68.9 0.3 deposit.1.own
  69.3 1.3 %collective-permute-start.11 = (f32[64,128]{1,0:T(8,128)S(1)}, f32[64,128]{1,0:T(8,128)S(1)}, u32[]{:S(2)}, u32[]{:S(2)}) collective-permute-start(f32[64,128]{1,0:T(8,128)S(1)} %deposit.1.own), channel_id=1, source_target_pairs={{32,0},{64,32},{96,64},{128,96},{160,128},{192,160},{224,192},{256... | collective-permute-start | bytes 98312 | tf_op jit(solution)/shard_map/ppermute | solution.py:326
  70.6 4.0 %collective-permute-start.10 = (f32[64,128]{1,0:T(8,128)S(1)}, f32[64,128]{1,0:T(8,128)S(1)}, u32[]{:S(2)}, u32[]{:S(2)}) collective-permute-start(f32[64,128]{1,0:T(8,128)S(1)} %deposit.1.own), channel_id=1, source_target_pairs={{0,32},{32,64},{64,96},{96,128},{128,160},{160,192},{192,224},{224... | collective-permute-start | bytes 98312 | tf_op jit(solution)/shard_map/ppermute | solution.py:326
  74.5 0.1 pad_add_fusion.coords
  74.6 0.0 collective-permute-done.11.after
  74.6 0.9 collective-permute-done.10.before
  75.6 0.9 planes.1.parts
  76.5 4.0 %all-to-all-done.energy = f32[16,8,128]{2,1,0:T(8,128)S(1)} async-done(((f32[16,8,128]{2,1,0:T(8,128)}), f32[16,8,128]{2,1,0:T(8,128)S(1)}, u32[]{:S(2)}, u32[]{:S(2)}) %all-to-all-start) | async-done | bytes 65568 | tf_op jit(solution)/shard_map/all_to_all | solution.py:441
  80.5 0.1 energies.1
  80.6 18.1 %all_to_all.10.parts = f32[32,8,128]{2,1,0:T(8,128)S(1)} all-to-all(f32[32,8,128]{2,1,0:T(8,128)S(1)} %energies.1), channel_id=1, replica_groups=mesh['gx'=16,'gy'=4,'gz'=8] {'gy','gz'}, dimensions={0} | all-to-all | bytes 262144 | tf_op jit(solution)/shard_map/all_to_all | solution.py:474
  98.7 0.8 lines.1
  (17 shorter events, 0.1 us)
Async XLA Ops:
  2.2 14.9 %copy-start = (f32[8,8,128]{2,1,0:T(8,128)S(1)}, f32[8,8,128]{2,1,0:T(8,128)}, u32[]{:S(2)}) copy-start(f32[8,8,128]{2,1,0:T(8,128)} %get-tuple-element.19.own) | copy-start | bytes 98308
  2.2 14.0 %collective-permute-start = (f32[3,8,128]{2,1,0:T(8,128)}, f32[3,8,128]{2,1,0:T(8,128)S(1)}, u32[]{:S(2)}, u32[]{:S(2)}) collective-permute-start(f32[3,8,128]{2,1,0:T(8,128)} %get-tuple-element.18), channel_id=1, source_target_pairs={{0,32},{32,64},{64,96},{96,128},{128,160},{160,192},{192,224},{224... | collective-permute-start | bytes 36872 | tf_op jit(solution)/shard_map/ppermute | solution.py:326
  6.6 10.5 %collective-permute-start.1 = (f32[3,8,128]{2,1,0:T(8,128)}, f32[3,8,128]{2,1,0:T(8,128)S(1)}, u32[]{:S(2)}, u32[]{:S(2)}) collective-permute-start(f32[3,8,128]{2,1,0:T(8,128)} %get-tuple-element.20), channel_id=1, source_target_pairs={{0,480},{32,0},{64,32},{96,64},{128,96},{160,128},{192,160},{224,1... | collective-permute-start | bytes 36872 | tf_op jit(solution)/shard_map/ppermute | solution.py:326
  16.1 1.0 copy-start.2
  17.2 6.5 %collective-permute-start.3 = (f32[12,8,128]{2,1,0:T(8,128)S(1)}, f32[12,8,128]{2,1,0:T(8,128)S(1)}, u32[]{:S(2)}, u32[]{:S(2)}) collective-permute-start(f32[12,8,128]{2,1,0:T(8,128)S(1)} %get-tuple-element.23), channel_id=1, source_target_pairs={{8,0},{16,8},{24,16},{9,1},{17,9},{25,17},{10,2},{18,10},{26,18},{... | collective-permute-start | bytes 147464 | tf_op jit(solution)/shard_map/ppermute | solution.py:326
  18.5 5.2 %collective-permute-start.2 = (f32[12,8,128]{2,1,0:T(8,128)S(1)}, f32[12,8,128]{2,1,0:T(8,128)S(1)}, u32[]{:S(2)}, u32[]{:S(2)}) collective-permute-start(f32[12,8,128]{2,1,0:T(8,128)S(1)} %get-tuple-element.23), channel_id=1, source_target_pairs={{0,8},{8,16},{16,24},{1,9},{9,17},{17,25},{2,10},{10,18},{18,26},{... | collective-permute-start | bytes 147464 | tf_op jit(solution)/shard_map/ppermute | solution.py:326
  23.7 7.0 %collective-permute-start.5 = (f32[36,8,128]{2,1,0:T(8,128)S(1)}, f32[36,8,128]{2,1,0:T(8,128)S(1)}, u32[]{:S(2)}, u32[]{:S(2)}) collective-permute-start(f32[36,8,128]{2,1,0:T(8,128)S(1)} %constant_dynamic-update-slice_fusion.middle), channel_id=1, source_target_pairs={{0,7},{1,0},{2,1},{3,2},{4,3},{5,4},{6,5},{7,6},{8,15},{9,8},{10,9... | collective-permute-start | bytes 442376 | tf_op jit(solution)/shard_map/ppermute | solution.py:326
  26.4 4.3 %collective-permute-start.4 = (f32[36,8,128]{2,1,0:T(8,128)S(1)}, f32[36,8,128]{2,1,0:T(8,128)S(1)}, u32[]{:S(2)}, u32[]{:S(2)}) collective-permute-start(f32[36,8,128]{2,1,0:T(8,128)S(1)} %constant_dynamic-update-slice_fusion.middle), channel_id=1, source_target_pairs={{0,1},{1,2},{2,3},{3,4},{4,5},{5,6},{6,7},{7,0},{8,9},{9,10},{10,1... | collective-permute-start | bytes 442376 | tf_op jit(solution)/shard_map/ppermute | solution.py:326
  38.4 6.0 %collective-permute-start.7 = (f32[10,8,128]{2,1,0:T(8,128)S(1)}, f32[10,8,128]{2,1,0:T(8,128)S(1)}, u32[]{:S(2)}, u32[]{:S(2)}) collective-permute-start(f32[10,8,128]{2,1,0:T(8,128)S(1)} %first_step.1), channel_id=1, source_target_pairs={{8,0},{16,8},{24,16},{9,1},{17,9},{25,17},{10,2},{18,10},{26,18},{... | collective-permute-start | bytes 122888 | tf_op jit(solution)/shard_map/ppermute | solution.py:326
  39.7 5.7 %collective-permute-start.6 = (f32[10,8,128]{2,1,0:T(8,128)S(1)}, f32[10,8,128]{2,1,0:T(8,128)S(1)}, u32[]{:S(2)}, u32[]{:S(2)}) collective-permute-start(f32[10,8,128]{2,1,0:T(8,128)S(1)} %first_step.1), channel_id=1, source_target_pairs={{0,8},{8,16},{16,24},{1,9},{9,17},{17,25},{2,10},{10,18},{18,26},{... | collective-permute-start | bytes 122888 | tf_op jit(solution)/shard_map/ppermute | solution.py:326
  45.4 4.9 %collective-permute-start.9 = (f32[30,8,128]{2,1,0:T(8,128)S(1)}, f32[30,8,128]{2,1,0:T(8,128)S(1)}, u32[]{:S(2)}, u32[]{:S(2)}) collective-permute-start(f32[30,8,128]{2,1,0:T(8,128)S(1)} %pad_maximum_fusion.middle), channel_id=1, source_target_pairs={{0,7},{1,0},{2,1},{3,2},{4,3},{5,4},{6,5},{7,6},{8,15},{9,8},{10,9... | collective-permute-start | bytes 368648 | tf_op jit(solution)/shard_map/ppermute | solution.py:326
  48.0 2.3 %collective-permute-start.8 = (f32[30,8,128]{2,1,0:T(8,128)S(1)}, f32[30,8,128]{2,1,0:T(8,128)S(1)}, u32[]{:S(2)}, u32[]{:S(2)}) collective-permute-start(f32[30,8,128]{2,1,0:T(8,128)S(1)} %pad_maximum_fusion.middle), channel_id=1, source_target_pairs={{0,1},{1,2},{2,3},{3,4},{4,5},{5,6},{6,7},{7,0},{8,9},{9,10},{10,1... | collective-permute-start | bytes 368648 | tf_op jit(solution)/shard_map/ppermute | solution.py:326
  59.3 9.6 %copy-start.1 = (s32[1,1,1,1024]{3,2,1,0:T(1,128)S(1)}, s32[1,1,1,1024]{3,2,1,0:T(1,128)}, u32[]{:S(2)}) copy-start(s32[1,1,1,1024]{3,2,1,0:T(1,128)} %param.13) | copy-start | bytes 12292
  59.3 21.2 %all-to-all-start = ((f32[16,8,128]{2,1,0:T(8,128)}), f32[16,8,128]{2,1,0:T(8,128)S(1)}, u32[]{:S(2)}, u32[]{:S(2)}) async-start(f32[16,8,128]{2,1,0:T(8,128)} %get-tuple-element.27), calls=%async_computation | async-start | bytes 131072 | tf_op jit(solution)/shard_map/all_to_all | solution.py:441
  69.3 5.4 %collective-permute-start.11 = (f32[64,128]{1,0:T(8,128)S(1)}, f32[64,128]{1,0:T(8,128)S(1)}, u32[]{:S(2)}, u32[]{:S(2)}) collective-permute-start(f32[64,128]{1,0:T(8,128)S(1)} %deposit.1.own), channel_id=1, source_target_pairs={{32,0},{64,32},{96,64},{128,96},{160,128},{192,160},{224,192},{256... | collective-permute-start | bytes 98312 | tf_op jit(solution)/shard_map/ppermute | solution.py:326
  70.6 5.0 %collective-permute-start.10 = (f32[64,128]{1,0:T(8,128)S(1)}, f32[64,128]{1,0:T(8,128)S(1)}, u32[]{:S(2)}, u32[]{:S(2)}) collective-permute-start(f32[64,128]{1,0:T(8,128)S(1)} %deposit.1.own), channel_id=1, source_target_pairs={{0,32},{32,64},{64,96},{96,128},{128,160},{160,192},{192,224},{224... | collective-permute-start | bytes 98312 | tf_op jit(solution)/shard_map/ppermute | solution.py:326

commit v6 on v5

--- a/solution.py
+++ b/solution.py
@@ -42,12 +42,29 @@
     return jnp.concatenate([value, value], axis=0)
 
 
-def own_columns(own, mine):
-    for c in range(8):
-        mine[c] = jnp.broadcast_to(own[c : c + 1, :], (128, 128)).T
-
-
-def pair_sums(tiles, meta, t, own, second, rows, mine):
+def turn_kernel(middle, out):
+    width = middle.shape[0] // 3
+
+    @pl.loop(0, out.shape[0])
+    def _(t):
+        own = middle[width + 1 + t]
+        for c in range(8):
+            out[t, c] = jnp.broadcast_to(own[c : c + 1, :], (128, 128)).T
+
+
+def turned(middle, count):
+    return pl.pallas_call(
+        turn_kernel,
+        out_shape=jax.ShapeDtypeStruct((count, 8, 128, 128), jnp.float32),
+        in_specs=[VMEM],
+        out_specs=VMEM,
+        compiler_params=SMALL,
+        cost_estimate=pl.CostEstimate(flops=0, bytes_accessed=count * (8 << 16), transcendentals=0),
+        name="turn",
+    )(middle)
+
+
+def pair_sums(tiles, meta, t, second, rows, mine):
     lane = lax.broadcasted_iota(jnp.int32, (8, 128), 1).astype(jnp.float32)
     stride = meta.shape[0] // K
     for slot in range(K):
@@ -63,12 +80,11 @@
             rows[9 * slot + c] = value
         if second and slot < 3:
             rows[9 * slot + 8] = jnp.where(lax.bitwise_and(entry, ITSELF) > 0, lane, -1.0)
-    own_columns(own, mine)
     number = lax.broadcasted_iota(jnp.int32, (16, 128), 0).astype(jnp.float32)
     count = 11 if second else 3
     stacks = []
     for block in range(8):
-        xi, yi, zi, ui, vi, wi, ri, ci = [mine[c, 16 * block : 16 * block + 16, :] for c in range(8)]
+        xi, yi, zi, ui, vi, wi, ri, ci = [mine[t, c, 16 * block : 16 * block + 16, :] for c in range(8)]
         ci = jnp.where(ci < 0.0, -5.0, ci)
         here = number + float(16 * block)
         added = [jnp.zeros((16, 128), jnp.float32)] * count
@@ -108,12 +124,7 @@
 
 
 def work_space():
-    return (
-        pltpu.VMEM((9 * K, 8, 128), jnp.float32),
-        pltpu.VMEM((8, 128, 128), jnp.float32),
-        pltpu.VMEM((9 * K, 8, 128), jnp.float32),
-        pltpu.VMEM((8, 128, 128), jnp.float32),
-    )
+    return (pltpu.VMEM((9 * K, 8, 128), jnp.float32), pltpu.VMEM((9 * K, 8, 128), jnp.float32))
 
 
 def fill(tiles, low, middle, high, size):
@@ -122,14 +133,14 @@
             tiles[part * size + i] = ref[i]
 
 
-def first_kernel(meta, low, middle, high, out, tiles, *work):
+def first_kernel(meta, low, middle, high, mine, out, tiles, *work):
     width = middle.shape[0] // 3
     fill(tiles, low, middle, high, 3 * width)
     sub = lax.broadcasted_iota(jnp.int32, (8, 128), 0)
 
-    def one(t, *work):
+    def one(t, rows):
         own = tiles[4 * width + t + 1]
-        sums = pair_sums(tiles, meta, t, own, False, *work)
+        sums = pair_sums(tiles, meta, t, False, rows, mine)
         radius = own[6:7, :]
         gain = STEP_DT / (DENS * radius * radius * radius)
         fresh = own
@@ -142,21 +153,21 @@
 
     @pl.loop(0, (width - 2) // 2)
     def _(t):
-        one(2 * t, work[0], work[1])
-        one(2 * t + 1, work[2], work[3])
+        one(2 * t, work[0])
+        one(2 * t + 1, work[1])
 
 
 def second_kernel(
-    meta, low, middle, high, place_out, speed_out, values_out, energy_out, tiles, total, *work
+    meta, low, middle, high, mine, place_out, speed_out, values_out, energy_out, tiles, total, *work
 ):
     width = middle.shape[0] // 3
     fill(tiles, low, middle, high, 3 * width)
     sub = lax.broadcasted_iota(jnp.int32, (8, 128), 0)
     total[...] = jnp.zeros((8, 128), jnp.float32)
 
-    def one(t, *work):
+    def one(t, rows):
         own = tiles[4 * width + t + 1]
-        sums = pair_sums(tiles, meta, t, own, True, *work)
+        sums = pair_sums(tiles, meta, t, True, rows, mine)
         radius = own[6:7, :]
         mass = DENS * radius * radius * radius
         gain = STEP_DT / mass
@@ -180,8 +191,8 @@
 
     @pl.loop(0, NT // 2)
     def _(t):
-        one(2 * t, work[0], work[1])
-        one(2 * t + 1, work[2], work[3])
+        one(2 * t, work[0])
+        one(2 * t + 1, work[1])
 
     for i in range(energy_out.shape[0]):
         energy_out[i] = total[...]
@@ -309,6 +320,11 @@
         ref[2] = notes[...]
 
 
+def keep_kernel(own, notes, own_out, notes_out):
+    own_out[...] = own[...]
+    notes_out[...] = notes[...]
+
+
 def join_kernel(left, own, right, mine, line, notes):
     for i in range(2):
         line[i] = left[i]
@@ -373,6 +389,15 @@
         scratch_shapes=[pltpu.VMEM(a.shape, a.dtype) for a in arguments] + [pltpu.SemaphoreType.DMA((7,))],
         name="pack",
     )(*arguments)
+    own, notes = pl.pallas_call(
+        keep_kernel,
+        out_shape=(tile, jax.ShapeDtypeStruct((8, 128), jnp.float32)),
+        in_specs=[VMEM] * 2,
+        out_specs=(VMEM,) * 2,
+        compiler_params=SMALL,
+        cost_estimate=pl.CostEstimate(flops=0, bytes_accessed=2 << 20, transcendentals=0),
+        name="keep",
+    )(own, notes)
     from_left = shifted(to_right, "gx", 1, True)
     from_right = shifted(to_left, "gx", -1, True)
     width = NT + 4
@@ -397,6 +422,7 @@
         return low, middle, high
 
     low, middle, high = extended(line)
+    mine = turned(middle, width - 2)
     listed = listed[0 : K + 1, 0 : NT + 2].astype(jnp.int32)
     spots = lax.broadcasted_iota(jnp.int32, (1, NT + 2), 1)
     shift = jnp.where(spots == 0, -1, jnp.where(spots == NT + 1, 1, 0))
@@ -407,7 +433,7 @@
     line = pl.pallas_call(
         first_kernel,
         out_shape=jax.ShapeDtypeStruct((width - 2, 8, 128), jnp.float32),
-        in_specs=[SMEM] + [VMEM] * 3,
+        in_specs=[SMEM] + [VMEM] * 4,
         out_specs=VMEM,
         scratch_shapes=[
             pltpu.VMEM((9 * width, 8, 128), jnp.float32),
@@ -415,8 +441,9 @@
         ],
         compiler_params=LARGE,
         name="first_step",
-    )(first_meta, low, middle, high)
+    )(first_meta, low, middle, high, mine)
     low, middle, high = extended(line)
+    mine = turned(middle, NT)
     width = width - 2
     peers = lax.axis_size("gx")
     block = jax.ShapeDtypeStruct((3, NT, 128), jnp.float32)
@@ -428,7 +455,7 @@
             jax.ShapeDtypeStruct((NT, 16, 128), jnp.float32),
             jax.ShapeDtypeStruct((peers, 8, 128), jnp.float32),
         ),
-        in_specs=[SMEM] + [VMEM] * 3,
+        in_specs=[SMEM] + [VMEM] * 4,
         out_specs=(VMEM,) * 4,
         scratch_shapes=[
             pltpu.VMEM((9 * width, 8, 128), jnp.float32),
@@ -437,7 +464,7 @@
         ],
         compiler_params=LARGE,
         name="second_step",
-    )(second_meta, low, middle, high)
+    )(second_meta, low, middle, high, mine)
     energy = lax.all_to_all(energy, "gx", 0, 0, tiled=True)
     grid = pl.pallas_call(
         deposit_kernel,

time: 100 us -> 97.9 us (0.979)
  waiting for transfers between devices: 12.8 us -> 7.57 us
  Pallas kernels: 20.4 us -> 21.9 us
  local copies, waits for them, and re-layouts: 0.26 us -> 1.69 us
    ppermute x12, waiting for transfers between devices: 8.79 us -> 3.56 us  [shifted(): return lax.ppermute(value, axis, pairs)]
    pallas_call x0 -> x3, Pallas kernels: none -> 3.61 us  [the longest x2 3.61 us: turned(): pl.pallas_call(turn_kernel, out_shape=jax.ShapeDtypeStruct((count, 8, 128...]
    unnamed x8, local copies, waits for them, and re-layouts: 0.02 us -> 1.45 us
    pallas_call x1, Pallas kernels: 7.72 us -> 6.47 us  [shards(): pl.pallas_call(first_kernel, out_shape=jax.ShapeDtypeStruct((width - 2, 8...]
  transfers between devices with their start and end apart: 13 -> 13, of which waited for: 7 -> 6; matrix products, arithmetic and copies ran while one was open for 1% -> 1% of each run, Pallas kernels for 1% -> 5%
where the time goes in v6:
time: 97.9 us; the launch traced here: 97.3 us
  starting transfers between devices  46.4 us (47%)
  Pallas kernels  21.9 us (22%)
  blocking collectives  18.2 us (19%)
  waiting for transfers between devices  7.57 us (8%)
  local copies, waits for them, and re-layouts  1.69 us (2%)
    ppermute x12, starting transfers between devices, shifted(): return lax.ppermute(value, axis, pairs)  37 us
    all_to_all x1, blocking collectives, shards(): parts = lax.all_to_all(parts, ('gy', 'gz'), 0, 0, tiled=True)  18.2 us
    all_to_all x1, starting transfers between devices, shards(): energy = lax.all_to_all(energy, 'gx', 0, 0, tiled=True)  9.46 us
    pallas_call x1, Pallas kernels, shards(): pl.pallas_call(second_kernel, out_shape=(block, block, jax.ShapeDtypeStru...  8.18 us
    pallas_call x1, Pallas kernels, shards(): pl.pallas_call(first_kernel, out_shape=jax.ShapeDtypeStruct((width - 2, 8...  6.47 us
    all_to_all x1, waiting for transfers between devices, shards(): energy = lax.all_to_all(energy, 'gx', 0, 0, tiled=True)  4.01 us
    pallas_call x2, Pallas kernels, turned(): pl.pallas_call(turn_kernel, out_shape=jax.ShapeDtypeStruct((count, 8, 128...  3.61 us
    ppermute x12, waiting for transfers between devices, shifted(): return lax.ppermute(value, axis, pairs)  3.56 us
  transfers between devices with their start and end apart: 13, of which 6 were waited for; matrix products, arithmetic and copies ran while one was open for 1% of the time, Pallas kernels for 5%

profile of v6, /device:TPU:1, one launch (start us, length us, event | category | flops | bytes accessed | tf_op | source)
XLA Modules:
  0.0 97.3 jit_solution(17841453823864590234)
XLA Ops:
  0.6 1.5 %pack.1 = (f32[8,8,128]{2,1,0:T(8,128)}, f32[3,8,128]{2,1,0:T(8,128)}, f32[3,8,128]{2,1,0:T(8,128)}, f32[8,128]{1,0:T(8,128)}) custom-call(f32[3,8,128]{2,1,0:T(8,128)} %bitcast.24, f32[3,8,128]{2,1,0:T(8,128)} %bitcast.25, f32[8,128]{1,0:T(8,128)} %bitcast.26, s32[8,128]{1,0:T(8,128)} %bitcast.27, s32[8,128]{1,0:T(8,128)} %bitcast.28, ...), custom_call_target="tpu_custom_call" | custom-call | tf_op jit(solution)/shard_map/pack/pallas_call | solution.py:384
  2.2 4.4 %collective-permute-start = (f32[3,8,128]{2,1,0:T(8,128)}, f32[3,8,128]{2,1,0:T(8,128)S(1)}, u32[]{:S(2)}, u32[]{:S(2)}) collective-permute-start(f32[3,8,128]{2,1,0:T(8,128)} %get-tuple-element.20), channel_id=1, source_target_pairs={{0,32},{32,64},{64,96},{96,128},{128,160},{160,192},{192,224},{224... | collective-permute-start | bytes 36872 | tf_op jit(solution)/shard_map/ppermute | solution.py:342
  6.5 9.5 %collective-permute-start.1 = (f32[3,8,128]{2,1,0:T(8,128)}, f32[3,8,128]{2,1,0:T(8,128)S(1)}, u32[]{:S(2)}, u32[]{:S(2)}) collective-permute-start(f32[3,8,128]{2,1,0:T(8,128)} %get-tuple-element.24), channel_id=1, source_target_pairs={{0,480},{32,0},{64,32},{96,64},{128,96},{160,128},{192,160},{224,1... | collective-permute-start | bytes 36872 | tf_op jit(solution)/shard_map/ppermute | solution.py:342
  16.1 0.7 copy-done
  16.9 0.7 copy-done.2
  17.6 0.0 collective-permute-done.left
  17.6 0.0 collective-permute-done.1.right
  17.6 0.1 join.1
  17.7 0.1 slice_bitcast_fusion.1
  17.7 1.3 %collective-permute-start.3 = (f32[12,8,128]{2,1,0:T(8,128)S(1)}, f32[12,8,128]{2,1,0:T(8,128)S(1)}, u32[]{:S(2)}, u32[]{:S(2)}) collective-permute-start(f32[12,8,128]{2,1,0:T(8,128)S(1)} %get-tuple-element.27), channel_id=1, source_target_pairs={{8,0},{16,8},{24,16},{9,1},{17,9},{25,17},{10,2},{18,10},{26,18},{... | collective-permute-start | bytes 147464 | tf_op jit(solution)/shard_map/ppermute | solution.py:342
  19.0 4.0 %collective-permute-start.2 = (f32[12,8,128]{2,1,0:T(8,128)S(1)}, f32[12,8,128]{2,1,0:T(8,128)S(1)}, u32[]{:S(2)}, u32[]{:S(2)}) collective-permute-start(f32[12,8,128]{2,1,0:T(8,128)S(1)} %get-tuple-element.27), channel_id=1, source_target_pairs={{0,8},{8,16},{16,24},{1,9},{9,17},{17,25},{2,10},{10,18},{18,26},{... | collective-permute-start | bytes 147464 | tf_op jit(solution)/shard_map/ppermute | solution.py:342
  23.0 0.1 convert_reduce_fusion
  23.1 0.1 select_reduce_fusion.1
  23.2 0.1 reshape.104.meta
  23.3 0.9 collective-permute-done.2
  24.2 0.0 collective-permute-done.3
  24.2 2.2 %collective-permute-start.5 = (f32[36,8,128]{2,1,0:T(8,128)S(1)}, f32[36,8,128]{2,1,0:T(8,128)S(1)}, u32[]{:S(2)}, u32[]{:S(2)}) collective-permute-start(f32[36,8,128]{2,1,0:T(8,128)S(1)} %constant_dynamic-update-slice_fusion.middle), channel_id=1, source_target_pairs={{0,7},{1,0},{2,1},{3,2},{4,3},{5,4},{6,5},{7,6},{8,15},{9,8},{10,9... | collective-permute-start | bytes 442376 | tf_op jit(solution)/shard_map/ppermute | solution.py:342
  26.4 1.2 %collective-permute-start.4 = (f32[36,8,128]{2,1,0:T(8,128)S(1)}, f32[36,8,128]{2,1,0:T(8,128)S(1)}, u32[]{:S(2)}, u32[]{:S(2)}) collective-permute-start(f32[36,8,128]{2,1,0:T(8,128)S(1)} %constant_dynamic-update-slice_fusion.middle), channel_id=1, source_target_pairs={{0,1},{1,2},{2,3},{3,4},{4,5},{5,6},{6,7},{7,0},{8,9},{9,10},{10,1... | collective-permute-start | bytes 442376 | tf_op jit(solution)/shard_map/ppermute | solution.py:342
  27.6 0.1 convert_reduce_fusion.1
  27.7 2.0 %turn.2.mine = f32[10,8,128,128]{3,2,1,0:T(8,128)S(1)} custom-call(f32[36,8,128]{2,1,0:T(8,128)S(1)} %constant_dynamic-update-slice_fusion.middle), custom_call_target="tpu_custom_call" | custom-call | bytes 5242880 | tf_op jit(solution)/shard_map/turn/pallas_call | solution.py:56
  29.7 0.7 collective-permute-done.5.high
  30.4 0.0 collective-permute-done.4.low
  30.4 6.5 %first_step.1 = f32[10,8,128]{2,1,0:T(8,128)S(1)} custom-call(s32[60]{0:T(128)S(1)} %reshape.104.meta, f32[36,8,128]{2,1,0:T(8,128)S(1)} %collective-permute-done.4.low, f32[36,8,128]{2,1,0:T(8,128)S(1)} %constant_dynamic-update-slice_fusion.middle, f32[36,8,128]{2,1,0:T(8,128)S(1)} %collective-permute-done.5.high, f32[10,8,128,128]{3,2,1,0:T(8,128)S(1)} %turn.2.mine), custom_call_target="tpu_custom_call" | custom-call | tf_op jit(solution)/shard_map/first_step/pallas_call | solution.py:433
  36.9 0.0 copy-start.1
  36.9 1.3 %collective-permute-start.7 = (f32[10,8,128]{2,1,0:T(8,128)S(1)}, f32[10,8,128]{2,1,0:T(8,128)S(1)}, u32[]{:S(2)}, u32[]{:S(2)}) collective-permute-start(f32[10,8,128]{2,1,0:T(8,128)S(1)} %first_step.1), channel_id=1, source_target_pairs={{8,0},{16,8},{24,16},{9,1},{17,9},{25,17},{10,2},{18,10},{26,18},{... | collective-permute-start | bytes 122888 | tf_op jit(solution)/shard_map/ppermute | solution.py:342
  38.2 4.6 %collective-permute-start.6 = (f32[10,8,128]{2,1,0:T(8,128)S(1)}, f32[10,8,128]{2,1,0:T(8,128)S(1)}, u32[]{:S(2)}, u32[]{:S(2)}) collective-permute-start(f32[10,8,128]{2,1,0:T(8,128)S(1)} %first_step.1), channel_id=1, source_target_pairs={{0,8},{8,16},{16,24},{1,9},{9,17},{17,25},{2,10},{10,18},{18,26},{... | collective-permute-start | bytes 122888 | tf_op jit(solution)/shard_map/ppermute | solution.py:342
  42.8 0.1 select_reduce_fusion.3
  42.9 0.0 collective-permute-done.7
  42.9 1.0 %collective-permute-done.6 = f32[10,8,128]{2,1,0:T(8,128)S(1)} collective-permute-done((f32[10,8,128]{2,1,0:T(8,128)S(1)}, f32[10,8,128]{2,1,0:T(8,128)S(1)}, u32[]{:S(2)}, u32[]{:S(2)}) %collective-permute-start.6) | collective-permute-done | bytes 40992 | tf_op jit(solution)/shard_map/ppermute | solution.py:342
  43.9 3.3 %collective-permute-start.9 = (f32[30,8,128]{2,1,0:T(8,128)S(1)}, f32[30,8,128]{2,1,0:T(8,128)S(1)}, u32[]{:S(2)}, u32[]{:S(2)}) collective-permute-start(f32[30,8,128]{2,1,0:T(8,128)S(1)} %pad_maximum_fusion.middle), channel_id=1, source_target_pairs={{0,7},{1,0},{2,1},{3,2},{4,3},{5,4},{6,5},{7,6},{8,15},{9,8},{10,9... | collective-permute-start | bytes 368648 | tf_op jit(solution)/shard_map/ppermute | solution.py:342
  47.2 0.0 collective-permute-start.8
  47.2 0.1 add_select_fusion.13
  47.3 0.1 reshape.103.meta
  47.4 1.6 %turn.3.mine = f32[8,8,128,128]{3,2,1,0:T(8,128)S(1)} custom-call(f32[30,8,128]{2,1,0:T(8,128)S(1)} %pad_maximum_fusion.middle), custom_call_target="tpu_custom_call" | custom-call | bytes 4194304 | tf_op jit(solution)/shard_map/turn/pallas_call | solution.py:56
  49.0 0.1 collective-permute-done.9.high
  49.1 0.0 collective-permute-done.8.low
  49.1 8.2 %second_step.1 = (f32[3,8,128]{2,1,0:T(8,128)}, f32[3,8,128]{2,1,0:T(8,128)}, f32[8,16,128]{2,1,0:T(8,128)S(1)}, f32[16,8,128]{2,1,0:T(8,128)}) custom-call(s32[48]{0:T(128)S(1)} %reshape.103.meta, f32[30,8,128]{2,1,0:T(8,128)S(1)} %collective-permute-done.8.low, f32[30,8,128]{2,1,0:T(8,128)S(1)} %pad_maximum_fusion.middle, ...), custom_call_target="tpu_custom_call" | custom-call | tf_op jit(solution)/shard_map/second_step/pallas_call | solution.py:450
  57.2 9.5 %all-to-all-start = ((f32[16,8,128]{2,1,0:T(8,128)}), f32[16,8,128]{2,1,0:T(8,128)S(1)}, u32[]{:S(2)}, u32[]{:S(2)}) async-start(f32[16,8,128]{2,1,0:T(8,128)} %get-tuple-element.31), calls=%async_computation | async-start | bytes 131072 | tf_op jit(solution)/shard_map/all_to_all | solution.py:468
  66.7 0.3 deposit.1.own
  67.0 1.3 %collective-permute-start.11 = (f32[64,128]{1,0:T(8,128)S(1)}, f32[64,128]{1,0:T(8,128)S(1)}, u32[]{:S(2)}, u32[]{:S(2)}) collective-permute-start(f32[64,128]{1,0:T(8,128)S(1)} %deposit.1.own), channel_id=1, source_target_pairs={{32,0},{64,32},{96,64},{128,96},{160,128},{192,160},{224,192},{256... | collective-permute-start | bytes 98312 | tf_op jit(solution)/shard_map/ppermute | solution.py:342
  68.3 4.0 %collective-permute-start.10 = (f32[64,128]{1,0:T(8,128)S(1)}, f32[64,128]{1,0:T(8,128)S(1)}, u32[]{:S(2)}, u32[]{:S(2)}) collective-permute-start(f32[64,128]{1,0:T(8,128)S(1)} %deposit.1.own), channel_id=1, source_target_pairs={{0,32},{32,64},{64,96},{96,128},{128,160},{160,192},{192,224},{224... | collective-permute-start | bytes 98312 | tf_op jit(solution)/shard_map/ppermute | solution.py:342
  72.3 0.1 pad_add_fusion.coords
  72.4 0.9 collective-permute-done.10.before
  73.3 0.9 planes.1.parts
  74.3 4.0 %all-to-all-done.energy = f32[16,8,128]{2,1,0:T(8,128)S(1)} async-done(((f32[16,8,128]{2,1,0:T(8,128)}), f32[16,8,128]{2,1,0:T(8,128)S(1)}, u32[]{:S(2)}, u32[]{:S(2)}) %all-to-all-start) | async-done | bytes 65568 | tf_op jit(solution)/shard_map/all_to_all | solution.py:468
  78.3 0.1 energies.1
  78.4 18.2 %all_to_all.10.parts = f32[32,8,128]{2,1,0:T(8,128)S(1)} all-to-all(f32[32,8,128]{2,1,0:T(8,128)S(1)} %energies.1), channel_id=1, replica_groups=mesh['gx'=16,'gy'=4,'gz'=8] {'gy','gz'}, dimensions={0} | all-to-all | bytes 262144 | tf_op jit(solution)/shard_map/all_to_all | solution.py:501
  96.5 0.8 lines.1
  (20 shorter events, 0.1 us)
Async XLA Ops:
  2.2 15.4 %collective-permute-start = (f32[3,8,128]{2,1,0:T(8,128)}, f32[3,8,128]{2,1,0:T(8,128)S(1)}, u32[]{:S(2)}, u32[]{:S(2)}) collective-permute-start(f32[3,8,128]{2,1,0:T(8,128)} %get-tuple-element.20), channel_id=1, source_target_pairs={{0,32},{32,64},{64,96},{96,128},{128,160},{160,192},{192,224},{224... | collective-permute-start | bytes 36872 | tf_op jit(solution)/shard_map/ppermute | solution.py:342
  6.5 11.0 %collective-permute-start.1 = (f32[3,8,128]{2,1,0:T(8,128)}, f32[3,8,128]{2,1,0:T(8,128)S(1)}, u32[]{:S(2)}, u32[]{:S(2)}) collective-permute-start(f32[3,8,128]{2,1,0:T(8,128)} %get-tuple-element.24), channel_id=1, source_target_pairs={{0,480},{32,0},{64,32},{96,64},{128,96},{160,128},{192,160},{224,1... | collective-permute-start | bytes 36872 | tf_op jit(solution)/shard_map/ppermute | solution.py:342
  16.1 0.8 copy-start
  16.9 0.7 copy-start.2
  17.7 6.5 %collective-permute-start.3 = (f32[12,8,128]{2,1,0:T(8,128)S(1)}, f32[12,8,128]{2,1,0:T(8,128)S(1)}, u32[]{:S(2)}, u32[]{:S(2)}) collective-permute-start(f32[12,8,128]{2,1,0:T(8,128)S(1)} %get-tuple-element.27), channel_id=1, source_target_pairs={{8,0},{16,8},{24,16},{9,1},{17,9},{25,17},{10,2},{18,10},{26,18},{... | collective-permute-start | bytes 147464 | tf_op jit(solution)/shard_map/ppermute | solution.py:342
  19.0 5.2 %collective-permute-start.2 = (f32[12,8,128]{2,1,0:T(8,128)S(1)}, f32[12,8,128]{2,1,0:T(8,128)S(1)}, u32[]{:S(2)}, u32[]{:S(2)}) collective-permute-start(f32[12,8,128]{2,1,0:T(8,128)S(1)} %get-tuple-element.27), channel_id=1, source_target_pairs={{0,8},{8,16},{16,24},{1,9},{9,17},{17,25},{2,10},{10,18},{18,26},{... | collective-permute-start | bytes 147464 | tf_op jit(solution)/shard_map/ppermute | solution.py:342
  24.2 6.2 %collective-permute-start.5 = (f32[36,8,128]{2,1,0:T(8,128)S(1)}, f32[36,8,128]{2,1,0:T(8,128)S(1)}, u32[]{:S(2)}, u32[]{:S(2)}) collective-permute-start(f32[36,8,128]{2,1,0:T(8,128)S(1)} %constant_dynamic-update-slice_fusion.middle), channel_id=1, source_target_pairs={{0,7},{1,0},{2,1},{3,2},{4,3},{5,4},{6,5},{7,6},{8,15},{9,8},{10,9... | collective-permute-start | bytes 442376 | tf_op jit(solution)/shard_map/ppermute | solution.py:342
  26.4 4.0 %collective-permute-start.4 = (f32[36,8,128]{2,1,0:T(8,128)S(1)}, f32[36,8,128]{2,1,0:T(8,128)S(1)}, u32[]{:S(2)}, u32[]{:S(2)}) collective-permute-start(f32[36,8,128]{2,1,0:T(8,128)S(1)} %constant_dynamic-update-slice_fusion.middle), channel_id=1, source_target_pairs={{0,1},{1,2},{2,3},{3,4},{4,5},{5,6},{6,7},{7,0},{8,9},{9,10},{10,1... | collective-permute-start | bytes 442376 | tf_op jit(solution)/shard_map/ppermute | solution.py:342
  36.9 29.8 %copy-start.1 = (s32[1,1,1,1024]{3,2,1,0:T(1,128)S(1)}, s32[1,1,1,1024]{3,2,1,0:T(1,128)}, u32[]{:S(2)}) copy-start(s32[1,1,1,1024]{3,2,1,0:T(1,128)} %param.13) | copy-start | bytes 12292
  36.9 6.0 %collective-permute-start.7 = (f32[10,8,128]{2,1,0:T(8,128)S(1)}, f32[10,8,128]{2,1,0:T(8,128)S(1)}, u32[]{:S(2)}, u32[]{:S(2)}) collective-permute-start(f32[10,8,128]{2,1,0:T(8,128)S(1)} %first_step.1), channel_id=1, source_target_pairs={{8,0},{16,8},{24,16},{9,1},{17,9},{25,17},{10,2},{18,10},{26,18},{... | collective-permute-start | bytes 122888 | tf_op jit(solution)/shard_map/ppermute | solution.py:342
  38.2 5.7 %collective-permute-start.6 = (f32[10,8,128]{2,1,0:T(8,128)S(1)}, f32[10,8,128]{2,1,0:T(8,128)S(1)}, u32[]{:S(2)}, u32[]{:S(2)}) collective-permute-start(f32[10,8,128]{2,1,0:T(8,128)S(1)} %first_step.1), channel_id=1, source_target_pairs={{0,8},{8,16},{16,24},{1,9},{9,17},{17,25},{2,10},{10,18},{18,26},{... | collective-permute-start | bytes 122888 | tf_op jit(solution)/shard_map/ppermute | solution.py:342
  43.9 5.2 %collective-permute-start.9 = (f32[30,8,128]{2,1,0:T(8,128)S(1)}, f32[30,8,128]{2,1,0:T(8,128)S(1)}, u32[]{:S(2)}, u32[]{:S(2)}) collective-permute-start(f32[30,8,128]{2,1,0:T(8,128)S(1)} %pad_maximum_fusion.middle), channel_id=1, source_target_pairs={{0,7},{1,0},{2,1},{3,2},{4,3},{5,4},{6,5},{7,6},{8,15},{9,8},{10,9... | collective-permute-start | bytes 368648 | tf_op jit(solution)/shard_map/ppermute | solution.py:342
  47.2 1.9 %collective-permute-start.8 = (f32[30,8,128]{2,1,0:T(8,128)S(1)}, f32[30,8,128]{2,1,0:T(8,128)S(1)}, u32[]{:S(2)}, u32[]{:S(2)}) collective-permute-start(f32[30,8,128]{2,1,0:T(8,128)S(1)} %pad_maximum_fusion.middle), channel_id=1, source_target_pairs={{0,1},{1,2},{2,3},{3,4},{4,5},{5,6},{6,7},{7,0},{8,9},{9,10},{10,1... | collective-permute-start | bytes 368648 | tf_op jit(solution)/shard_map/ppermute | solution.py:342
  57.2 21.0 %all-to-all-start = ((f32[16,8,128]{2,1,0:T(8,128)}), f32[16,8,128]{2,1,0:T(8,128)S(1)}, u32[]{:S(2)}, u32[]{:S(2)}) async-start(f32[16,8,128]{2,1,0:T(8,128)} %get-tuple-element.31), calls=%async_computation | async-start | bytes 131072 | tf_op jit(solution)/shard_map/all_to_all | solution.py:468
  67.0 5.4 %collective-permute-start.11 = (f32[64,128]{1,0:T(8,128)S(1)}, f32[64,128]{1,0:T(8,128)S(1)}, u32[]{:S(2)}, u32[]{:S(2)}) collective-permute-start(f32[64,128]{1,0:T(8,128)S(1)} %deposit.1.own), channel_id=1, source_target_pairs={{32,0},{64,32},{96,64},{128,96},{160,128},{192,160},{224,192},{256... | collective-permute-start | bytes 98312 | tf_op jit(solution)/shard_map/ppermute | solution.py:342
  68.3 5.0 %collective-permute-start.10 = (f32[64,128]{1,0:T(8,128)S(1)}, f32[64,128]{1,0:T(8,128)S(1)}, u32[]{:S(2)}, u32[]{:S(2)}) collective-permute-start(f32[64,128]{1,0:T(8,128)S(1)} %deposit.1.own), channel_id=1, source_target_pairs={{0,32},{32,64},{64,96},{96,128},{128,160},{160,192},{192,224},{224... | collective-permute-start | bytes 98312 | tf_op jit(solution)/shard_map/ppermute | solution.py:342

commit v7 on v6

--- a/solution.py
+++ b/solution.py
@@ -28,6 +28,7 @@
 INSIDE = 2048
 ITSELF = 4096
 COMPS = 10
+GROUP = 5
 VMEM = pl.BlockSpec(memory_space=pltpu.VMEM)
 SMALL = pltpu.CompilerParams(vmem_limit_bytes=4 << 20)
 LARGE = pltpu.CompilerParams(vmem_limit_bytes=10 << 20)
@@ -124,7 +125,7 @@
 
 
 def work_space():
-    return (pltpu.VMEM((9 * K, 8, 128), jnp.float32), pltpu.VMEM((9 * K, 8, 128), jnp.float32))
+    return (pltpu.VMEM((9 * K, 8, 128), jnp.float32),) * GROUP
 
 
 def fill(tiles, low, middle, high, size):
@@ -151,10 +152,10 @@
             fresh = jnp.where(sub == 3 + axis, speed, fresh)
         out[t] = fresh
 
-    @pl.loop(0, (width - 2) // 2)
+    @pl.loop(0, (width - 2) // GROUP)
     def _(t):
-        one(2 * t, work[0])
-        one(2 * t + 1, work[1])
+        for i in range(GROUP):
+            one(GROUP * t + i, work[i])
 
 
 def second_kernel(
@@ -189,10 +190,10 @@
         for c in range(COMPS):
             values_out[t, c : c + 1, :] = values[c]
 
-    @pl.loop(0, NT // 2)
+    @pl.loop(0, NT // 4)
     def _(t):
-        one(2 * t, work[0])
-        one(2 * t + 1, work[1])
+        for i in range(4):
+            one(4 * t + i, work[i])
 
     for i in range(energy_out.shape[0]):
         energy_out[i] = total[...]

time: 97.9 us -> 97.5 us (level)
  no operation moved by 1% of the time
where the time goes in v7:
time: 97.5 us; the launch traced here: 97 us
  starting transfers between devices  46.5 us (48%)
  Pallas kernels  21.6 us (22%)
  blocking collectives  18.2 us (19%)
  waiting for transfers between devices  7.56 us (8%)
  local copies, waits for them, and re-layouts  1.69 us (2%)
    ppermute x12, starting transfers between devices, shifted(): return lax.ppermute(value, axis, pairs)  37 us
    all_to_all x1, blocking collectives, shards(): parts = lax.all_to_all(parts, ('gy', 'gz'), 0, 0, tiled=True)  18.2 us
    all_to_all x1, starting transfers between devices, shards(): energy = lax.all_to_all(energy, 'gx', 0, 0, tiled=True)  9.48 us
    pallas_call x1, Pallas kernels, shards(): pl.pallas_call(second_kernel, out_shape=(block, block, jax.ShapeDtypeStru...  8.03 us
    pallas_call x1, Pallas kernels, shards(): pl.pallas_call(first_kernel, out_shape=jax.ShapeDtypeStruct((width - 2, 8...  6.27 us
    all_to_all x1, waiting for transfers between devices, shards(): energy = lax.all_to_all(energy, 'gx', 0, 0, tiled=True)  4.01 us
    pallas_call x2, Pallas kernels, turned(): pl.pallas_call(turn_kernel, out_shape=jax.ShapeDtypeStruct((count, 8, 128...  3.61 us
    ppermute x12, waiting for transfers between devices, shifted(): return lax.ppermute(value, axis, pairs)  3.54 us
  transfers between devices with their start and end apart: 13, of which 6 were waited for; matrix products, arithmetic and copies ran while one was open for 1% of the time, Pallas kernels for 5%

profile of v7, /device:TPU:1, one launch (start us, length us, event | category | flops | bytes accessed | tf_op | source)
XLA Modules:
  0.0 97.0 jit_solution(12645857799021061452)
XLA Ops:
  0.6 1.5 %pack.1 = (f32[8,8,128]{2,1,0:T(8,128)}, f32[3,8,128]{2,1,0:T(8,128)}, f32[3,8,128]{2,1,0:T(8,128)}, f32[8,128]{1,0:T(8,128)}) custom-call(f32[3,8,128]{2,1,0:T(8,128)} %bitcast.24, f32[3,8,128]{2,1,0:T(8,128)} %bitcast.25, f32[8,128]{1,0:T(8,128)} %bitcast.26, s32[8,128]{1,0:T(8,128)} %bitcast.27, s32[8,128]{1,0:T(8,128)} %bitcast.28, ...), custom_call_target="tpu_custom_call" | custom-call | tf_op jit(solution)/shard_map/pack/pallas_call | solution.py:385
  2.2 4.4 %collective-permute-start = (f32[3,8,128]{2,1,0:T(8,128)}, f32[3,8,128]{2,1,0:T(8,128)S(1)}, u32[]{:S(2)}, u32[]{:S(2)}) collective-permute-start(f32[3,8,128]{2,1,0:T(8,128)} %get-tuple-element.20), channel_id=1, source_target_pairs={{0,32},{32,64},{64,96},{96,128},{128,160},{160,192},{192,224},{224... | collective-permute-start | bytes 36872 | tf_op jit(solution)/shard_map/ppermute | solution.py:343
  6.5 9.5 %collective-permute-start.1 = (f32[3,8,128]{2,1,0:T(8,128)}, f32[3,8,128]{2,1,0:T(8,128)S(1)}, u32[]{:S(2)}, u32[]{:S(2)}) collective-permute-start(f32[3,8,128]{2,1,0:T(8,128)} %get-tuple-element.24), channel_id=1, source_target_pairs={{0,480},{32,0},{64,32},{96,64},{128,96},{160,128},{192,160},{224,1... | collective-permute-start | bytes 36872 | tf_op jit(solution)/shard_map/ppermute | solution.py:343
  16.1 0.7 copy-done
  16.9 0.7 copy-done.2
  17.6 0.0 collective-permute-done.left
  17.6 0.0 collective-permute-done.1.right
  17.6 0.1 join.1
  17.7 0.1 slice_bitcast_fusion.1
  17.7 1.3 %collective-permute-start.3 = (f32[12,8,128]{2,1,0:T(8,128)S(1)}, f32[12,8,128]{2,1,0:T(8,128)S(1)}, u32[]{:S(2)}, u32[]{:S(2)}) collective-permute-start(f32[12,8,128]{2,1,0:T(8,128)S(1)} %get-tuple-element.27), channel_id=1, source_target_pairs={{8,0},{16,8},{24,16},{9,1},{17,9},{25,17},{10,2},{18,10},{26,18},{... | collective-permute-start | bytes 147464 | tf_op jit(solution)/shard_map/ppermute | solution.py:343
  19.0 4.0 %collective-permute-start.2 = (f32[12,8,128]{2,1,0:T(8,128)S(1)}, f32[12,8,128]{2,1,0:T(8,128)S(1)}, u32[]{:S(2)}, u32[]{:S(2)}) collective-permute-start(f32[12,8,128]{2,1,0:T(8,128)S(1)} %get-tuple-element.27), channel_id=1, source_target_pairs={{0,8},{8,16},{16,24},{1,9},{9,17},{17,25},{2,10},{10,18},{18,26},{... | collective-permute-start | bytes 147464 | tf_op jit(solution)/shard_map/ppermute | solution.py:343
  23.0 0.1 convert_reduce_fusion
  23.1 0.1 select_reduce_fusion.1
  23.2 0.1 reshape.104.meta
  23.3 0.9 collective-permute-done.2
  24.2 0.0 collective-permute-done.3
  24.2 2.2 %collective-permute-start.5 = (f32[36,8,128]{2,1,0:T(8,128)S(1)}, f32[36,8,128]{2,1,0:T(8,128)S(1)}, u32[]{:S(2)}, u32[]{:S(2)}) collective-permute-start(f32[36,8,128]{2,1,0:T(8,128)S(1)} %constant_dynamic-update-slice_fusion.middle), channel_id=1, source_target_pairs={{0,7},{1,0},{2,1},{3,2},{4,3},{5,4},{6,5},{7,6},{8,15},{9,8},{10,9... | collective-permute-start | bytes 442376 | tf_op jit(solution)/shard_map/ppermute | solution.py:343
  26.4 1.2 %collective-permute-start.4 = (f32[36,8,128]{2,1,0:T(8,128)S(1)}, f32[36,8,128]{2,1,0:T(8,128)S(1)}, u32[]{:S(2)}, u32[]{:S(2)}) collective-permute-start(f32[36,8,128]{2,1,0:T(8,128)S(1)} %constant_dynamic-update-slice_fusion.middle), channel_id=1, source_target_pairs={{0,1},{1,2},{2,3},{3,4},{4,5},{5,6},{6,7},{7,0},{8,9},{9,10},{10,1... | collective-permute-start | bytes 442376 | tf_op jit(solution)/shard_map/ppermute | solution.py:343
  27.6 0.1 convert_reduce_fusion.1
  27.7 2.0 %turn.2.mine = f32[10,8,128,128]{3,2,1,0:T(8,128)S(1)} custom-call(f32[36,8,128]{2,1,0:T(8,128)S(1)} %constant_dynamic-update-slice_fusion.middle), custom_call_target="tpu_custom_call" | custom-call | bytes 5242880 | tf_op jit(solution)/shard_map/turn/pallas_call | solution.py:57
  29.7 0.7 collective-permute-done.5.high
  30.4 0.0 collective-permute-done.4.low
  30.4 6.3 %first_step.1 = f32[10,8,128]{2,1,0:T(8,128)S(1)} custom-call(s32[60]{0:T(128)S(1)} %reshape.104.meta, f32[36,8,128]{2,1,0:T(8,128)S(1)} %collective-permute-done.4.low, f32[36,8,128]{2,1,0:T(8,128)S(1)} %constant_dynamic-update-slice_fusion.middle, f32[36,8,128]{2,1,0:T(8,128)S(1)} %collective-permute-done.5.high, f32[10,8,128,128]{3,2,1,0:T(8,128)S(1)} %turn.2.mine), custom_call_target="tpu_custom_call" | custom-call | tf_op jit(solution)/shard_map/first_step/pallas_call | solution.py:434
  36.7 1.3 %collective-permute-start.7 = (f32[10,8,128]{2,1,0:T(8,128)S(1)}, f32[10,8,128]{2,1,0:T(8,128)S(1)}, u32[]{:S(2)}, u32[]{:S(2)}) collective-permute-start(f32[10,8,128]{2,1,0:T(8,128)S(1)} %first_step.1), channel_id=1, source_target_pairs={{8,0},{16,8},{24,16},{9,1},{17,9},{25,17},{10,2},{18,10},{26,18},{... | collective-permute-start | bytes 122888 | tf_op jit(solution)/shard_map/ppermute | solution.py:343
  38.0 4.6 %collective-permute-start.6 = (f32[10,8,128]{2,1,0:T(8,128)S(1)}, f32[10,8,128]{2,1,0:T(8,128)S(1)}, u32[]{:S(2)}, u32[]{:S(2)}) collective-permute-start(f32[10,8,128]{2,1,0:T(8,128)S(1)} %first_step.1), channel_id=1, source_target_pairs={{0,8},{8,16},{16,24},{1,9},{9,17},{17,25},{2,10},{10,18},{18,26},{... | collective-permute-start | bytes 122888 | tf_op jit(solution)/shard_map/ppermute | solution.py:343
  42.6 0.1 select_reduce_fusion.3
  42.7 0.0 collective-permute-done.7
  42.7 1.0 %collective-permute-done.6 = f32[10,8,128]{2,1,0:T(8,128)S(1)} collective-permute-done((f32[10,8,128]{2,1,0:T(8,128)S(1)}, f32[10,8,128]{2,1,0:T(8,128)S(1)}, u32[]{:S(2)}, u32[]{:S(2)}) %collective-permute-start.6) | collective-permute-done | bytes 40992 | tf_op jit(solution)/shard_map/ppermute | solution.py:343
  43.7 3.3 %collective-permute-start.9 = (f32[30,8,128]{2,1,0:T(8,128)S(1)}, f32[30,8,128]{2,1,0:T(8,128)S(1)}, u32[]{:S(2)}, u32[]{:S(2)}) collective-permute-start(f32[30,8,128]{2,1,0:T(8,128)S(1)} %pad_maximum_fusion.middle), channel_id=1, source_target_pairs={{0,7},{1,0},{2,1},{3,2},{4,3},{5,4},{6,5},{7,6},{8,15},{9,8},{10,9... | collective-permute-start | bytes 368648 | tf_op jit(solution)/shard_map/ppermute | solution.py:343
  47.0 0.0 collective-permute-start.8
  47.0 0.1 add_select_fusion.13
  47.1 0.1 reshape.103.meta
  47.2 1.6 %turn.3.mine = f32[8,8,128,128]{3,2,1,0:T(8,128)S(1)} custom-call(f32[30,8,128]{2,1,0:T(8,128)S(1)} %pad_maximum_fusion.middle), custom_call_target="tpu_custom_call" | custom-call | bytes 4194304 | tf_op jit(solution)/shard_map/turn/pallas_call | solution.py:57
  48.8 0.1 collective-permute-done.9.high
  48.9 0.0 collective-permute-done.8.low
  48.9 8.0 %second_step.1 = (f32[3,8,128]{2,1,0:T(8,128)}, f32[3,8,128]{2,1,0:T(8,128)}, f32[8,16,128]{2,1,0:T(8,128)S(1)}, f32[16,8,128]{2,1,0:T(8,128)}) custom-call(s32[48]{0:T(128)S(1)} %reshape.103.meta, f32[30,8,128]{2,1,0:T(8,128)S(1)} %collective-permute-done.8.low, f32[30,8,128]{2,1,0:T(8,128)S(1)} %pad_maximum_fusion.middle, ...), custom_call_target="tpu_custom_call" | custom-call | tf_op jit(solution)/shard_map/second_step/pallas_call | solution.py:451
  56.9 9.5 %all-to-all-start = ((f32[16,8,128]{2,1,0:T(8,128)}), f32[16,8,128]{2,1,0:T(8,128)S(1)}, u32[]{:S(2)}, u32[]{:S(2)}) async-start(f32[16,8,128]{2,1,0:T(8,128)} %get-tuple-element.31), calls=%async_computation | async-start | bytes 131072 | tf_op jit(solution)/shard_map/all_to_all | solution.py:469
  66.4 0.3 deposit.1.own
  66.7 1.3 %collective-permute-start.11 = (f32[64,128]{1,0:T(8,128)S(1)}, f32[64,128]{1,0:T(8,128)S(1)}, u32[]{:S(2)}, u32[]{:S(2)}) collective-permute-start(f32[64,128]{1,0:T(8,128)S(1)} %deposit.1.own), channel_id=1, source_target_pairs={{32,0},{64,32},{96,64},{128,96},{160,128},{192,160},{224,192},{256... | collective-permute-start | bytes 98312 | tf_op jit(solution)/shard_map/ppermute | solution.py:343
  68.0 4.0 %collective-permute-start.10 = (f32[64,128]{1,0:T(8,128)S(1)}, f32[64,128]{1,0:T(8,128)S(1)}, u32[]{:S(2)}, u32[]{:S(2)}) collective-permute-start(f32[64,128]{1,0:T(8,128)S(1)} %deposit.1.own), channel_id=1, source_target_pairs={{0,32},{32,64},{64,96},{96,128},{128,160},{160,192},{192,224},{224... | collective-permute-start | bytes 98312 | tf_op jit(solution)/shard_map/ppermute | solution.py:343
  72.0 0.1 pad_add_fusion.coords
  72.1 0.0 collective-permute-done.11.after
  72.1 0.9 collective-permute-done.10.before
  73.0 0.9 planes.1.parts
  73.9 4.0 %all-to-all-done.energy = f32[16,8,128]{2,1,0:T(8,128)S(1)} async-done(((f32[16,8,128]{2,1,0:T(8,128)}), f32[16,8,128]{2,1,0:T(8,128)S(1)}, u32[]{:S(2)}, u32[]{:S(2)}) %all-to-all-start) | async-done | bytes 65568 | tf_op jit(solution)/shard_map/all_to_all | solution.py:469
  78.0 0.1 energies.1
  78.1 18.2 %all_to_all.10.parts = f32[32,8,128]{2,1,0:T(8,128)S(1)} all-to-all(f32[32,8,128]{2,1,0:T(8,128)S(1)} %energies.1), channel_id=1, replica_groups=mesh['gx'=16,'gy'=4,'gz'=8] {'gy','gz'}, dimensions={0} | all-to-all | bytes 262144 | tf_op jit(solution)/shard_map/all_to_all | solution.py:502
  96.2 0.8 lines.1
  (20 shorter events, 0.1 us)
Async XLA Ops:
  2.2 15.4 %collective-permute-start = (f32[3,8,128]{2,1,0:T(8,128)}, f32[3,8,128]{2,1,0:T(8,128)S(1)}, u32[]{:S(2)}, u32[]{:S(2)}) collective-permute-start(f32[3,8,128]{2,1,0:T(8,128)} %get-tuple-element.20), channel_id=1, source_target_pairs={{0,32},{32,64},{64,96},{96,128},{128,160},{160,192},{192,224},{224... | collective-permute-start | bytes 36872 | tf_op jit(solution)/shard_map/ppermute | solution.py:343
  6.5 11.0 %collective-permute-start.1 = (f32[3,8,128]{2,1,0:T(8,128)}, f32[3,8,128]{2,1,0:T(8,128)S(1)}, u32[]{:S(2)}, u32[]{:S(2)}) collective-permute-start(f32[3,8,128]{2,1,0:T(8,128)} %get-tuple-element.24), channel_id=1, source_target_pairs={{0,480},{32,0},{64,32},{96,64},{128,96},{160,128},{192,160},{224,1... | collective-permute-start | bytes 36872 | tf_op jit(solution)/shard_map/ppermute | solution.py:343
  16.1 0.8 copy-start
  16.9 0.7 copy-start.2
  17.7 6.5 %collective-permute-start.3 = (f32[12,8,128]{2,1,0:T(8,128)S(1)}, f32[12,8,128]{2,1,0:T(8,128)S(1)}, u32[]{:S(2)}, u32[]{:S(2)}) collective-permute-start(f32[12,8,128]{2,1,0:T(8,128)S(1)} %get-tuple-element.27), channel_id=1, source_target_pairs={{8,0},{16,8},{24,16},{9,1},{17,9},{25,17},{10,2},{18,10},{26,18},{... | collective-permute-start | bytes 147464 | tf_op jit(solution)/shard_map/ppermute | solution.py:343
  19.0 5.2 %collective-permute-start.2 = (f32[12,8,128]{2,1,0:T(8,128)S(1)}, f32[12,8,128]{2,1,0:T(8,128)S(1)}, u32[]{:S(2)}, u32[]{:S(2)}) collective-permute-start(f32[12,8,128]{2,1,0:T(8,128)S(1)} %get-tuple-element.27), channel_id=1, source_target_pairs={{0,8},{8,16},{16,24},{1,9},{9,17},{17,25},{2,10},{10,18},{18,26},{... | collective-permute-start | bytes 147464 | tf_op jit(solution)/shard_map/ppermute | solution.py:343
  24.2 6.2 %collective-permute-start.5 = (f32[36,8,128]{2,1,0:T(8,128)S(1)}, f32[36,8,128]{2,1,0:T(8,128)S(1)}, u32[]{:S(2)}, u32[]{:S(2)}) collective-permute-start(f32[36,8,128]{2,1,0:T(8,128)S(1)} %constant_dynamic-update-slice_fusion.middle), channel_id=1, source_target_pairs={{0,7},{1,0},{2,1},{3,2},{4,3},{5,4},{6,5},{7,6},{8,15},{9,8},{10,9... | collective-permute-start | bytes 442376 | tf_op jit(solution)/shard_map/ppermute | solution.py:343
  26.4 4.0 %collective-permute-start.4 = (f32[36,8,128]{2,1,0:T(8,128)S(1)}, f32[36,8,128]{2,1,0:T(8,128)S(1)}, u32[]{:S(2)}, u32[]{:S(2)}) collective-permute-start(f32[36,8,128]{2,1,0:T(8,128)S(1)} %constant_dynamic-update-slice_fusion.middle), channel_id=1, source_target_pairs={{0,1},{1,2},{2,3},{3,4},{4,5},{5,6},{6,7},{7,0},{8,9},{9,10},{10,1... | collective-permute-start | bytes 442376 | tf_op jit(solution)/shard_map/ppermute | solution.py:343
  36.7 29.7 %copy-start.1 = (s32[1,1,1,1024]{3,2,1,0:T(1,128)S(1)}, s32[1,1,1,1024]{3,2,1,0:T(1,128)}, u32[]{:S(2)}) copy-start(s32[1,1,1,1024]{3,2,1,0:T(1,128)} %param.13) | copy-start | bytes 12292
  36.7 6.0 %collective-permute-start.7 = (f32[10,8,128]{2,1,0:T(8,128)S(1)}, f32[10,8,128]{2,1,0:T(8,128)S(1)}, u32[]{:S(2)}, u32[]{:S(2)}) collective-permute-start(f32[10,8,128]{2,1,0:T(8,128)S(1)} %first_step.1), channel_id=1, source_target_pairs={{8,0},{16,8},{24,16},{9,1},{17,9},{25,17},{10,2},{18,10},{26,18},{... | collective-permute-start | bytes 122888 | tf_op jit(solution)/shard_map/ppermute | solution.py:343
  38.0 5.7 %collective-permute-start.6 = (f32[10,8,128]{2,1,0:T(8,128)S(1)}, f32[10,8,128]{2,1,0:T(8,128)S(1)}, u32[]{:S(2)}, u32[]{:S(2)}) collective-permute-start(f32[10,8,128]{2,1,0:T(8,128)S(1)} %first_step.1), channel_id=1, source_target_pairs={{0,8},{8,16},{16,24},{1,9},{9,17},{17,25},{2,10},{10,18},{18,26},{... | collective-permute-start | bytes 122888 | tf_op jit(solution)/shard_map/ppermute | solution.py:343
  43.7 5.2 %collective-permute-start.9 = (f32[30,8,128]{2,1,0:T(8,128)S(1)}, f32[30,8,128]{2,1,0:T(8,128)S(1)}, u32[]{:S(2)}, u32[]{:S(2)}) collective-permute-start(f32[30,8,128]{2,1,0:T(8,128)S(1)} %pad_maximum_fusion.middle), channel_id=1, source_target_pairs={{0,7},{1,0},{2,1},{3,2},{4,3},{5,4},{6,5},{7,6},{8,15},{9,8},{10,9... | collective-permute-start | bytes 368648 | tf_op jit(solution)/shard_map/ppermute | solution.py:343
  47.0 1.9 %collective-permute-start.8 = (f32[30,8,128]{2,1,0:T(8,128)S(1)}, f32[30,8,128]{2,1,0:T(8,128)S(1)}, u32[]{:S(2)}, u32[]{:S(2)}) collective-permute-start(f32[30,8,128]{2,1,0:T(8,128)S(1)} %pad_maximum_fusion.middle), channel_id=1, source_target_pairs={{0,1},{1,2},{2,3},{3,4},{4,5},{5,6},{6,7},{7,0},{8,9},{9,10},{10,1... | collective-permute-start | bytes 368648 | tf_op jit(solution)/shard_map/ppermute | solution.py:343
  56.9 21.1 %all-to-all-start = ((f32[16,8,128]{2,1,0:T(8,128)}), f32[16,8,128]{2,1,0:T(8,128)S(1)}, u32[]{:S(2)}, u32[]{:S(2)}) async-start(f32[16,8,128]{2,1,0:T(8,128)} %get-tuple-element.31), calls=%async_computation | async-start | bytes 131072 | tf_op jit(solution)/shard_map/all_to_all | solution.py:469
  66.7 5.4 %collective-permute-start.11 = (f32[64,128]{1,0:T(8,128)S(1)}, f32[64,128]{1,0:T(8,128)S(1)}, u32[]{:S(2)}, u32[]{:S(2)}) collective-permute-start(f32[64,128]{1,0:T(8,128)S(1)} %deposit.1.own), channel_id=1, source_target_pairs={{32,0},{64,32},{96,64},{128,96},{160,128},{192,160},{224,192},{256... | collective-permute-start | bytes 98312 | tf_op jit(solution)/shard_map/ppermute | solution.py:343
  68.0 5.0 %collective-permute-start.10 = (f32[64,128]{1,0:T(8,128)S(1)}, f32[64,128]{1,0:T(8,128)S(1)}, u32[]{:S(2)}, u32[]{:S(2)}) collective-permute-start(f32[64,128]{1,0:T(8,128)S(1)} %deposit.1.own), channel_id=1, source_target_pairs={{0,32},{32,64},{64,96},{96,128},{128,160},{160,192},{192,224},{224... | collective-permute-start | bytes 98312 | tf_op jit(solution)/shard_map/ppermute | solution.py:343
